TPU v7x, 128 devices: a whole 4x4x4 slice. The times are simulated.
128 devices in a mesh: lat: 32 (over x, z, core), tp: 4 (over y).
Axes of the slice: x: 4, y: 4, z: 4, core: 2. Of those that a mesh axis runs over, the one named last changes fastest.
Arguments:
- z_clean: bfloat16 [128, 4096], P(None, 'tp'), may hold values from -6 to 6
- z_corrupt: bfloat16 [128, 4096], P(None, 'tp'), may hold values from -6 to 6
- resid_clean: bfloat16 [128, 3584], replicated, may hold values from -6 to 6
- resid_corrupt: bfloat16 [128, 3584], replicated, may hold values from -6 to 6
- w_out: bfloat16 [4096, 3584], P('tp'), may hold values from -0.09375 to 0.09375
- post_gain: float32 [3584], replicated, may hold values from 0.1 to 1.9
- w_enc: bfloat16 [3584, 131072], P(None, ('lat', 'tp')), may hold values from -0.09375 to 0.09375
- w_dec: bfloat16 [131072, 3584], P(('lat', 'tp')), may hold values from -1 to 1
- cot: bfloat16 [128, 4, 3584], replicated, may hold values from -6 to 6
- active: int32 [128, 131072], P(None, ('lat', 'tp')), may hold values 0 or 1
Outputs:
- latent_attr: float32 [128, 131072], P(None, ('lat', 'tp'))
- head_attr: float32 [128, 16], P('lat', 'tp')
All inputs are finite; a program needn't handle non-finite values. No bound on the sum of `active` on one device may be relied on, other than what follows from the above.
Results may differ from a plain program's by a relative error of at most 0.0043.
Values sent between devices are 32-bit elements; how exact they have to be, the bound alone decides.
No kernel may reach another device: no remote copies, remote signals or barrier semaphores. Data moves between devices by JAX's collectives and lax.ppermute only.
A program may use at most 192 MiB of HBM per device.

v0:
```python
import jax
import jax.numpy as jnp
from jax import lax
from jax.sharding import PartitionSpec as P

HEAD_DIM = 256
LAT = 131072


EPSILON = 1e-06


def contract_last(left_side, right_side):
    return lax.dot_general(
        left_side, right_side, (((1,), (1,)), ((), ())), preferred_element_type=jnp.float32
    )


def interpolate(clean, corrupt, alphas):
    clean_f = clean.astype(jnp.float32)
    corrupt_f = corrupt.astype(jnp.float32)
    return corrupt_f[:, None, :] + alphas[None, :, None] * (clean_f - corrupt_f)[:, None, :]


def norm_backward(attn_out, inv_rms, grad_mid, post_gain):
    scaled = grad_mid * post_gain
    inner = jnp.mean(attn_out * scaled, axis=-1, keepdims=True)
    return (inv_rms * scaled - attn_out * inv_rms**3 * inner).astype(jnp.bfloat16)


def head_terms(grad_attn, w_out, delta_rows, step_count):
    heads_local = w_out.shape[0] // HEAD_DIM
    grad_heads = contract_last(grad_attn, w_out).reshape(-1, step_count, heads_local, HEAD_DIM)
    return jnp.mean(delta_rows * jnp.mean(grad_heads, axis=1), axis=-1)


def body(
    z_clean, z_corrupt, resid_clean, resid_corrupt, w_out, post_gain, w_enc, w_dec, cot, active
):
    tokens = z_clean.shape[0]
    step_count = cot.shape[1]
    model_width = cot.shape[2]
    lat_local = w_enc.shape[1]
    heads_local = w_out.shape[0] // HEAD_DIM
    row_count = tokens * step_count
    alphas = jnp.arange(step_count, dtype=jnp.float32) / (step_count - 1)
    z_mix = (
        interpolate(z_clean, z_corrupt, alphas)
        .astype(jnp.bfloat16)
        .reshape(row_count, w_out.shape[0])
    )
    partial_out = jnp.dot(z_mix, w_out, preferred_element_type=jnp.float32)
    attn_out = lax.psum(partial_out, "tp")
    inv_rms = lax.rsqrt(jnp.mean(attn_out * attn_out, axis=-1, keepdims=True) + EPSILON)
    resid_mid = (
        interpolate(resid_clean, resid_corrupt, alphas).reshape(row_count, model_width)
        + attn_out * inv_rms * post_gain
    )
    sae_in = resid_mid.astype(jnp.bfloat16)
    pre_act = jnp.dot(sae_in, w_enc, preferred_element_type=jnp.float32).reshape(
        tokens, step_count, lat_local
    )
    active_mask = active.astype(jnp.float32)
    latents = pre_act * active_mask[:, None, :]
    delta_f = latents[:, step_count - 1] - latents[:, 0]
    grad_f = contract_last(cot.reshape(row_count, model_width), w_dec).reshape(
        tokens, step_count, lat_local
    )
    raw_attr = delta_f * jnp.mean(grad_f, axis=1)
    local_total = jnp.sum(jnp.abs(raw_attr), axis=-1, keepdims=True)
    grad_latent = (
        (grad_f * active_mask[:, None, :]).reshape(row_count, lat_local).astype(jnp.bfloat16)
    )
    delta_z = (z_clean.astype(jnp.float32) - z_corrupt.astype(jnp.float32)).reshape(
        tokens, heads_local, HEAD_DIM
    )
    partial_grad = contract_last(grad_latent, w_enc)
    grad_mid, token_total = lax.psum((partial_grad, local_total), ("lat", "tp"))
    grad_attn = norm_backward(attn_out, inv_rms, grad_mid, post_gain)
    head_all = head_terms(grad_attn, w_out, delta_z, step_count)
    token_share = tokens // lax.axis_size("lat")
    head_attr = lax.dynamic_slice_in_dim(
        head_all, lax.axis_index("lat") * token_share, token_share, 0
    )
    latent_attr = raw_attr / (token_total / LAT + EPSILON)
    return (latent_attr, head_attr)


def solution(mesh):
    placed = (
        P(None, "tp"),
        P(None, "tp"),
        P(),
        P(),
        P("tp", None),
        P(),
        P(None, ("lat", "tp")),
        P(("lat", "tp"), None),
        P(),
        P(None, ("lat", "tp")),
    )
    return jax.shard_map(
        body,
        mesh=mesh,
        in_specs=placed,
        out_specs=(P(None, ("lat", "tp")), P("lat", "tp")),
        check_vma=False,
    )
```

profile of v0, /device:TPU:0, one launch (start us, length us, event | category | flops | bytes accessed | tf_op | source)
XLA Modules:
  0.0 453.1 jit_solution(6559520843452456404)
XLA Ops:
  7.2 1.1 convert_element_type.39
  8.3 8.4 %multiply_convert_fusion = (bf16[128,4,1024]{2,0,1:T(8,128)(2,1)S(1)}, f32[128,1024]{1,0:T(8,128)S(1)}) fusion(f32[128,1024]{1,0:T(8,128)S(1)} %convert_element_type.39, bf16[1024,3584]{1,0:T(8,128)(2,1)} %param.17, bf16[128,4,3584]{2,1,0:T(4,128)(2,1)} %param.18), kind=kOutput, calls=%fused_computation.17 | convolution fusion | flops 3759538176 | bytes 13107200 | tf_op jit(solution)/shard_map/dot_general | solution.py:14
  17.8 9.2 %fusion.16 = f32[512,3584]{1,0:T(8,128)} fusion(bf16[512,1024]{1,0:T(8,128)(2,1)S(1)} %convert_element_type.41, bf16[3584,1024]{1,0:T(8,128)(2,1)} %param.16), kind=kOutput, calls=%fused_computation.35 | convolution fusion | flops 3758096384 | bytes 15728640 | tf_op jit(solution)/shard_map/dot_general | solution.py:14
  28.7 1.8 mul.121
  31.2 1.8 add.58
  33.0 11.3 %fusion.12 = f32[512,3584]{1,0:T(8,128)} fusion(bf16[1024,3584]{1,0:T(8,128)(2,1)} %param.14, f32[512,1024]{1,0:T(8,128)} %add.58, f32[512,1024]{1,0:T(8,128)} %mul.121, f32[512]{0:T(512)S(1)} %mul.114), kind=kOutput, calls=%fused_computation.20 | convolution fusion | flops 3759669248 | bytes 18876416 | tf_op jit(solution)/shard_map/dot_general | solution.py:52
  44.3 1.0 reshape.57
  46.2 4.3 mul.116
  50.5 9.0 %mul.117 = f32[512,3584]{1,0:T(8,128)} reshape(f32[128,4,3584]{2,1,0:T(4,128)} %mul.116) | data formatting | bytes 14680064 | tf_op jit(solution)/shard_map/mul | solution.py:22
  59.5 3.9 add.54
  63.5 9.1 %add.55 = f32[512,3584]{1,0:T(8,128)} reshape(f32[128,4,3584]{2,1,0:T(4,128)} %add.54) | data formatting | bytes 14680064 | tf_op jit(solution)/shard_map/add | solution.py:22
  72.5 117.0 %all-reduce.5.cloned.1.call-done = f32[512,3584]{1,0:T(8,128)} async-done(((f32[512,3584]{1,0:T(8,128)}), f32[512,3584]{1,0:T(8,128)}) %all-reduce.5.cloned.1.call-update) | async-done | bytes 7340048 | tf_op jit(solution)/shard_map/psum | solution.py:78
  189.6 144.6 %all-reduce.3.cloned.1.call-done = f32[512,3584]{1,0:T(8,128)} async-done(((f32[512,3584]{1,0:T(8,128)}), f32[512,3584]{1,0:T(8,128)}) %all-reduce.3.cloned.1.call-update) | async-done | bytes 7340048 | tf_op jit(solution)/shard_map/psum | solution.py:53
  334.2 6.6 %multiply_reduce_fusion = (f32[512]{0:T(512)S(1)}, f32[512]{0:T(512)S(1)}) fusion(f32[512,3584]{1,0:T(8,128)} %all-reduce.3.cloned.1.call-done, f32[512,3584]{1,0:T(8,128)} %all-reduce.5.cloned.1.call-done, f32[3584]{0:T(1024)S(1)} %copy-done.8), kind=kLoop, calls=%fused_computation.3 | loop fusion | flops 9174016 | bytes 14698496 | tf_op jit(solution)/shard_map/reduce_sum | solution.py:27
  341.5 10.6 %fusion.3 = f32[512,1024]{1,0:T(8,128)} fusion(bf16[1024,3584]{1,0:T(8,128)(2,1)} %param.14, f32[512,3584]{1,0:T(8,128)} %all-reduce.3.cloned.1.call-done, f32[512,3584]{1,0:T(8,128)S(1)} %copy-done.1, f32[512]{0:T(512)S(1)} %get-tuple-element.9, f32[512]{0:T(512)S(1)} %get-tuple-element.6, f32[3584]{0:T(1024)S(1)} %copy-done.8, f32[512]{0:T(512)S(1)} %get-tuple-element.7), kind=kOutput, calls=%fused_computation.7 | convolution fusion | flops 3769106432 | bytes 24137728 | tf_op jit(solution)/shard_map/dot_general | solution.py:14
  352.1 2.2 reshape.58
  354.3 14.8 %fusion.2 = f32[512,1024]{1,0:T(8,128)} fusion(bf16[3584,1024]{1,0:T(8,128)(2,1)} %param.16, f32[512,3584]{1,0:T(8,128)} %all-reduce.3.cloned.1.call-done, f32[512,3584]{1,0:T(8,128)} %add.55, f32[512,3584]{1,0:T(8,128)} %mul.117, f32[3584]{0:T(1024)S(1)} %copy-done.8, f32[512]{0:T(512)S(1)} %get-tuple-element.7, f32[512]{0:T(512)S(1)} %mul.114), kind=kOutput, calls=%fused_computation.6 | convolution fusion | flops 3769106432 | bytes 31475712 | tf_op jit(solution)/shard_map/dot_general | solution.py:60
  369.1 2.9 reshape.56
  372.0 2.8 copy_multiply_fusion
  374.8 1.3 copy-done
  376.4 65.0 %psum.22 = f32[128,1]{0,1:T(1,128)S(1)} all-reduce(f32[128,1]{0,1:T(1,128)S(1)} %bitcast.21), channel_id=1, replica_groups=mesh['lat'=32,'tp'=4] {'lat','tp'}, use_global_device_ids=true, to_apply=%region_4.0 | all-reduce | flops 128 | bytes 1024 | tf_op jit(solution)/shard_map/psum | solution.py:78
  441.3 2.1 broadcast_divide_fusion
  443.5 1.0 reduce_sum.58
  444.4 1.3 multiply_reduce_fusion.2
  (34 shorter events, 5.8 us)
Async XLA Ops:
  7.2 182.4 %all-reduce.5.cloned.1.call-start = ((), (), s32[]{:S(2)}) async-start(), calls=%async_computation.1 | async-start | bytes 14680064 | tf_op jit(solution)/shard_map/psum | solution.py:78
  8.3 8.4 %copy-start.3 = (f32[128,1024]{1,0:T(8,128)}, f32[128,1024]{1,0:T(8,128)S(1)}, u32[]{:S(2)}) copy-start(f32[128,1024]{1,0:T(8,128)S(1)} %convert_element_type.39) | copy-start | bytes 1572868
  27.1 0.9 copy-start.5
  27.1 1.0 copy-start.7
  27.1 307.1 %all-reduce.3.cloned.1.call-start = ((), (), s32[]{:S(2)}) async-start(), calls=%async_computation | async-start | bytes 14680064 | tf_op jit(solution)/shard_map/psum | solution.py:53
  44.3 1.3 copy-start.2
  44.3 1.7 copy-start.6
  63.5 270.7 %copy-start.8 = (f32[3584]{0:T(1024)S(1)}, f32[3584]{0:T(1024)}, u32[]{:S(2)}) copy-start(f32[3584]{0:T(1024)} %param.15) | copy-start | bytes 43012
  334.2 7.3 %copy-start.1 = (f32[512,3584]{1,0:T(8,128)S(1)}, f32[512,3584]{1,0:T(8,128)}, u32[]{:S(2)}) copy-start(f32[512,3584]{1,0:T(8,128)} %all-reduce.5.cloned.1.call-done) | copy-start | bytes 22020100
  354.3 17.7 %copy-start.4 = (f32[128,1024]{1,0:T(8,128)S(1)}, f32[128,1024]{1,0:T(8,128)}, u32[]{:S(2)}) copy-start(f32[128,1024]{1,0:T(8,128)} %copy-done.3) | copy-start | bytes 1572868
  374.8 1.4 copy-start
Sparse Core Ops, SparseCore 0:
  27.2 162.3 all-reduce.4
  191.9 142.2 all-reduce.2
where the time goes:
time: 455 us; the launch traced here: 453 us
  waiting for transfers between devices  262 us (58%)
  blocking collectives  65 us (14%)
  matrix products  54.4 us (12%)
  local copies, waits for them, and re-layouts  41.7 us (9%)
  other arithmetic  16 us (4%)
  between operations  14.2 us (3%)
    psum x1, waiting for transfers between devices, body(): attn_out = lax.psum(partial_out, 'tp')  145 us
    psum x1, waiting for transfers between devices, body(): grad_mid, token_total = lax.psum((partial_grad, local_total), ('lat', 'tp'))  117 us
    psum x1, blocking collectives, body(): grad_mid, token_total = lax.psum((partial_grad, local_total), ('lat', 'tp'))  65 us
    dot_general x3, matrix products, contract_last(): lax.dot_general(left_side, right_side, (((1,), (1,)), ((), ())), preferre...  28.2 us
    mul x6, local copies, waits for them, and re-layouts, interpolate(): alphas[None, :, None] * (clean_f - corrupt_f)[:, None, :]  15.8 us
    add x4, local copies, waits for them, and re-layouts, interpolate(): corrupt_f[:, None, :]  15.3 us
    dot_general x1, matrix products, body(): jnp.dot(sae_in, w_enc, preferred_element_type=jnp.float32)  14.8 us
    dot_general x1, matrix products, body(): partial_out = jnp.dot(z_mix, w_out, preferred_element_type=jnp.float32)  11.3 us
  transfers between devices with their start and end apart: 2, of which 2 were waited for; matrix products, arithmetic and copies ran while one was open for 10% of the time, Pallas kernels for 0%

commit v1 on v0

v1 whole, which is shorter than its diff:
```python
import jax
import jax.numpy as jnp
from jax import lax
from jax.experimental import pallas as pl
from jax.experimental.pallas import tpu as pltpu
from jax.sharding import PartitionSpec as P

D = 3584
TOKENS = 128
STEPS = 4
HEAD_DIM = 256
HEADS_LOCAL = 4
LAT = 131072
LAT_LOCAL = 1024
EPSILON = 1e-06
OWN = 4
PLANE = 16
SIDE = 128
MSG = D + SIDE
RED = D + 2 * SIDE
HALF = RED // 2
ALPHAS = tuple(k / 3.0 for k in range(STEPS))
F32 = jnp.float32
BF16 = jnp.bfloat16
VMEM = pltpu.VMEM
MIB = 1024 * 1024


def lat_index(x, z, core):
    return ((x % 4) * 4 + z % 4) * 2 + core


PLANES = [[lat_index(x, z, c) for x in range(4) for z in range(4)] for c in range(2)]
CORE_SWAP = [(i, i ^ 1) for i in range(32)]


def call(kernel, name, operands, outs, scratch=(), mib=8, flops=10**6, hbm=()):
    spaces = [pltpu.HBM if i in hbm else VMEM for i in range(len(operands))]
    nbytes = sum(x.size * x.dtype.itemsize for x in operands)
    return pl.pallas_call(
        kernel,
        in_specs=[pl.BlockSpec(memory_space=s) for s in spaces],
        out_specs=[pl.BlockSpec(memory_space=VMEM)] * len(outs),
        out_shape=[VMEM(shape, dtype) for shape, dtype in outs],
        scratch_shapes=list(scratch),
        compiler_params=pltpu.CompilerParams(vmem_limit_bytes=mib * MIB),
        cost_estimate=pl.CostEstimate(flops=flops, bytes_accessed=nbytes, transcendentals=0),
        name=name,
    )(*[pltpu.with_memory_space_constraint(x, s) for x, s in zip(operands, spaces)])


def nt(a, b):
    return lax.dot_general(a, b, (((1,), (1,)), ((), ())), preferred_element_type=F32)


def nn(a, b):
    return lax.dot_general(a, b, (((1,), (0,)), ((), ())), preferred_element_type=F32)


def project_kernel(zc_ref, zn_ref, w_ref, heads_ref, part_ref, w_s, sems):
    copies = []
    for h in range(HEADS_LOCAL):
        rows = pl.ds(h * HEAD_DIM, HEAD_DIM)
        copies.append(pltpu.make_async_copy(w_ref.at[rows, :], w_s.at[rows, :], sems.at[h]))
        copies[-1].start()
    first = lax.axis_index("lat") * OWN
    row = lax.broadcasted_iota(jnp.int32, (16, TOKENS), 0)
    token = lax.broadcasted_iota(jnp.int32, (16, TOKENS), 1)
    pick_c = ((row < OWN) & (token == first + row)).astype(F32).astype(BF16)
    pick_n = ((row >= OWN) & (row < 2 * OWN) & (token == first + row - OWN)).astype(F32).astype(BF16)
    z = (nn(pick_c, zc_ref[...]) + nn(pick_n, zn_ref[...])).astype(BF16)
    for h in range(HEADS_LOCAL):
        copies[h].wait()
        cols = slice(h * HEAD_DIM, (h + 1) * HEAD_DIM)
        out = nn(z[:, cols], w_s[cols, :])[: 2 * OWN]
        heads_ref[h] = out
        if h == 0:
            part_ref[...] = out
        else:
            part_ref[...] += out


def project(z_corrupt, z_clean, w_out):
    return call(
        project_kernel,
        "project",
        (z_corrupt, z_clean, w_out),
        [((HEADS_LOCAL, 2 * OWN, D), F32), ((2 * OWN, D), F32)],
        [VMEM((1024, D), BF16), pltpu.SemaphoreType.DMA((HEADS_LOCAL,))],
        mib=12,
        flops=2 * 16 * 1024 * D,
        hbm=(2,),
    )


def grad_f_kernel(cot_ref, w_ref, out_ref, rows, acc):
    rows[...] = cot_ref[...].reshape(TOKENS * STEPS, D)
    for n in range(w_ref.shape[0] // acc.shape[0] // SIDE):
        base = n * acc.shape[0] * SIDE
        out = nt(rows[...], w_ref[base : base + acc.shape[0] * SIDE, :])
        for j in range(acc.shape[0]):
            acc[j] = out[:, j * SIDE : (j + 1) * SIDE]
            cols = slice(base + j * SIDE, base + (j + 1) * SIDE)
            for k in range(STEPS):
                out_ref[k, :, cols] = acc[j, pl.ds(k, TOKENS, stride=STEPS), :]


def grad_f(cot, w_dec):
    return call(
        grad_f_kernel,
        "grad_f",
        (cot, w_dec),
        [((STEPS, TOKENS, LAT_LOCAL), F32)],
        [VMEM((TOKENS * STEPS, D), BF16), VMEM((2, TOKENS * STEPS, SIDE), F32)],
        mib=8,
        flops=2 * 512 * 1024 * D,
    )[0]


def norm_kernel(a_ref, b_ref, c_ref, d_ref, rc_ref, rn_ref, gain_ref, attn_ref, msg_ref):
    attn = (a_ref[...] + b_ref[...]) + (c_ref[...] + d_ref[...])
    attn_ref[...] = attn
    first = lax.axis_index("lat") * OWN
    row = lax.broadcasted_iota(jnp.int32, (16, TOKENS), 0)
    token = lax.broadcasted_iota(jnp.int32, (16, TOKENS), 1)
    pick = ((row < 2 * OWN) & (token == first + row % OWN)).astype(F32).astype(BF16)
    corrupt = nn(pick, rc_ref[...])[: 2 * OWN]
    clean = nn(pick, rn_ref[...])[: 2 * OWN]
    upper = lax.broadcasted_iota(jnp.int32, (2 * OWN, D), 0) >= OWN
    resid = jnp.where(upper, corrupt + (clean - corrupt), corrupt)
    other = pltpu.roll(attn, OWN, 0)
    a_0 = jnp.where(upper, other, attn)
    delta = jnp.where(upper, attn, other) - a_0
    lane = lax.broadcasted_iota(jnp.int32, (2 * OWN, SIDE), 1)
    side = jnp.zeros((2 * OWN, SIDE), F32)
    invs = []
    for k in range(STEPS):
        a_k = a_0 + ALPHAS[k] * delta
        inv = lax.rsqrt(jnp.sum(a_k * a_k, axis=1, keepdims=True) * (1.0 / D) + EPSILON)
        invs.append(inv)
        side = jnp.where(lane == k, inv, side)
    low = lax.broadcasted_iota(jnp.int32, (2 * OWN, 1), 0) < OWN
    own_inv = jnp.where(low, invs[0], invs[3])
    sae_in = resid + attn * own_inv * gain_ref[...]
    for g in range(PLANE):
        msg_ref[g, :, :D] = sae_in
        msg_ref[g, :, D:] = side


def norm(parts, resid_corrupt, resid_clean, gain):
    return call(
        norm_kernel,
        "norm",
        (*parts, resid_corrupt, resid_clean, gain),
        [((2 * OWN, D), F32), ((PLANE, 2 * OWN, MSG), F32)],
    )


def resid_kernel(rc_ref, rn_ref, w_ref, out_ref):
    out_ref[0] = nn(rc_ref[...], w_ref[...])
    out_ref[1] = nn(rn_ref[...], w_ref[...])


def resid_project(resid_corrupt, resid_clean, w_enc):
    return call(
        resid_kernel,
        "resid_project",
        (resid_corrupt, resid_clean, w_enc),
        [((2, TOKENS, LAT_LOCAL), F32)],
        flops=2 * 256 * 1024 * D,
    )[0]


def own_kernel(x_ref, w_ref, out_ref):
    out_ref[...] = nn(x_ref[:, :, :D].reshape(TOKENS, D).astype(BF16), w_ref[...])


def own_project(x_own, w_enc):
    return call(
        own_kernel,
        "own_project",
        (x_own, w_enc),
        [((TOKENS, LAT_LOCAL), F32)],
        flops=2 * 128 * 1024 * D,
    )[0]


def upper_rows(width):
    return lax.broadcasted_iota(jnp.int32, (TOKENS, width), 0) % 8 >= OWN


def swap_rows(x):
    width = x.shape[-1]
    return pltpu.roll(x.reshape(PLANE, 8, width), OWN, 1).reshape(TOKENS, width)


def by_step(own, other, core):
    up = upper_rows(own.shape[-1])
    is_0 = core == 0
    x_0 = jnp.where(is_0, own, other)
    x_1 = jnp.where(is_0, other, own)
    return jnp.where(up, swap_rows(x_1), x_0), jnp.where(up, x_1, swap_rows(x_0))


def by_core(x, core):
    width = x.shape[-1]
    pairs = x.reshape(PLANE // 2, 2, 8, width)
    even, odd = pairs[:, 0], pairs[:, 1]
    up = lax.broadcasted_iota(jnp.int32, even.shape, 1) >= OWN
    core_0 = jnp.where(up, pltpu.roll(odd, OWN, 1), even).reshape(TOKENS // 2, width)
    core_1 = jnp.where(up, odd, pltpu.roll(even, OWN, 1)).reshape(TOKENS // 2, width)
    is_0 = core == 0
    return jnp.where(is_0, core_0, core_1), jnp.where(is_0, core_1, core_0)


def lane_fold(x):
    total = x[:, :SIDE]
    for start in range(SIDE, x.shape[1], SIDE):
        total = total + x[:, start : start + SIDE]
    return total


def latents_kernel(
    own_ref, other_ref, pre_ref, resid_ref, gf_ref, active_ref, w_ref,
    raw_ref, keep_ref, send_ref,
    pre_s, hidden_s, inv_s,
):
    core = lax.axis_index("lat") % 2
    pre_s[...] = nn(other_ref[:, :, :D].reshape(TOKENS, D).astype(BF16), w_ref[...])
    side = by_step(
        own_ref[:, :, D:].reshape(TOKENS, SIDE), other_ref[:, :, D:].reshape(TOKENS, SIDE), core
    )[0]
    for k in range(STEPS):
        inv_s[k] = jnp.broadcast_to(side[:, k : k + 1], (TOKENS, SIDE))
    for k, j in ((0, STEPS), (STEPS - 1, STEPS + 1)):
        inv_s[j] = 1.0 / inv_s[k]
    tot = jnp.zeros((TOKENS, SIDE), F32)
    s_0 = jnp.zeros((TOKENS, SIDE), F32)
    s_1 = jnp.zeros((TOKENS, SIDE), F32)
    half = TOKENS // 2
    for start in range(0, LAT_LOCAL, SIDE):
        cols = slice(start, start + SIDE)
        pre_0, pre_3 = by_step(pre_ref[:, cols], pre_s[:, cols], core)
        act = active_ref[:, cols].astype(F32)
        gf = [gf_ref[k, :, cols] for k in range(STEPS)]
        raw = act * (pre_3 - pre_0) * (((gf[0] + gf[1]) + (gf[2] + gf[3])) * 0.25)
        raw_ref[:, cols] = raw
        tot = tot + jnp.abs(raw)
        q_0 = act * (pre_0 - resid_ref[0, :, cols]) * inv_s[STEPS]
        q_d = act * (pre_3 - resid_ref[1, :, cols]) * inv_s[STEPS + 1] - q_0
        hidden = jnp.zeros((TOKENS, SIDE), F32)
        for k in range(STEPS):
            inv = inv_s[k]
            scaled = inv * gf[k]
            hidden = hidden + scaled
            term = inv * inv * scaled * (q_0 + ALPHAS[k] * q_d)
            s_0 = s_0 + term
            s_1 = s_1 + ALPHAS[k] * term
        own, other = by_core(act * hidden, core)
        hidden_s[:half, cols] = own.astype(BF16)
        hidden_s[half:, cols] = other.astype(BF16)
    grad = nt(hidden_s[...], w_ref[...])
    keep_ref[:, :D] = grad[:half]
    send_ref[:, :D] = grad[half:]
    row = lax.broadcasted_iota(jnp.int32, (TOKENS, SIDE), 0)
    lane = lax.broadcasted_iota(jnp.int32, (TOKENS, SIDE), 1)
    tot = jnp.sum(tot, axis=1, keepdims=True)
    tot_row = jnp.sum(jnp.where(row == lane, tot, 0.0), axis=0, keepdims=True)
    tot_all = jnp.broadcast_to(tot_row, (half, SIDE))
    s_0 = jnp.sum(s_0, axis=1, keepdims=True)
    s_1 = jnp.sum(s_1, axis=1, keepdims=True)
    own, other = by_core(jnp.where(lane == 0, s_0, jnp.where(lane == 1, s_1, 0.0)), core)
    keep_ref[:, D : D + SIDE] = tot_all
    send_ref[:, D : D + SIDE] = tot_all
    keep_ref[:, D + SIDE :] = own
    send_ref[:, D + SIDE :] = other


def latents(x_own, x_other, pre_own, resid, gf, active, w_enc):
    half = TOKENS // 2
    return call(
        latents_kernel,
        "latents",
        (x_own, x_other, pre_own, resid, gf, active, w_enc),
        [((TOKENS, LAT_LOCAL), F32), ((half, RED), F32), ((half, RED), F32)],
        [
            VMEM((TOKENS, LAT_LOCAL), F32),
            VMEM((TOKENS, LAT_LOCAL), BF16),
            VMEM((STEPS + 2, TOKENS, SIDE), F32),
        ],
        flops=4 * 128 * 1024 * D,
    )


def pair_kernel(a_ref, b_ref, out_ref):
    up = lax.broadcasted_iota(jnp.int32, (8, HALF), 0) >= OWN
    for g in range(PLANE // 2):
        tile = a_ref[8 * g : 8 * g + 8, :] + b_ref[8 * g : 8 * g + 8, :]
        left, right = tile[:, :HALF], tile[:, HALF:]
        out_ref[2 * g] = jnp.where(up, pltpu.roll(right, OWN, 0), left)
        out_ref[2 * g + 1] = jnp.where(up, right, pltpu.roll(left, OWN, 0))


def pair_sum(keep, received):
    return call(pair_kernel, "pair_sum", (keep, received), [((PLANE, 8, HALF), F32)])[0]


def plane_kernel(x_ref, out_ref):
    total = x_ref[0]
    for g in range(1, PLANE):
        total = total + x_ref[g]
    out_ref[...] = total


def plane_sum(x):
    return call(plane_kernel, "plane_sum", (x,), [((8, HALF), F32)])[0]


def result_kernel(
    a_ref, b_ref, c_ref, d_ref, attn_ref, heads_ref, gain_ref, raw_ref, latent_ref, head_ref
):
    total = (a_ref[...] + b_ref[...]) + (c_ref[...] + d_ref[...])
    rest = D - HALF
    g_left, g_right = total[:OWN], total[OWN:, :rest]
    tot_row = total[OWN : OWN + 1, rest : rest + SIDE]
    sums = total[OWN:, rest + SIDE :]
    s_0 = sums[:, 0:1] * (1.0 / D)
    s_1 = sums[:, 1:2] * (1.0 / D)
    head = jnp.zeros((OWN, HEADS_LOCAL), F32)
    lane = lax.broadcasted_iota(jnp.int32, (OWN, HEADS_LOCAL), 1)
    for part, cols in ((g_left, slice(0, HALF)), (g_right, slice(HALF, D))):
        a_0 = attn_ref[:OWN, cols]
        vec = gain_ref[:, cols] * part - (s_0 * a_0 + s_1 * (attn_ref[OWN:, cols] - a_0))
        for h in range(HEADS_LOCAL):
            v = heads_ref[h, OWN:, cols] - heads_ref[h, :OWN, cols]
            dots = jnp.sum(vec * v, axis=1, keepdims=True)
            head = head + jnp.where(lane == h, dots, 0.0)
    head_ref[...] = head * (1.0 / (HEAD_DIM * STEPS))
    row = lax.broadcasted_iota(jnp.int32, (TOKENS, SIDE), 0)
    col = lax.broadcasted_iota(jnp.int32, (TOKENS, SIDE), 1)
    tot = jnp.sum(jnp.where(row == col, tot_row, 0.0), axis=1, keepdims=True)
    latent_ref[...] = raw_ref[...] * (1.0 / (tot * (1.0 / LAT) + EPSILON))


def result(parts, attn, heads, gain, raw):
    return call(
        result_kernel,
        "result",
        (*parts, attn, heads, gain, raw),
        [((TOKENS, LAT_LOCAL), F32), ((OWN, HEADS_LOCAL), F32)],
    )


def over_tp(x):
    others = [lax.ppermute(x, "tp", [(i, (i + d) % 4) for i in range(4)]) for d in (1, 3, 2)]
    return [x] + others


def body(
    z_clean, z_corrupt, resid_clean, resid_corrupt, w_out, post_gain, w_enc, w_dec, cot, active
):
    gain = post_gain.reshape(1, D)
    heads, part = project(z_corrupt, z_clean, w_out)
    parts = over_tp(part)
    resid = resid_project(resid_corrupt, resid_clean, w_enc)
    parts, resid = lax.optimization_barrier((parts, resid))
    attn, msg = norm(parts, resid_corrupt, resid_clean, gain)
    x_own = lax.all_to_all(msg, "lat", 0, 0, axis_index_groups=PLANES)
    x_other = lax.ppermute(x_own, "lat", CORE_SWAP)
    gf = grad_f(cot, w_dec)
    pre_own = own_project(x_own, w_enc)
    raw, keep, send = latents(x_own, x_other, pre_own, resid, gf, active, w_enc)
    received = lax.ppermute(send, "lat", CORE_SWAP)
    shares = pair_sum(keep, received)
    shares = lax.all_to_all(shares, "lat", 0, 0, axis_index_groups=PLANES)
    shares = over_tp(plane_sum(shares))
    return tuple(result(shares, attn, heads, gain, raw))


def solution(mesh):
    placed = (
        P(None, "tp"),
        P(None, "tp"),
        P(),
        P(),
        P("tp", None),
        P(),
        P(None, ("lat", "tp")),
        P(("lat", "tp"), None),
        P(),
        P(None, ("lat", "tp")),
    )
    return jax.shard_map(
        body,
        mesh=mesh,
        in_specs=placed,
        out_specs=(P(None, ("lat", "tp")), P("lat", "tp")),
        check_vma=False,
    )
```

time: 455 us -> 94.6 us (0.21)
  waiting for transfers between devices: 262 us -> 7.72 us
  matrix products: 54.4 us -> 0 us
  local copies, waits for them, and re-layouts: 41.7 us -> 6.02 us
  Pallas kernels: 0 us -> 16.1 us
  other arithmetic: 16 us -> 0 us
  between operations: 14.2 us -> 0.78 us
  blocking collectives: 65 us -> 53.2 us
  starting transfers between devices: 0.26 us -> 10.6 us
    psum x2 -> x0, waiting for transfers between devices: 262 us -> none  [the longest x1 145 us: body(): attn_out = lax.psum(partial_out, 'tp')]
    psum x1 -> x0, blocking collectives: 65 us -> none  [body(): grad_mid, token_total = lax.psum((partial_grad, local_total), ('lat', 'tp'))]
    dot_general x5 -> x0, matrix products: 54.4 us -> none  [the longest x3 28.2 us: contract_last(): lax.dot_general(left_side, right_side, (((1,), (1,)), ((), ())), preferre...]
    all_to_all x0 -> x2, blocking collectives: none -> 53.2 us  [the longest x1 32.6 us: body(): x_own = lax.all_to_all(msg, 'lat', 0, 0, axis_index_groups=PLANES)]
    pallas_call x0 -> x9, Pallas kernels: none -> 16.1 us  [call(): pl.pallas_call(kernel, in_specs=[pl.BlockSpec(memory_space=s) for s in sp...]
    mul x6 -> x0, local copies, waits for them, and re-layouts: 15.8 us -> none  [interpolate(): alphas[None, :, None] * (clean_f - corrupt_f)[:, None, :]]
    add x4 -> x0, local copies, waits for them, and re-layouts: 15.3 us -> none  [interpolate(): corrupt_f[:, None, :]]
    ppermute x0 -> x8, starting transfers between devices: none -> 10.6 us  [the longest x6 9.99 us: over_tp(): lax.ppermute(x, 'tp', [(i, (i + d) % 4) for i in range(4)])]
  transfers between devices with their start and end apart: 2 -> 8, of which waited for: 2 -> 5; matrix products, arithmetic and copies ran while one was open for 10% -> 0% of each run, Pallas kernels for 0% -> 8%
where the time goes in v1:
time: 94.6 us; the launch traced here: 94.4 us
  blocking collectives  53.2 us (56%)
  Pallas kernels  16.1 us (17%)
  starting transfers between devices  10.6 us (11%)
  waiting for transfers between devices  7.72 us (8%)
  local copies, waits for them, and re-layouts  6.02 us (6%)
    all_to_all x1, blocking collectives, body(): x_own = lax.all_to_all(msg, 'lat', 0, 0, axis_index_groups=PLANES)  32.6 us
    all_to_all x1, blocking collectives, body(): shares = lax.all_to_all(shares, 'lat', 0, 0, axis_index_groups=PLANES)  20.6 us
    pallas_call x9, Pallas kernels, call(): pl.pallas_call(kernel, in_specs=[pl.BlockSpec(memory_space=s) for s in sp...  16.1 us
    ppermute x6, starting transfers between devices, over_tp(): lax.ppermute(x, 'tp', [(i, (i + d) % 4) for i in range(4)])  9.99 us
    unnamed x22, local copies, waits for them, and re-layouts  6.01 us
    ppermute x6, waiting for transfers between devices, over_tp(): lax.ppermute(x, 'tp', [(i, (i + d) % 4) for i in range(4)])  5.52 us
    ppermute x1, waiting for transfers between devices, body(): received = lax.ppermute(send, 'lat', CORE_SWAP)  2.19 us
  transfers between devices with their start and end apart: 8, of which 5 were waited for; matrix products, arithmetic and copies ran while one was open for 0% of the time, Pallas kernels for 8%

profile of v1, /device:TPU:0, one launch (start us, length us, event | category | flops | bytes accessed | tf_op | source)
XLA Modules:
  0.0 94.4 jit_solution(3688643113197898982)
XLA Ops:
  0.7 1.1 %copy-done.5 = bf16[128,1024]{1,0:T(8,128)(2,1)S(1)} copy-done((bf16[128,1024]{1,0:T(8,128)(2,1)S(1)}, bf16[128,1024]{1,0:T(8,128)(2,1)}, u32[]{:S(2)}) %copy-start.5) | copy-done | bytes 262168
  1.7 1.2 %copy-done.6 = bf16[128,1024]{1,0:T(8,128)(2,1)S(1)} copy-done((bf16[128,1024]{1,0:T(8,128)(2,1)S(1)}, bf16[128,1024]{1,0:T(8,128)(2,1)}, u32[]{:S(2)}) %copy-start.6) | copy-done | bytes 262168
  2.9 3.6 %project.1 = (f32[4,8,3584]{2,1,0:T(8,128)S(1)}, f32[8,3584]{1,0:T(8,128)S(1)}) custom-call(bf16[128,1024]{1,0:T(8,128)(2,1)S(1)} %copy-done.5, bf16[128,1024]{1,0:T(8,128)(2,1)S(1)} %copy-done.6, bf16[1024,3584]{1,0:T(8,128)(2,1)} %w_ref.5), custom_call_target="tpu_custom_call" | custom-call | flops 117440512 | bytes 7864320 | tf_op jit(solution)/shard_map/project/pallas_call | solution.py:40
  6.5 3.4 %collective-permute-start.2 = (f32[8,3584]{1,0:T(8,128)S(1)}, f32[8,3584]{1,0:T(8,128)S(1)}, u32[]{:S(2)}, u32[]{:S(2)}) collective-permute-start(f32[8,3584]{1,0:T(8,128)S(1)} %get-tuple-element.15.a_ref), channel_id=1, source_target_pairs={{0,2},{1,3},{2,0},{3,1},{4,6},{5,7},{6,4},{7,5},{8,10},{9,11},{10,... | collective-permute-start | bytes 344072 | tf_op jit(solution)/shard_map/ppermute | solution.py:355
  9.9 1.1 %collective-permute-start.1 = (f32[8,3584]{1,0:T(8,128)S(1)}, f32[8,3584]{1,0:T(8,128)S(1)}, u32[]{:S(2)}, u32[]{:S(2)}) collective-permute-start(f32[8,3584]{1,0:T(8,128)S(1)} %get-tuple-element.15.a_ref), channel_id=1, source_target_pairs={{0,3},{1,0},{2,1},{3,2},{4,7},{5,4},{6,5},{7,6},{8,11},{9,8},{10,9... | collective-permute-start | bytes 344072 | tf_op jit(solution)/shard_map/ppermute | solution.py:355
  10.9 1.0 %collective-permute-start = (f32[8,3584]{1,0:T(8,128)S(1)}, f32[8,3584]{1,0:T(8,128)S(1)}, u32[]{:S(2)}, u32[]{:S(2)}) collective-permute-start(f32[8,3584]{1,0:T(8,128)S(1)} %get-tuple-element.15.a_ref), channel_id=1, source_target_pairs={{0,1},{1,2},{2,3},{3,0},{4,5},{5,6},{6,7},{7,4},{8,9},{9,10},{10,1... | collective-permute-start | bytes 344072 | tf_op jit(solution)/shard_map/ppermute | solution.py:355
  11.9 1.2 %copy-done.1 = bf16[128,3584]{1,0:T(8,128)(2,1)S(1)} copy-done((bf16[128,3584]{1,0:T(8,128)(2,1)S(1)}, bf16[128,3584]{1,0:T(8,128)(2,1)}, u32[]{:S(2)}) %copy-start.1) | copy-done | bytes 917528
  13.1 1.2 %copy-done.3 = bf16[128,3584]{1,0:T(8,128)(2,1)S(1)} copy-done((bf16[128,3584]{1,0:T(8,128)(2,1)S(1)}, bf16[128,3584]{1,0:T(8,128)(2,1)}, u32[]{:S(2)}) %copy-start.3) | copy-done | bytes 917528
  14.3 2.1 %resid_project.1.resid_ref = f32[2,128,1024]{2,1,0:T(8,128)S(1)} custom-call(bf16[128,3584]{1,0:T(8,128)(2,1)S(1)} %copy-done.1, bf16[128,3584]{1,0:T(8,128)(2,1)S(1)} %copy-done.3, bf16[3584,1024]{1,0:T(8,128)(2,1)S(1)} %copy-done), custom_call_target="tpu_custom_call" | custom-call | flops 1879048192 | bytes 9175040 | tf_op jit(solution)/shard_map/resid_project/pallas_call | solution.py:40
  16.4 0.5 collective-permute-done.b_ref
  17.4 32.6 %all_to_all.10.x_ref.own_ref = f32[16,8,3712]{2,1,0:T(8,128)S(1)} all-to-all(f32[16,8,3712]{2,1,0:T(8,128)S(1)} %get-tuple-element.19), channel_id=1, replica_groups={{0,8,16,24,32,40,48,56,64,72,80,88,96,104,112,120},{4,12,20,28,36,44,52..., dimensions={0} | all-to-all | bytes 3801088 | tf_op jit(solution)/shard_map/all_to_all | solution.py:368
  50.0 4.1 %grad_f.1.gf_ref = f32[4,128,1024]{2,1,0:T(8,128)S(1)} custom-call(bf16[128,4,3584]{2,1,0:T(4,128)(2,1)S(1)} %copy-done.8, bf16[1024,3584]{1,0:T(8,128)(2,1)S(1)} %copy-done.7), custom_call_target="tpu_custom_call" | custom-call | flops 3758096384 | bytes 11010048 | tf_op jit(solution)/shard_map/grad_f/pallas_call | solution.py:40
  54.1 1.1 %own_project.1.pre_ref = f32[128,1024]{1,0:T(8,128)S(1)} custom-call(f32[16,8,3712]{2,1,0:T(8,128)S(1)} %all_to_all.10.x_ref.own_ref, bf16[3584,1024]{1,0:T(8,128)(2,1)S(1)} %copy-done), custom_call_target="tpu_custom_call" | custom-call | flops 939524096 | bytes 9240576 | tf_op jit(solution)/shard_map/own_project/pallas_call | solution.py:40
  55.3 4.3 %latents.1 = (f32[128,1024]{1,0:T(8,128)S(1)}, f32[64,3840]{1,0:T(8,128)S(1)}, f32[64,3840]{1,0:T(8,128)S(1)}) custom-call(f32[16,8,3712]{2,1,0:T(8,128)S(1)} %all_to_all.10.x_ref.own_ref, f32[16,8,3712]{2,1,0:T(8,128)S(1)} %collective-permute-done.3.other_ref, f32[128,1024]{1,0:T(8,128)S(1)} %own_project.1.pre_ref, ...), custom_call_target="tpu_custom_call" | custom-call | flops 1879048192 | bytes 15335424 | tf_op jit(solution)/shard_map/latents/pallas_call | solution.py:40
  59.6 0.6 collective-permute-start.4
  60.2 2.2 %collective-permute-done.4.b_ref = f32[64,3840]{1,0:T(8,128)S(1)} collective-permute-done((f32[64,3840]{1,0:T(8,128)S(1)}, f32[64,3840]{1,0:T(8,128)S(1)}, u32[]{:S(2)}, u32[]{:S(2)}) %collective-permute-start.4) | collective-permute-done | bytes 983072 | tf_op jit(solution)/shard_map/ppermute | solution.py:373
  62.5 20.6 %all_to_all.11.x_ref = f32[16,8,1920]{2,1,0:T(8,128)S(1)} all-to-all(f32[16,8,1920]{2,1,0:T(8,128)S(1)} %pair_sum.1), channel_id=1, replica_groups={{0,8,16,24,32,40,48,56,64,72,80,88,96,104,112,120},{4,12,20,28,36,44,52..., dimensions={0} | all-to-all | bytes 1966080 | tf_op jit(solution)/shard_map/all_to_all | solution.py:375
  83.1 2.6 %collective-permute-start.7 = (f32[8,1920]{1,0:T(8,128)S(1)}, f32[8,1920]{1,0:T(8,128)S(1)}, u32[]{:S(2)}, u32[]{:S(2)}) collective-permute-start(f32[8,1920]{1,0:T(8,128)S(1)} %plane_sum.1.a_ref), channel_id=1, source_target_pairs={{0,2},{1,3},{2,0},{3,1},{4,6},{5,7},{6,4},{7,5},{8,10},{9,11},{10,... | collective-permute-start | bytes 184328 | tf_op jit(solution)/shard_map/ppermute | solution.py:355
  85.7 1.6 %collective-permute-start.6 = (f32[8,1920]{1,0:T(8,128)S(1)}, f32[8,1920]{1,0:T(8,128)S(1)}, u32[]{:S(2)}, u32[]{:S(2)}) collective-permute-start(f32[8,1920]{1,0:T(8,128)S(1)} %plane_sum.1.a_ref), channel_id=1, source_target_pairs={{0,3},{1,0},{2,1},{3,2},{4,7},{5,4},{6,5},{7,6},{8,11},{9,8},{10,9... | collective-permute-start | bytes 184328 | tf_op jit(solution)/shard_map/ppermute | solution.py:355
  87.7 1.2 %collective-permute-done.7.d_ref = f32[8,1920]{1,0:T(8,128)S(1)} collective-permute-done((f32[8,1920]{1,0:T(8,128)S(1)}, f32[8,1920]{1,0:T(8,128)S(1)}, u32[]{:S(2)}, u32[]{:S(2)}) %collective-permute-start.7) | collective-permute-done | bytes 61472 | tf_op jit(solution)/shard_map/ppermute | solution.py:355
  88.9 1.0 %collective-permute-done.6.c_ref = f32[8,1920]{1,0:T(8,128)S(1)} collective-permute-done((f32[8,1920]{1,0:T(8,128)S(1)}, f32[8,1920]{1,0:T(8,128)S(1)}, u32[]{:S(2)}, u32[]{:S(2)}) %collective-permute-start.6) | collective-permute-done | bytes 61472 | tf_op jit(solution)/shard_map/ppermute | solution.py:355
  89.9 2.8 %collective-permute-done.5.b_ref = f32[8,1920]{1,0:T(8,128)S(1)} collective-permute-done((f32[8,1920]{1,0:T(8,128)S(1)}, f32[8,1920]{1,0:T(8,128)S(1)}, u32[]{:S(2)}, u32[]{:S(2)}) %collective-permute-start.5) | collective-permute-done | bytes 61472 | tf_op jit(solution)/shard_map/ppermute | solution.py:355
  93.0 0.8 copy.12
  93.8 0.6 copy.13
  (26 shorter events, 1.3 us)
Async XLA Ops:
  0.6 11.3 %copy-start = (bf16[3584,1024]{1,0:T(8,128)(2,1)S(1)}, bf16[3584,1024]{1,0:T(8,128)(2,1)}, u32[]{:S(2)}) copy-start(bf16[3584,1024]{1,0:T(8,128)(2,1)} %w_ref.9) | copy-start | bytes 22020100
  0.6 1.1 %copy-start.5 = (bf16[128,1024]{1,0:T(8,128)(2,1)S(1)}, bf16[128,1024]{1,0:T(8,128)(2,1)}, u32[]{:S(2)}) copy-start(bf16[128,1024]{1,0:T(8,128)(2,1)} %zc_ref.1) | copy-start | bytes 786436
  1.7 1.2 %copy-start.6 = (bf16[128,1024]{1,0:T(8,128)(2,1)S(1)}, bf16[128,1024]{1,0:T(8,128)(2,1)}, u32[]{:S(2)}) copy-start(bf16[128,1024]{1,0:T(8,128)(2,1)} %zn_ref.1) | copy-start | bytes 786436
  2.9 9.0 %copy-start.9 = (f32[3584]{0:T(1024)S(1)}, f32[3584]{0:T(1024)}, u32[]{:S(2)}) copy-start(f32[3584]{0:T(1024)} %param.15) | copy-start | bytes 43012
  6.5 9.9 %collective-permute-start.2 = (f32[8,3584]{1,0:T(8,128)S(1)}, f32[8,3584]{1,0:T(8,128)S(1)}, u32[]{:S(2)}, u32[]{:S(2)}) collective-permute-start(f32[8,3584]{1,0:T(8,128)S(1)} %get-tuple-element.15.a_ref), channel_id=1, source_target_pairs={{0,2},{1,3},{2,0},{3,1},{4,6},{5,7},{6,4},{7,5},{8,10},{9,11},{10,... | collective-permute-start | bytes 344072 | tf_op jit(solution)/shard_map/ppermute | solution.py:355
  9.9 6.5 %collective-permute-start.1 = (f32[8,3584]{1,0:T(8,128)S(1)}, f32[8,3584]{1,0:T(8,128)S(1)}, u32[]{:S(2)}, u32[]{:S(2)}) collective-permute-start(f32[8,3584]{1,0:T(8,128)S(1)} %get-tuple-element.15.a_ref), channel_id=1, source_target_pairs={{0,3},{1,0},{2,1},{3,2},{4,7},{5,4},{6,5},{7,6},{8,11},{9,8},{10,9... | collective-permute-start | bytes 344072 | tf_op jit(solution)/shard_map/ppermute | solution.py:355
  10.9 6.0 %collective-permute-start = (f32[8,3584]{1,0:T(8,128)S(1)}, f32[8,3584]{1,0:T(8,128)S(1)}, u32[]{:S(2)}, u32[]{:S(2)}) collective-permute-start(f32[8,3584]{1,0:T(8,128)S(1)} %get-tuple-element.15.a_ref), channel_id=1, source_target_pairs={{0,1},{1,2},{2,3},{3,0},{4,5},{5,6},{6,7},{7,4},{8,9},{9,10},{10,1... | collective-permute-start | bytes 344072 | tf_op jit(solution)/shard_map/ppermute | solution.py:355
  11.9 1.2 %copy-start.1 = (bf16[128,3584]{1,0:T(8,128)(2,1)S(1)}, bf16[128,3584]{1,0:T(8,128)(2,1)}, u32[]{:S(2)}) copy-start(bf16[128,3584]{1,0:T(8,128)(2,1)} %rc_ref.3) | copy-start | bytes 2752516
  13.1 1.2 %copy-start.3 = (bf16[128,3584]{1,0:T(8,128)(2,1)S(1)}, bf16[128,3584]{1,0:T(8,128)(2,1)}, u32[]{:S(2)}) copy-start(bf16[128,3584]{1,0:T(8,128)(2,1)} %rn_ref.3) | copy-start | bytes 2752516
  14.3 2.6 %copy-start.2 = (bf16[128,3584]{1,0:T(8,128)(2,1)S(1)}, bf16[128,3584]{1,0:T(8,128)(2,1)}, u32[]{:S(2)}) copy-start(bf16[128,3584]{1,0:T(8,128)(2,1)} %rc_ref.3) | copy-start | bytes 2752516
  14.3 35.7 %copy-start.7 = (bf16[1024,3584]{1,0:T(8,128)(2,1)S(1)}, bf16[1024,3584]{1,0:T(8,128)(2,1)}, u32[]{:S(2)}) copy-start(bf16[1024,3584]{1,0:T(8,128)(2,1)} %w_ref.8) | copy-start | bytes 22020100
  16.4 33.6 %copy-start.8 = (bf16[128,4,3584]{2,1,0:T(4,128)(2,1)S(1)}, bf16[128,4,3584]{2,1,0:T(4,128)(2,1)}, u32[]{:S(2)}) copy-start(bf16[128,4,3584]{2,1,0:T(4,128)(2,1)} %cot_ref.1) | copy-start | bytes 11010052
  50.0 5.3 %collective-permute-start.3 = (f32[16,8,3712]{2,1,0:T(8,128)S(1)}, f32[16,8,3712]{2,1,0:T(8,128)S(1)}, u32[]{:S(2)}, u32[]{:S(2)}) collective-permute-start(f32[16,8,3712]{2,1,0:T(8,128)S(1)} %all_to_all.10.x_ref.own_ref), channel_id=1, source_target_pairs={{0,4},{4,0},{8,12},{12,8},{16,20},{20,16},{24,28},{28,24},{32,36},... | collective-permute-start | bytes 5701640 | tf_op jit(solution)/shard_map/ppermute | solution.py:369
  54.1 1.2 %copy-start.4 = (s32[128,1024]{1,0:T(8,128)S(1)}, s32[128,1024]{1,0:T(8,128)}, u32[]{:S(2)}) copy-start(s32[128,1024]{1,0:T(8,128)} %active_ref.1) | copy-start | bytes 1572868
  59.6 2.8 %collective-permute-start.4 = (f32[64,3840]{1,0:T(8,128)S(1)}, f32[64,3840]{1,0:T(8,128)S(1)}, u32[]{:S(2)}, u32[]{:S(2)}) collective-permute-start(f32[64,3840]{1,0:T(8,128)S(1)} %get-tuple-element.22), channel_id=1, source_target_pairs={{0,4},{4,0},{8,12},{12,8},{16,20},{20,16},{24,28},{28,24},{32,36},... | collective-permute-start | bytes 2949128 | tf_op jit(solution)/shard_map/ppermute | solution.py:373
  83.1 5.8 %collective-permute-start.7 = (f32[8,1920]{1,0:T(8,128)S(1)}, f32[8,1920]{1,0:T(8,128)S(1)}, u32[]{:S(2)}, u32[]{:S(2)}) collective-permute-start(f32[8,1920]{1,0:T(8,128)S(1)} %plane_sum.1.a_ref), channel_id=1, source_target_pairs={{0,2},{1,3},{2,0},{3,1},{4,6},{5,7},{6,4},{7,5},{8,10},{9,11},{10,... | collective-permute-start | bytes 184328 | tf_op jit(solution)/shard_map/ppermute | solution.py:355
  85.7 4.2 %collective-permute-start.6 = (f32[8,1920]{1,0:T(8,128)S(1)}, f32[8,1920]{1,0:T(8,128)S(1)}, u32[]{:S(2)}, u32[]{:S(2)}) collective-permute-start(f32[8,1920]{1,0:T(8,128)S(1)} %plane_sum.1.a_ref), channel_id=1, source_target_pairs={{0,3},{1,0},{2,1},{3,2},{4,7},{5,4},{6,5},{7,6},{8,11},{9,8},{10,9... | collective-permute-start | bytes 184328 | tf_op jit(solution)/shard_map/ppermute | solution.py:355
  87.3 5.4 %collective-permute-start.5 = (f32[8,1920]{1,0:T(8,128)S(1)}, f32[8,1920]{1,0:T(8,128)S(1)}, u32[]{:S(2)}, u32[]{:S(2)}) collective-permute-start(f32[8,1920]{1,0:T(8,128)S(1)} %plane_sum.1.a_ref), channel_id=1, source_target_pairs={{0,1},{1,2},{2,3},{3,0},{4,5},{5,6},{6,7},{7,4},{8,9},{9,10},{10,1... | collective-permute-start | bytes 184328 | tf_op jit(solution)/shard_map/ppermute | solution.py:355

commit v2 on v1

--- a/solution.py
+++ b/solution.py
@@ -30,18 +30,33 @@
     return ((x % 4) * 4 + z % 4) * 2 + core
 
 
-PLANES = [[lat_index(x, z, c) for x in range(4) for z in range(4)] for c in range(2)]
+def shift(stage, d):
+    pairs = []
+    for x in range(4):
+        for z in range(4):
+            for core in range(2):
+                along_x = (stage == 0) == (core == 0)
+                to = (x + d, z) if along_x else (x, z + d)
+                pairs.append((lat_index(x, z, core), lat_index(*to, core)))
+    return pairs
+
+
 CORE_SWAP = [(i, i ^ 1) for i in range(32)]
 
 
-def call(kernel, name, operands, outs, scratch=(), mib=8, flops=10**6, hbm=()):
+def place():
+    index = lax.axis_index("lat")
+    return index // 8, (index // 2) % 4, index % 2
+
+
+def call(kernel, name, operands, outs, scratch=(), mib=8, flops=10**6, hbm=(), final=False):
     spaces = [pltpu.HBM if i in hbm else VMEM for i in range(len(operands))]
     nbytes = sum(x.size * x.dtype.itemsize for x in operands)
     return pl.pallas_call(
         kernel,
         in_specs=[pl.BlockSpec(memory_space=s) for s in spaces],
         out_specs=[pl.BlockSpec(memory_space=VMEM)] * len(outs),
-        out_shape=[VMEM(shape, dtype) for shape, dtype in outs],
+        out_shape=[(jax.ShapeDtypeStruct if final else VMEM)(shape, dtype) for shape, dtype in outs],
         scratch_shapes=list(scratch),
         compiler_params=pltpu.CompilerParams(vmem_limit_bytes=mib * MIB),
         cost_estimate=pl.CostEstimate(flops=flops, bytes_accessed=nbytes, transcendentals=0),
@@ -57,18 +72,28 @@
     return lax.dot_general(a, b, (((1,), (0,)), ((), ())), preferred_element_type=F32)
 
 
-def project_kernel(zc_ref, zn_ref, w_ref, heads_ref, part_ref, w_s, sems):
+def project_kernel(zc_ref, zn_ref, w_ref, heads_ref, part_ref, z_s, w_s, z_sems, sems):
+    index = lax.axis_index("lat")
+    block = pl.ds(pl.multiple_of((index // 4) * 16, 16), 16)
+    z_copies = [
+        pltpu.make_async_copy(ref.at[block, :], z_s.at[i], z_sems.at[i])
+        for i, ref in enumerate((zc_ref, zn_ref))
+    ]
+    for copy in z_copies:
+        copy.start()
     copies = []
     for h in range(HEADS_LOCAL):
         rows = pl.ds(h * HEAD_DIM, HEAD_DIM)
         copies.append(pltpu.make_async_copy(w_ref.at[rows, :], w_s.at[rows, :], sems.at[h]))
         copies[-1].start()
-    first = lax.axis_index("lat") * OWN
-    row = lax.broadcasted_iota(jnp.int32, (16, TOKENS), 0)
-    token = lax.broadcasted_iota(jnp.int32, (16, TOKENS), 1)
+    first = (index % 4) * OWN
+    row = lax.broadcasted_iota(jnp.int32, (16, 16), 0)
+    token = lax.broadcasted_iota(jnp.int32, (16, 16), 1)
     pick_c = ((row < OWN) & (token == first + row)).astype(F32).astype(BF16)
     pick_n = ((row >= OWN) & (row < 2 * OWN) & (token == first + row - OWN)).astype(F32).astype(BF16)
-    z = (nn(pick_c, zc_ref[...]) + nn(pick_n, zn_ref[...])).astype(BF16)
+    for copy in z_copies:
+        copy.wait()
+    z = (nn(pick_c, z_s[0]) + nn(pick_n, z_s[1])).astype(BF16)
     for h in range(HEADS_LOCAL):
         copies[h].wait()
         cols = slice(h * HEAD_DIM, (h + 1) * HEAD_DIM)
@@ -86,10 +111,15 @@
         "project",
         (z_corrupt, z_clean, w_out),
         [((HEADS_LOCAL, 2 * OWN, D), F32), ((2 * OWN, D), F32)],
-        [VMEM((1024, D), BF16), pltpu.SemaphoreType.DMA((HEADS_LOCAL,))],
+        [
+            VMEM((2, 16, 1024), BF16),
+            VMEM((1024, D), BF16),
+            pltpu.SemaphoreType.DMA((2,)),
+            pltpu.SemaphoreType.DMA((HEADS_LOCAL,)),
+        ],
         mib=12,
         flops=2 * 16 * 1024 * D,
-        hbm=(2,),
+        hbm=(0, 1, 2),
     )
 
 
@@ -142,9 +172,8 @@
     low = lax.broadcasted_iota(jnp.int32, (2 * OWN, 1), 0) < OWN
     own_inv = jnp.where(low, invs[0], invs[3])
     sae_in = resid + attn * own_inv * gain_ref[...]
-    for g in range(PLANE):
-        msg_ref[g, :, :D] = sae_in
-        msg_ref[g, :, D:] = side
+    msg_ref[:, :D] = sae_in
+    msg_ref[:, D:] = side
 
 
 def norm(parts, resid_corrupt, resid_clean, gain):
@@ -152,8 +181,26 @@
         norm_kernel,
         "norm",
         (*parts, resid_corrupt, resid_clean, gain),
-        [((2 * OWN, D), F32), ((PLANE, 2 * OWN, MSG), F32)],
-    )
+        [((2 * OWN, D), F32), ((2 * OWN, MSG), F32)],
+    )
+
+
+def line_kernel(a_ref, b_ref, c_ref, d_ref, out_ref):
+    for d, ref in enumerate((a_ref, b_ref, c_ref, d_ref)):
+        out_ref[d] = ref[...]
+
+
+def line(parts):
+    return call(line_kernel, "line", parts, [((4, 2 * OWN, MSG), F32)])[0]
+
+
+def assemble(refs, core, out):
+    x, z, _ = place()
+    for e, ref in enumerate(refs):
+        for d in range(4):
+            from_x = (x + 4 - jnp.where(core == 0, d, e)) % 4
+            from_z = (z + 4 - jnp.where(core == 0, e, d)) % 4
+            out[from_x * 4 + from_z] = ref[d]
 
 
 def resid_kernel(rc_ref, rn_ref, w_ref, out_ref):
@@ -171,18 +218,21 @@
     )[0]
 
 
-def own_kernel(x_ref, w_ref, out_ref):
-    out_ref[...] = nn(x_ref[:, :, :D].reshape(TOKENS, D).astype(BF16), w_ref[...])
-
-
-def own_project(x_own, w_enc):
+def own_kernel(a_ref, b_ref, c_ref, d_ref, w_ref, out_ref, side_ref, rows):
+    assemble((a_ref, b_ref, c_ref, d_ref), place()[2], rows)
+    side_ref[...] = rows[:, :, D:]
+    out_ref[...] = nn(rows[:, :, :D].reshape(TOKENS, D).astype(BF16), w_ref[...])
+
+
+def own_project(blocks, w_enc):
     return call(
         own_kernel,
         "own_project",
-        (x_own, w_enc),
-        [((TOKENS, LAT_LOCAL), F32)],
+        (*blocks, w_enc),
+        [((TOKENS, LAT_LOCAL), F32), ((PLANE, 2 * OWN, SIDE), F32)],
+        [VMEM((PLANE, 2 * OWN, MSG), F32)],
         flops=2 * 128 * 1024 * D,
-    )[0]
+    )
 
 
 def upper_rows(width):
@@ -221,14 +271,15 @@
 
 
 def latents_kernel(
-    own_ref, other_ref, pre_ref, resid_ref, gf_ref, active_ref, w_ref,
+    a_ref, b_ref, c_ref, d_ref, side_ref, pre_ref, resid_ref, gf_ref, active_ref, w_ref,
     raw_ref, keep_ref, send_ref,
-    pre_s, hidden_s, inv_s,
+    other, pre_s, hidden_s, inv_s,
 ):
-    core = lax.axis_index("lat") % 2
-    pre_s[...] = nn(other_ref[:, :, :D].reshape(TOKENS, D).astype(BF16), w_ref[...])
+    core = place()[2]
+    assemble((a_ref, b_ref, c_ref, d_ref), 1 - core, other)
+    pre_s[...] = nn(other[:, :, :D].reshape(TOKENS, D).astype(BF16), w_ref[...])
     side = by_step(
-        own_ref[:, :, D:].reshape(TOKENS, SIDE), other_ref[:, :, D:].reshape(TOKENS, SIDE), core
+        side_ref[...].reshape(TOKENS, SIDE), other[:, :, D:].reshape(TOKENS, SIDE), core
     )[0]
     for k in range(STEPS):
         inv_s[k] = jnp.broadcast_to(side[:, k : k + 1], (TOKENS, SIDE))
@@ -256,9 +307,9 @@
             term = inv * inv * scaled * (q_0 + ALPHAS[k] * q_d)
             s_0 = s_0 + term
             s_1 = s_1 + ALPHAS[k] * term
-        own, other = by_core(act * hidden, core)
-        hidden_s[:half, cols] = own.astype(BF16)
-        hidden_s[half:, cols] = other.astype(BF16)
+        first, second = by_core(act * hidden, core)
+        hidden_s[:half, cols] = first.astype(BF16)
+        hidden_s[half:, cols] = second.astype(BF16)
     grad = nt(hidden_s[...], w_ref[...])
     keep_ref[:, :D] = grad[:half]
     send_ref[:, :D] = grad[half:]
@@ -269,21 +320,22 @@
     tot_all = jnp.broadcast_to(tot_row, (half, SIDE))
     s_0 = jnp.sum(s_0, axis=1, keepdims=True)
     s_1 = jnp.sum(s_1, axis=1, keepdims=True)
-    own, other = by_core(jnp.where(lane == 0, s_0, jnp.where(lane == 1, s_1, 0.0)), core)
+    first, second = by_core(jnp.where(lane == 0, s_0, jnp.where(lane == 1, s_1, 0.0)), core)
     keep_ref[:, D : D + SIDE] = tot_all
     send_ref[:, D : D + SIDE] = tot_all
-    keep_ref[:, D + SIDE :] = own
-    send_ref[:, D + SIDE :] = other
-
-
-def latents(x_own, x_other, pre_own, resid, gf, active, w_enc):
+    keep_ref[:, D + SIDE :] = first
+    send_ref[:, D + SIDE :] = second
+
+
+def latents(others, side, pre_own, resid, gf, active, w_enc):
     half = TOKENS // 2
     return call(
         latents_kernel,
         "latents",
-        (x_own, x_other, pre_own, resid, gf, active, w_enc),
+        (*others, side, pre_own, resid, gf, active, w_enc),
         [((TOKENS, LAT_LOCAL), F32), ((half, RED), F32), ((half, RED), F32)],
         [
+            VMEM((PLANE, 2 * OWN, MSG), F32),
             VMEM((TOKENS, LAT_LOCAL), F32),
             VMEM((TOKENS, LAT_LOCAL), BF16),
             VMEM((STEPS + 2, TOKENS, SIDE), F32),
@@ -292,28 +344,51 @@
     )
 
 
-def pair_kernel(a_ref, b_ref, out_ref):
+def pair_kernel(a_ref, b_ref, p0_ref, p1_ref, p2_ref, p3_ref, packed):
     up = lax.broadcasted_iota(jnp.int32, (8, HALF), 0) >= OWN
     for g in range(PLANE // 2):
         tile = a_ref[8 * g : 8 * g + 8, :] + b_ref[8 * g : 8 * g + 8, :]
         left, right = tile[:, :HALF], tile[:, HALF:]
-        out_ref[2 * g] = jnp.where(up, pltpu.roll(right, OWN, 0), left)
-        out_ref[2 * g + 1] = jnp.where(up, right, pltpu.roll(left, OWN, 0))
+        packed[2 * g] = jnp.where(up, pltpu.roll(right, OWN, 0), left)
+        packed[2 * g + 1] = jnp.where(up, right, pltpu.roll(left, OWN, 0))
+    x, z, core = place()
+    for d, ref in enumerate((p0_ref, p1_ref, p2_ref, p3_ref)):
+        for b in range(4):
+            to_x = jnp.where(core == 0, (x + d) % 4, b)
+            to_z = jnp.where(core == 0, b, (z + d) % 4)
+            ref[b] = packed[to_x * 4 + to_z]
 
 
 def pair_sum(keep, received):
-    return call(pair_kernel, "pair_sum", (keep, received), [((PLANE, 8, HALF), F32)])[0]
-
-
-def plane_kernel(x_ref, out_ref):
-    total = x_ref[0]
-    for g in range(1, PLANE):
-        total = total + x_ref[g]
-    out_ref[...] = total
-
-
-def plane_sum(x):
-    return call(plane_kernel, "plane_sum", (x,), [((8, HALF), F32)])[0]
+    return call(
+        pair_kernel,
+        "pair_sum",
+        (keep, received),
+        [((4, 8, HALF), F32)] * 4,
+        [VMEM((PLANE, 8, HALF), F32)],
+    )
+
+
+def line_sum_kernel(a_ref, b_ref, c_ref, d_ref, p0_ref, p1_ref, p2_ref, p3_ref, total):
+    total[...] = (a_ref[...] + b_ref[...]) + (c_ref[...] + d_ref[...])
+    x, z, core = place()
+    own = jnp.where(core == 0, z, x)
+    for e, ref in enumerate((p0_ref, p1_ref, p2_ref, p3_ref)):
+        ref[...] = total[(own + e) % 4]
+
+
+def line_sum(parts):
+    return call(
+        line_sum_kernel, "line_sum", parts, [((8, HALF), F32)] * 4, [VMEM((4, 8, HALF), F32)]
+    )
+
+
+def plane_kernel(a_ref, b_ref, c_ref, d_ref, out_ref):
+    out_ref[...] = (a_ref[...] + b_ref[...]) + (c_ref[...] + d_ref[...])
+
+
+def plane_sum(parts):
+    return call(plane_kernel, "plane_sum", parts, [((8, HALF), F32)])[0]
 
 
 def result_kernel(
@@ -348,6 +423,7 @@
         "result",
         (*parts, attn, heads, gain, raw),
         [((TOKENS, LAT_LOCAL), F32), ((OWN, HEADS_LOCAL), F32)],
+        final=True,
     )
 
 
@@ -356,25 +432,36 @@
     return [x] + others
 
 
+def send(x, stage, d):
+    return lax.ppermute(x, "lat", shift(stage, d))
+
+
+def swap(x):
+    return lax.ppermute(x, "lat", CORE_SWAP)
+
+
 def body(
     z_clean, z_corrupt, resid_clean, resid_corrupt, w_out, post_gain, w_enc, w_dec, cot, active
 ):
+    heads, part = project(z_corrupt, z_clean, w_out)
+    part, post_gain, resid_clean, resid_corrupt, w_enc, w_dec, cot, active = lax.optimization_barrier(
+        (part, post_gain, resid_clean, resid_corrupt, w_enc, w_dec, cot, active)
+    )
     gain = post_gain.reshape(1, D)
-    heads, part = project(z_corrupt, z_clean, w_out)
-    parts = over_tp(part)
     resid = resid_project(resid_corrupt, resid_clean, w_enc)
-    parts, resid = lax.optimization_barrier((parts, resid))
+    *parts, resid = lax.optimization_barrier((*over_tp(part), resid))
     attn, msg = norm(parts, resid_corrupt, resid_clean, gain)
-    x_own = lax.all_to_all(msg, "lat", 0, 0, axis_index_groups=PLANES)
-    x_other = lax.ppermute(x_own, "lat", CORE_SWAP)
     gf = grad_f(cot, w_dec)
-    pre_own = own_project(x_own, w_enc)
-    raw, keep, send = latents(x_own, x_other, pre_own, resid, gf, active, w_enc)
-    received = lax.ppermute(send, "lat", CORE_SWAP)
-    shares = pair_sum(keep, received)
-    shares = lax.all_to_all(shares, "lat", 0, 0, axis_index_groups=PLANES)
-    shares = over_tp(plane_sum(shares))
-    return tuple(result(shares, attn, heads, gain, raw))
+    *parts, gf = lax.optimization_barrier((msg, *[send(msg, 0, d) for d in (1, 2, 3)], gf))
+    block = line(parts)
+    blocks = [block] + [send(block, 1, e) for e in (1, 2, 3)]
+    others = [swap(b) for b in blocks]
+    pre_own, side = own_project(blocks, w_enc)
+    raw, keep, give = latents(others, side, pre_own, resid, gf, active, w_enc)
+    parts = pair_sum(keep, swap(give))
+    parts = line_sum([parts[0]] + [send(parts[d], 0, d) for d in (1, 2, 3)])
+    total = plane_sum([parts[0]] + [send(parts[e], 1, e) for e in (1, 2, 3)])
+    return tuple(result(over_tp(total), attn, heads, gain, raw))
 
 
 def solution(mesh):

time: 94.6 us -> 82.7 us (0.87)
  blocking collectives: 53.2 us -> 0 us
  waiting for transfers between devices: 7.72 us -> 34.3 us
  starting transfers between devices: 10.6 us -> 26.7 us
  local copies, waits for them, and re-layouts: 6.02 us -> 2.39 us
  Pallas kernels: 16.1 us -> 18.3 us
    all_to_all x2 -> x0, blocking collectives: 53.2 us -> none  [the longest x1 32.6 us: body(): x_own = lax.all_to_all(msg, 'lat', 0, 0, axis_index_groups=PLANES)]
    ppermute x2 -> x17, waiting for transfers between devices: 2.2 us -> 29.2 us  [the longest x12 26.3 us: send(): return lax.ppermute(x, 'lat', shift(stage, d))]
    ppermute x2 -> x17, starting transfers between devices: 0.58 us -> 17.5 us  [the longest x12 16.7 us: send(): return lax.ppermute(x, 'lat', shift(stage, d))]
    unnamed x22 -> x16, local copies, waits for them, and re-layouts: 6.01 us -> 2.38 us
    pallas_call x9 -> x11, Pallas kernels: 16.1 us -> 18.3 us  [call(): pl.pallas_call(kernel, in_specs=[pl.BlockSpec(memory_space=s) for s in sp...]
  transfers between devices with their start and end apart: 8 -> 23, of which waited for: 5 -> 14; matrix products, arithmetic and copies ran while one was open for 0% -> 0% of each run, Pallas kernels for 8% -> 9%
where the time goes in v2:
time: 82.7 us; the launch traced here: 82.5 us
  waiting for transfers between devices  34.3 us (41%)
  starting transfers between devices  26.7 us (32%)
  Pallas kernels  18.3 us (22%)
  local copies, waits for them, and re-layouts  2.39 us (3%)
    ppermute x12, waiting for transfers between devices, send(): return lax.ppermute(x, 'lat', shift(stage, d))  26.3 us
    pallas_call x11, Pallas kernels, call(): pl.pallas_call(kernel, in_specs=[pl.BlockSpec(memory_space=s) for s in sp...  18.3 us
    ppermute x12, starting transfers between devices, send(): return lax.ppermute(x, 'lat', shift(stage, d))  16.7 us
    ppermute x6, starting transfers between devices, over_tp(): lax.ppermute(x, 'tp', [(i, (i + d) % 4) for i in range(4)])  9.25 us
    ppermute x6, waiting for transfers between devices, over_tp(): lax.ppermute(x, 'tp', [(i, (i + d) % 4) for i in range(4)])  5.12 us
    ppermute x5, waiting for transfers between devices, swap(): return lax.ppermute(x, 'lat', CORE_SWAP)  2.94 us
    unnamed x16, local copies, waits for them, and re-layouts  2.38 us
  transfers between devices with their start and end apart: 23, of which 14 were waited for; matrix products, arithmetic and copies ran while one was open for 0% of the time, Pallas kernels for 9%

profile of v2, /device:TPU:0, one launch (start us, length us, event | category | flops | bytes accessed | tf_op | source)
XLA Modules:
  0.0 82.5 jit_solution(6457996539625229626)
XLA Ops:
  0.7 4.7 %project.1 = (f32[4,8,3584]{2,1,0:T(8,128)S(1)}, f32[8,3584]{1,0:T(8,128)S(1)}) custom-call(bf16[128,1024]{1,0:T(8,128)(2,1)} %zc_ref.1, bf16[128,1024]{1,0:T(8,128)(2,1)} %zn_ref.1, bf16[1024,3584]{1,0:T(8,128)(2,1)} %w_ref.1), custom_call_target="tpu_custom_call" | custom-call | flops 117440512 | bytes 7864320 | tf_op jit(solution)/shard_map/project/pallas_call | solution.py:55
  5.4 3.4 %collective-permute-start.2 = (f32[8,3584]{1,0:T(8,128)S(1)}, f32[8,3584]{1,0:T(8,128)S(1)}, u32[]{:S(2)}, u32[]{:S(2)}) collective-permute-start(f32[8,3584]{1,0:T(8,128)S(1)} %get-tuple-element.42.a_ref), channel_id=1, source_target_pairs={{0,2},{1,3},{2,0},{3,1},{4,6},{5,7},{6,4},{7,5},{8,10},{9,11},{10,... | collective-permute-start | bytes 344072 | tf_op jit(solution)/shard_map/ppermute | solution.py:431
  10.8 1.2 %copy-done.1 = bf16[128,3584]{1,0:T(8,128)(2,1)S(1)} copy-done((bf16[128,3584]{1,0:T(8,128)(2,1)S(1)}, bf16[128,3584]{1,0:T(8,128)(2,1)}, u32[]{:S(2)}) %copy-start.1) | copy-done | bytes 917528
  12.0 1.2 %copy-done.3 = bf16[128,3584]{1,0:T(8,128)(2,1)S(1)} copy-done((bf16[128,3584]{1,0:T(8,128)(2,1)S(1)}, bf16[128,3584]{1,0:T(8,128)(2,1)}, u32[]{:S(2)}) %copy-start.3) | copy-done | bytes 917528
  13.1 2.1 %resid_project.1.resid_ref = f32[2,128,1024]{2,1,0:T(8,128)S(1)} custom-call(bf16[128,3584]{1,0:T(8,128)(2,1)S(1)} %copy-done.1, bf16[128,3584]{1,0:T(8,128)(2,1)S(1)} %copy-done.3, bf16[3584,1024]{1,0:T(8,128)(2,1)S(1)} %copy-done), custom_call_target="tpu_custom_call" | custom-call | flops 1879048192 | bytes 9175040 | tf_op jit(solution)/shard_map/resid_project/pallas_call | solution.py:55
  16.1 2.8 %collective-permute-start.5 = (f32[8,3712]{1,0:T(8,128)S(1)}, f32[8,3712]{1,0:T(8,128)S(1)}, u32[]{:S(2)}, u32[]{:S(2)}) collective-permute-start(f32[8,3712]{1,0:T(8,128)S(1)} %get-tuple-element.50.a_ref), channel_id=1, source_target_pairs={{0,96},{4,28},{8,104},{12,4},{16,112},{20,12},{24,120},{28,20},{32... | collective-permute-start | bytes 356360 | tf_op jit(solution)/shard_map/ppermute | solution.py:436
  20.7 4.1 %grad_f.1.gf_ref = f32[4,128,1024]{2,1,0:T(8,128)S(1)} custom-call(bf16[128,4,3584]{2,1,0:T(4,128)(2,1)S(1)} %copy-done.6, bf16[1024,3584]{1,0:T(8,128)(2,1)S(1)} %copy-done.5), custom_call_target="tpu_custom_call" | custom-call | flops 3758096384 | bytes 11010048 | tf_op jit(solution)/shard_map/grad_f/pallas_call | solution.py:55
  25.4 1.2 %collective-permute-done.3.b_ref = f32[8,3712]{1,0:T(8,128)S(1)} collective-permute-done((f32[8,3712]{1,0:T(8,128)S(1)}, f32[8,3712]{1,0:T(8,128)S(1)}, u32[]{:S(2)}, u32[]{:S(2)}) %collective-permute-start.3) | collective-permute-done | bytes 118816 | tf_op jit(solution)/shard_map/ppermute | solution.py:436
  26.6 4.1 %collective-permute-start.11 = (f32[4,8,3712]{2,1,0:T(8,128)S(1)}, f32[4,8,3712]{2,1,0:T(8,128)S(1)}, u32[]{:S(2)}, u32[]{:S(2)}) collective-permute-start(f32[4,8,3712]{2,1,0:T(8,128)S(1)} %line.1.a_ref), channel_id=1, source_target_pairs={{0,24},{4,100},{8,0},{12,108},{16,8},{20,116},{24,16},{28,124},{32... | collective-permute-start | bytes 1425416 | tf_op jit(solution)/shard_map/ppermute | solution.py:436
  30.7 1.3 %collective-permute-start.7 = (f32[4,8,3712]{2,1,0:T(8,128)S(1)}, f32[4,8,3712]{2,1,0:T(8,128)S(1)}, u32[]{:S(2)}, u32[]{:S(2)}) collective-permute-start(f32[4,8,3712]{2,1,0:T(8,128)S(1)} %line.1.a_ref), channel_id=1, source_target_pairs={{0,8},{4,36},{8,16},{12,44},{16,24},{20,52},{24,0},{28,60},{32,40}... | collective-permute-start | bytes 1425416 | tf_op jit(solution)/shard_map/ppermute | solution.py:436
  32.0 10.0 %collective-permute-done.11.d_ref = f32[4,8,3712]{2,1,0:T(8,128)S(1)} collective-permute-done((f32[4,8,3712]{2,1,0:T(8,128)S(1)}, f32[4,8,3712]{2,1,0:T(8,128)S(1)}, u32[]{:S(2)}, u32[]{:S(2)}) %collective-permute-start.11) | collective-permute-done | bytes 475168 | tf_op jit(solution)/shard_map/ppermute | solution.py:436
  42.5 3.2 %collective-permute-done.7.b_ref = f32[4,8,3712]{2,1,0:T(8,128)S(1)} collective-permute-done((f32[4,8,3712]{2,1,0:T(8,128)S(1)}, f32[4,8,3712]{2,1,0:T(8,128)S(1)}, u32[]{:S(2)}, u32[]{:S(2)}) %collective-permute-start.7) | collective-permute-done | bytes 475168 | tf_op jit(solution)/shard_map/ppermute | solution.py:436
  45.7 1.3 %own_project.1 = (f32[128,1024]{1,0:T(8,128)S(1)}, f32[16,8,128]{2,1,0:T(8,128)S(1)}) custom-call(f32[4,8,3712]{2,1,0:T(8,128)S(1)} %line.1.a_ref, f32[4,8,3712]{2,1,0:T(8,128)S(1)} %collective-permute-done.7.b_ref, f32[4,8,3712]{2,1,0:T(8,128)S(1)} %collective-permute-done.9.c_ref, f32[4,8,3712]{2,1,0:T(8,128)S(1)} %collective-permute-done.11.d_ref, ...), custom_call_target="tpu_custom_call" | custom-call | flops 939524096 | bytes 9240576 | tf_op jit(solution)/shard_map/own_project/pallas_call | solution.py:55
  47.5 4.4 %latents.1 = (f32[128,1024]{1,0:T(8,128)S(1)}, f32[64,3840]{1,0:T(8,128)S(1)}, f32[64,3840]{1,0:T(8,128)S(1)}) custom-call(f32[4,8,3712]{2,1,0:T(8,128)S(1)} %collective-permute-done.6.a_ref, f32[4,8,3712]{2,1,0:T(8,128)S(1)} %collective-permute-done.8.b_ref, f32[4,8,3712]{2,1,0:T(8,128)S(1)} %collective-permute-done.10.c_ref, ...), custom_call_target="tpu_custom_call" | custom-call | flops 1879048192 | bytes 13500416 | tf_op jit(solution)/shard_map/latents/pallas_call | solution.py:55
  52.2 2.4 %collective-permute-done.13.b_ref = f32[64,3840]{1,0:T(8,128)S(1)} collective-permute-done((f32[64,3840]{1,0:T(8,128)S(1)}, f32[64,3840]{1,0:T(8,128)S(1)}, u32[]{:S(2)}, u32[]{:S(2)}) %collective-permute-start.13) | collective-permute-done | bytes 983072 | tf_op jit(solution)/shard_map/ppermute | solution.py:440
  55.0 2.0 %collective-permute-start.15 = (f32[4,8,1920]{2,1,0:T(8,128)S(1)}, f32[4,8,1920]{2,1,0:T(8,128)S(1)}, u32[]{:S(2)}, u32[]{:S(2)}) collective-permute-start(f32[4,8,1920]{2,1,0:T(8,128)S(1)} %get-tuple-element.63), channel_id=1, source_target_pairs={{0,64},{4,20},{8,72},{12,28},{16,80},{20,4},{24,88},{28,12},{32,96... | collective-permute-start | bytes 737288 | tf_op jit(solution)/shard_map/ppermute | solution.py:436
  57.0 1.3 %collective-permute-start.16 = (f32[4,8,1920]{2,1,0:T(8,128)S(1)}, f32[4,8,1920]{2,1,0:T(8,128)S(1)}, u32[]{:S(2)}, u32[]{:S(2)}) collective-permute-start(f32[4,8,1920]{2,1,0:T(8,128)S(1)} %get-tuple-element.64), channel_id=1, source_target_pairs={{0,96},{4,28},{8,104},{12,4},{16,112},{20,12},{24,120},{28,20},{32... | collective-permute-start | bytes 737288 | tf_op jit(solution)/shard_map/ppermute | solution.py:436
  58.3 6.6 %collective-permute-done.14.b_ref = f32[4,8,1920]{2,1,0:T(8,128)S(1)} collective-permute-done((f32[4,8,1920]{2,1,0:T(8,128)S(1)}, f32[4,8,1920]{2,1,0:T(8,128)S(1)}, u32[]{:S(2)}, u32[]{:S(2)}) %collective-permute-start.14) | collective-permute-done | bytes 245792 | tf_op jit(solution)/shard_map/ppermute | solution.py:436
  66.0 2.9 %collective-permute-start.18 = (f32[8,1920]{1,0:T(8,128)S(1)}, f32[8,1920]{1,0:T(8,128)S(1)}, u32[]{:S(2)}, u32[]{:S(2)}) collective-permute-start(f32[8,1920]{1,0:T(8,128)S(1)} %get-tuple-element.67), channel_id=1, source_target_pairs={{0,16},{4,68},{8,24},{12,76},{16,0},{20,84},{24,8},{28,92},{32,48}... | collective-permute-start | bytes 184328 | tf_op jit(solution)/shard_map/ppermute | solution.py:436
  69.2 2.9 %collective-permute-done.17.b_ref = f32[8,1920]{1,0:T(8,128)S(1)} collective-permute-done((f32[8,1920]{1,0:T(8,128)S(1)}, f32[8,1920]{1,0:T(8,128)S(1)}, u32[]{:S(2)}, u32[]{:S(2)}) %collective-permute-start.17) | collective-permute-done | bytes 61472 | tf_op jit(solution)/shard_map/ppermute | solution.py:436
  73.1 1.8 %collective-permute-start.22 = (f32[8,1920]{1,0:T(8,128)S(1)}, f32[8,1920]{1,0:T(8,128)S(1)}, u32[]{:S(2)}, u32[]{:S(2)}) collective-permute-start(f32[8,1920]{1,0:T(8,128)S(1)} %plane_sum.1.a_ref), channel_id=1, source_target_pairs={{0,2},{1,3},{2,0},{3,1},{4,6},{5,7},{6,4},{7,5},{8,10},{9,11},{10,... | collective-permute-start | bytes 184328 | tf_op jit(solution)/shard_map/ppermute | solution.py:431
  74.9 1.2 %collective-permute-start.21 = (f32[8,1920]{1,0:T(8,128)S(1)}, f32[8,1920]{1,0:T(8,128)S(1)}, u32[]{:S(2)}, u32[]{:S(2)}) collective-permute-start(f32[8,1920]{1,0:T(8,128)S(1)} %plane_sum.1.a_ref), channel_id=1, source_target_pairs={{0,3},{1,0},{2,1},{3,2},{4,7},{5,4},{6,5},{7,6},{8,11},{9,8},{10,9... | collective-permute-start | bytes 184328 | tf_op jit(solution)/shard_map/ppermute | solution.py:431
  76.9 1.9 %collective-permute-done.22.d_ref = f32[8,1920]{1,0:T(8,128)S(1)} collective-permute-done((f32[8,1920]{1,0:T(8,128)S(1)}, f32[8,1920]{1,0:T(8,128)S(1)}, u32[]{:S(2)}, u32[]{:S(2)}) %collective-permute-start.22) | collective-permute-done | bytes 61472 | tf_op jit(solution)/shard_map/ppermute | solution.py:431
  79.1 2.4 %collective-permute-done.20.b_ref = f32[8,1920]{1,0:T(8,128)S(1)} collective-permute-done((f32[8,1920]{1,0:T(8,128)S(1)}, f32[8,1920]{1,0:T(8,128)S(1)}, u32[]{:S(2)}, u32[]{:S(2)}) %collective-permute-start.20) | collective-permute-done | bytes 61472 | tf_op jit(solution)/shard_map/ppermute | solution.py:431
  (50 shorter events, 11.5 us)
Async XLA Ops:
  5.4 9.9 %collective-permute-start.2 = (f32[8,3584]{1,0:T(8,128)S(1)}, f32[8,3584]{1,0:T(8,128)S(1)}, u32[]{:S(2)}, u32[]{:S(2)}) collective-permute-start(f32[8,3584]{1,0:T(8,128)S(1)} %get-tuple-element.42.a_ref), channel_id=1, source_target_pairs={{0,2},{1,3},{2,0},{3,1},{4,6},{5,7},{6,4},{7,5},{8,10},{9,11},{10,... | collective-permute-start | bytes 344072 | tf_op jit(solution)/shard_map/ppermute | solution.py:431
  8.7 6.5 %collective-permute-start.1 = (f32[8,3584]{1,0:T(8,128)S(1)}, f32[8,3584]{1,0:T(8,128)S(1)}, u32[]{:S(2)}, u32[]{:S(2)}) collective-permute-start(f32[8,3584]{1,0:T(8,128)S(1)} %get-tuple-element.42.a_ref), channel_id=1, source_target_pairs={{0,3},{1,0},{2,1},{3,2},{4,7},{5,4},{6,5},{7,6},{8,11},{9,8},{10,9... | collective-permute-start | bytes 344072 | tf_op jit(solution)/shard_map/ppermute | solution.py:431
  9.8 6.0 %collective-permute-start = (f32[8,3584]{1,0:T(8,128)S(1)}, f32[8,3584]{1,0:T(8,128)S(1)}, u32[]{:S(2)}, u32[]{:S(2)}) collective-permute-start(f32[8,3584]{1,0:T(8,128)S(1)} %get-tuple-element.42.a_ref), channel_id=1, source_target_pairs={{0,1},{1,2},{2,3},{3,0},{4,5},{5,6},{6,7},{7,4},{8,9},{9,10},{10,1... | collective-permute-start | bytes 344072 | tf_op jit(solution)/shard_map/ppermute | solution.py:431
  16.1 8.7 %collective-permute-start.5 = (f32[8,3712]{1,0:T(8,128)S(1)}, f32[8,3712]{1,0:T(8,128)S(1)}, u32[]{:S(2)}, u32[]{:S(2)}) collective-permute-start(f32[8,3712]{1,0:T(8,128)S(1)} %get-tuple-element.50.a_ref), channel_id=1, source_target_pairs={{0,96},{4,28},{8,104},{12,4},{16,112},{20,12},{24,120},{28,20},{32... | collective-permute-start | bytes 356360 | tf_op jit(solution)/shard_map/ppermute | solution.py:436
  19.0 6.4 %collective-permute-start.4 = (f32[8,3712]{1,0:T(8,128)S(1)}, f32[8,3712]{1,0:T(8,128)S(1)}, u32[]{:S(2)}, u32[]{:S(2)}) collective-permute-start(f32[8,3712]{1,0:T(8,128)S(1)} %get-tuple-element.50.a_ref), channel_id=1, source_target_pairs={{0,64},{4,20},{8,72},{12,28},{16,80},{20,4},{24,88},{28,12},{32,96... | collective-permute-start | bytes 356360 | tf_op jit(solution)/shard_map/ppermute | solution.py:436
  19.8 6.8 %collective-permute-start.3 = (f32[8,3712]{1,0:T(8,128)S(1)}, f32[8,3712]{1,0:T(8,128)S(1)}, u32[]{:S(2)}, u32[]{:S(2)}) collective-permute-start(f32[8,3712]{1,0:T(8,128)S(1)} %get-tuple-element.50.a_ref), channel_id=1, source_target_pairs={{0,32},{4,12},{8,40},{12,20},{16,48},{20,28},{24,56},{28,4},{32,64... | collective-permute-start | bytes 356360 | tf_op jit(solution)/shard_map/ppermute | solution.py:436
  24.8 22.7 %copy-start.4 = (s32[128,1024]{1,0:T(8,128)S(1)}, s32[128,1024]{1,0:T(8,128)}, u32[]{:S(2)}) copy-start(s32[128,1024]{1,0:T(8,128)} %active_ref) | copy-start | bytes 1572868
  26.6 15.4 %collective-permute-start.11 = (f32[4,8,3712]{2,1,0:T(8,128)S(1)}, f32[4,8,3712]{2,1,0:T(8,128)S(1)}, u32[]{:S(2)}, u32[]{:S(2)}) collective-permute-start(f32[4,8,3712]{2,1,0:T(8,128)S(1)} %line.1.a_ref), channel_id=1, source_target_pairs={{0,24},{4,100},{8,0},{12,108},{16,8},{20,116},{24,16},{28,124},{32... | collective-permute-start | bytes 1425416 | tf_op jit(solution)/shard_map/ppermute | solution.py:436
  30.7 11.3 %collective-permute-start.9 = (f32[4,8,3712]{2,1,0:T(8,128)S(1)}, f32[4,8,3712]{2,1,0:T(8,128)S(1)}, u32[]{:S(2)}, u32[]{:S(2)}) collective-permute-start(f32[4,8,3712]{2,1,0:T(8,128)S(1)} %line.1.a_ref), channel_id=1, source_target_pairs={{0,16},{4,68},{8,24},{12,76},{16,0},{20,84},{24,8},{28,92},{32,48}... | collective-permute-start | bytes 1425416 | tf_op jit(solution)/shard_map/ppermute | solution.py:436
  30.7 15.0 %collective-permute-start.7 = (f32[4,8,3712]{2,1,0:T(8,128)S(1)}, f32[4,8,3712]{2,1,0:T(8,128)S(1)}, u32[]{:S(2)}, u32[]{:S(2)}) collective-permute-start(f32[4,8,3712]{2,1,0:T(8,128)S(1)} %line.1.a_ref), channel_id=1, source_target_pairs={{0,8},{4,36},{8,16},{12,44},{16,24},{20,52},{24,0},{28,60},{32,40}... | collective-permute-start | bytes 1425416 | tf_op jit(solution)/shard_map/ppermute | solution.py:436
  32.0 15.0 %collective-permute-start.6 = (f32[4,8,3712]{2,1,0:T(8,128)S(1)}, f32[4,8,3712]{2,1,0:T(8,128)S(1)}, u32[]{:S(2)}, u32[]{:S(2)}) collective-permute-start(f32[4,8,3712]{2,1,0:T(8,128)S(1)} %line.1.a_ref), channel_id=1, source_target_pairs={{0,4},{4,0},{8,12},{12,8},{16,20},{20,16},{24,28},{28,24},{32,36},... | collective-permute-start | bytes 1425416 | tf_op jit(solution)/shard_map/ppermute | solution.py:440
  42.0 5.0 %collective-permute-start.12 = (f32[4,8,3712]{2,1,0:T(8,128)S(1)}, f32[4,8,3712]{2,1,0:T(8,128)S(1)}, u32[]{:S(2)}, u32[]{:S(2)}) collective-permute-start(f32[4,8,3712]{2,1,0:T(8,128)S(1)} %collective-permute-done.11.d_ref), channel_id=1, source_target_pairs={{0,4},{4,0},{8,12},{12,8},{16,20},{20,16},{24,28},{28,24},{32,36},... | collective-permute-start | bytes 1425416 | tf_op jit(solution)/shard_map/ppermute | solution.py:440
  42.0 5.0 %collective-permute-start.10 = (f32[4,8,3712]{2,1,0:T(8,128)S(1)}, f32[4,8,3712]{2,1,0:T(8,128)S(1)}, u32[]{:S(2)}, u32[]{:S(2)}) collective-permute-start(f32[4,8,3712]{2,1,0:T(8,128)S(1)} %collective-permute-done.9.c_ref), channel_id=1, source_target_pairs={{0,4},{4,0},{8,12},{12,8},{16,20},{20,16},{24,28},{28,24},{32,36},... | collective-permute-start | bytes 1425416 | tf_op jit(solution)/shard_map/ppermute | solution.py:440
  45.7 1.8 %collective-permute-start.8 = (f32[4,8,3712]{2,1,0:T(8,128)S(1)}, f32[4,8,3712]{2,1,0:T(8,128)S(1)}, u32[]{:S(2)}, u32[]{:S(2)}) collective-permute-start(f32[4,8,3712]{2,1,0:T(8,128)S(1)} %collective-permute-done.7.b_ref), channel_id=1, source_target_pairs={{0,4},{4,0},{8,12},{12,8},{16,20},{20,16},{24,28},{28,24},{32,36},... | collective-permute-start | bytes 1425416 | tf_op jit(solution)/shard_map/ppermute | solution.py:440
  52.0 2.6 %collective-permute-start.13 = (f32[64,3840]{1,0:T(8,128)S(1)}, f32[64,3840]{1,0:T(8,128)S(1)}, u32[]{:S(2)}, u32[]{:S(2)}) collective-permute-start(f32[64,3840]{1,0:T(8,128)S(1)} %get-tuple-element.60), channel_id=1, source_target_pairs={{0,4},{4,0},{8,12},{12,8},{16,20},{20,16},{24,28},{28,24},{32,36},... | collective-permute-start | bytes 2949128 | tf_op jit(solution)/shard_map/ppermute | solution.py:440
  54.8 10.1 %collective-permute-start.14 = (f32[4,8,1920]{2,1,0:T(8,128)S(1)}, f32[4,8,1920]{2,1,0:T(8,128)S(1)}, u32[]{:S(2)}, u32[]{:S(2)}) collective-permute-start(f32[4,8,1920]{2,1,0:T(8,128)S(1)} %get-tuple-element.62), channel_id=1, source_target_pairs={{0,32},{4,12},{8,40},{12,20},{16,48},{20,28},{24,56},{28,4},{32,64... | collective-permute-start | bytes 737288 | tf_op jit(solution)/shard_map/ppermute | solution.py:436
  55.0 9.9 %collective-permute-start.15 = (f32[4,8,1920]{2,1,0:T(8,128)S(1)}, f32[4,8,1920]{2,1,0:T(8,128)S(1)}, u32[]{:S(2)}, u32[]{:S(2)}) collective-permute-start(f32[4,8,1920]{2,1,0:T(8,128)S(1)} %get-tuple-element.63), channel_id=1, source_target_pairs={{0,64},{4,20},{8,72},{12,28},{16,80},{20,4},{24,88},{28,12},{32,96... | collective-permute-start | bytes 737288 | tf_op jit(solution)/shard_map/ppermute | solution.py:436
  57.0 8.8 %collective-permute-start.16 = (f32[4,8,1920]{2,1,0:T(8,128)S(1)}, f32[4,8,1920]{2,1,0:T(8,128)S(1)}, u32[]{:S(2)}, u32[]{:S(2)}) collective-permute-start(f32[4,8,1920]{2,1,0:T(8,128)S(1)} %get-tuple-element.64), channel_id=1, source_target_pairs={{0,96},{4,28},{8,104},{12,4},{16,112},{20,12},{24,120},{28,20},{32... | collective-permute-start | bytes 737288 | tf_op jit(solution)/shard_map/ppermute | solution.py:436
  65.9 6.2 %collective-permute-start.17 = (f32[8,1920]{1,0:T(8,128)S(1)}, f32[8,1920]{1,0:T(8,128)S(1)}, u32[]{:S(2)}, u32[]{:S(2)}) collective-permute-start(f32[8,1920]{1,0:T(8,128)S(1)} %get-tuple-element.66), channel_id=1, source_target_pairs={{0,8},{4,36},{8,16},{12,44},{16,24},{20,52},{24,0},{28,60},{32,40}... | collective-permute-start | bytes 184328 | tf_op jit(solution)/shard_map/ppermute | solution.py:436
  66.0 6.1 %collective-permute-start.18 = (f32[8,1920]{1,0:T(8,128)S(1)}, f32[8,1920]{1,0:T(8,128)S(1)}, u32[]{:S(2)}, u32[]{:S(2)}) collective-permute-start(f32[8,1920]{1,0:T(8,128)S(1)} %get-tuple-element.67), channel_id=1, source_target_pairs={{0,16},{4,68},{8,24},{12,76},{16,0},{20,84},{24,8},{28,92},{32,48}... | collective-permute-start | bytes 184328 | tf_op jit(solution)/shard_map/ppermute | solution.py:436
  68.8 4.2 %collective-permute-start.19 = (f32[8,1920]{1,0:T(8,128)S(1)}, f32[8,1920]{1,0:T(8,128)S(1)}, u32[]{:S(2)}, u32[]{:S(2)}) collective-permute-start(f32[8,1920]{1,0:T(8,128)S(1)} %get-tuple-element.68), channel_id=1, source_target_pairs={{0,24},{4,100},{8,0},{12,108},{16,8},{20,116},{24,16},{28,124},{32... | collective-permute-start | bytes 184328 | tf_op jit(solution)/shard_map/ppermute | solution.py:436
  73.1 5.8 %collective-permute-start.22 = (f32[8,1920]{1,0:T(8,128)S(1)}, f32[8,1920]{1,0:T(8,128)S(1)}, u32[]{:S(2)}, u32[]{:S(2)}) collective-permute-start(f32[8,1920]{1,0:T(8,128)S(1)} %plane_sum.1.a_ref), channel_id=1, source_target_pairs={{0,2},{1,3},{2,0},{3,1},{4,6},{5,7},{6,4},{7,5},{8,10},{9,11},{10,... | collective-permute-start | bytes 184328 | tf_op jit(solution)/shard_map/ppermute | solution.py:431
  74.9 4.2 %collective-permute-start.21 = (f32[8,1920]{1,0:T(8,128)S(1)}, f32[8,1920]{1,0:T(8,128)S(1)}, u32[]{:S(2)}, u32[]{:S(2)}) collective-permute-start(f32[8,1920]{1,0:T(8,128)S(1)} %plane_sum.1.a_ref), channel_id=1, source_target_pairs={{0,3},{1,0},{2,1},{3,2},{4,7},{5,4},{6,5},{7,6},{8,11},{9,8},{10,9... | collective-permute-start | bytes 184328 | tf_op jit(solution)/shard_map/ppermute | solution.py:431
  76.1 5.4 %collective-permute-start.20 = (f32[8,1920]{1,0:T(8,128)S(1)}, f32[8,1920]{1,0:T(8,128)S(1)}, u32[]{:S(2)}, u32[]{:S(2)}) collective-permute-start(f32[8,1920]{1,0:T(8,128)S(1)} %plane_sum.1.a_ref), channel_id=1, source_target_pairs={{0,1},{1,2},{2,3},{3,0},{4,5},{5,6},{6,7},{7,4},{8,9},{9,10},{10,1... | collective-permute-start | bytes 184328 | tf_op jit(solution)/shard_map/ppermute | solution.py:431
  (7 other events, 40.3 us)

commit v3 on v2

--- a/solution.py
+++ b/solution.py
@@ -123,7 +123,7 @@
     )
 
 
-def grad_f_kernel(cot_ref, w_ref, out_ref, rows, acc):
+def grad_f_kernel(cot_ref, w_ref, active_ref, out_ref, rows, acc):
     rows[...] = cot_ref[...].reshape(TOKENS * STEPS, D)
     for n in range(w_ref.shape[0] // acc.shape[0] // SIDE):
         base = n * acc.shape[0] * SIDE
@@ -131,15 +131,16 @@
         for j in range(acc.shape[0]):
             acc[j] = out[:, j * SIDE : (j + 1) * SIDE]
             cols = slice(base + j * SIDE, base + (j + 1) * SIDE)
+            act = active_ref[:, cols].astype(F32)
             for k in range(STEPS):
-                out_ref[k, :, cols] = acc[j, pl.ds(k, TOKENS, stride=STEPS), :]
-
-
-def grad_f(cot, w_dec):
+                out_ref[k, :, cols] = act * acc[j, pl.ds(k, TOKENS, stride=STEPS), :]
+
+
+def grad_f(cot, w_dec, active):
     return call(
         grad_f_kernel,
         "grad_f",
-        (cot, w_dec),
+        (cot, w_dec, active),
         [((STEPS, TOKENS, LAT_LOCAL), F32)],
         [VMEM((TOKENS * STEPS, D), BF16), VMEM((2, TOKENS * STEPS, SIDE), F32)],
         mib=8,
@@ -203,6 +204,14 @@
             out[from_x * 4 + from_z] = ref[d]
 
 
+def flip_kernel(w_ref, out_ref):
+    out_ref[...] = w_ref[...].T
+
+
+def flip(w_enc):
+    return call(flip_kernel, "flip", (w_enc,), [((LAT_LOCAL, D), BF16)])[0]
+
+
 def resid_kernel(rc_ref, rn_ref, w_ref, out_ref):
     out_ref[0] = nn(rc_ref[...], w_ref[...])
     out_ref[1] = nn(rn_ref[...], w_ref[...])
@@ -271,7 +280,7 @@
 
 
 def latents_kernel(
-    a_ref, b_ref, c_ref, d_ref, side_ref, pre_ref, resid_ref, gf_ref, active_ref, w_ref,
+    a_ref, b_ref, c_ref, d_ref, side_ref, pre_ref, resid_ref, gf_ref, w_ref, flip_ref,
     raw_ref, keep_ref, send_ref,
     other, pre_s, hidden_s, inv_s,
 ):
@@ -282,8 +291,10 @@
         side_ref[...].reshape(TOKENS, SIDE), other[:, :, D:].reshape(TOKENS, SIDE), core
     )[0]
     for k in range(STEPS):
-        inv_s[k] = jnp.broadcast_to(side[:, k : k + 1], (TOKENS, SIDE))
-    for k, j in ((0, STEPS), (STEPS - 1, STEPS + 1)):
+        inv = jnp.broadcast_to(side[:, k : k + 1], (TOKENS, SIDE))
+        inv_s[k] = inv
+        inv_s[STEPS + k] = inv * inv * inv
+    for k, j in ((0, 2 * STEPS), (STEPS - 1, 2 * STEPS + 1)):
         inv_s[j] = 1.0 / inv_s[k]
     tot = jnp.zeros((TOKENS, SIDE), F32)
     s_0 = jnp.zeros((TOKENS, SIDE), F32)
@@ -292,25 +303,23 @@
     for start in range(0, LAT_LOCAL, SIDE):
         cols = slice(start, start + SIDE)
         pre_0, pre_3 = by_step(pre_ref[:, cols], pre_s[:, cols], core)
-        act = active_ref[:, cols].astype(F32)
         gf = [gf_ref[k, :, cols] for k in range(STEPS)]
-        raw = act * (pre_3 - pre_0) * (((gf[0] + gf[1]) + (gf[2] + gf[3])) * 0.25)
+        raw = (pre_3 - pre_0) * (((gf[0] + gf[1]) + (gf[2] + gf[3])) * 0.25)
         raw_ref[:, cols] = raw
         tot = tot + jnp.abs(raw)
-        q_0 = act * (pre_0 - resid_ref[0, :, cols]) * inv_s[STEPS]
-        q_d = act * (pre_3 - resid_ref[1, :, cols]) * inv_s[STEPS + 1] - q_0
-        hidden = jnp.zeros((TOKENS, SIDE), F32)
-        for k in range(STEPS):
-            inv = inv_s[k]
-            scaled = inv * gf[k]
-            hidden = hidden + scaled
-            term = inv * inv * scaled * (q_0 + ALPHAS[k] * q_d)
-            s_0 = s_0 + term
-            s_1 = s_1 + ALPHAS[k] * term
-        first, second = by_core(act * hidden, core)
+        q_0 = (pre_0 - resid_ref[0, :, cols]) * inv_s[2 * STEPS]
+        q_d = (pre_3 - resid_ref[1, :, cols]) * inv_s[2 * STEPS + 1] - q_0
+        u = [inv_s[STEPS + k] * gf[k] for k in range(STEPS)]
+        sum_0 = (u[0] + u[1]) + (u[2] + u[3])
+        sum_1 = ALPHAS[1] * u[1] + (ALPHAS[2] * u[2] + u[3])
+        sum_2 = ALPHAS[1] ** 2 * u[1] + (ALPHAS[2] ** 2 * u[2] + u[3])
+        s_0 = s_0 + (sum_0 * q_0 + sum_1 * q_d)
+        s_1 = s_1 + (sum_1 * q_0 + sum_2 * q_d)
+        hidden = (inv_s[0] * gf[0] + inv_s[1] * gf[1]) + (inv_s[2] * gf[2] + inv_s[3] * gf[3])
+        first, second = by_core(hidden, core)
         hidden_s[:half, cols] = first.astype(BF16)
         hidden_s[half:, cols] = second.astype(BF16)
-    grad = nt(hidden_s[...], w_ref[...])
+    grad = nn(hidden_s[...], flip_ref[...])
     keep_ref[:, :D] = grad[:half]
     send_ref[:, :D] = grad[half:]
     row = lax.broadcasted_iota(jnp.int32, (TOKENS, SIDE), 0)
@@ -327,18 +336,18 @@
     send_ref[:, D + SIDE :] = second
 
 
-def latents(others, side, pre_own, resid, gf, active, w_enc):
+def latents(others, side, pre_own, resid, gf, w_enc, flipped):
     half = TOKENS // 2
     return call(
         latents_kernel,
         "latents",
-        (*others, side, pre_own, resid, gf, active, w_enc),
+        (*others, side, pre_own, resid, gf, w_enc, flipped),
         [((TOKENS, LAT_LOCAL), F32), ((half, RED), F32), ((half, RED), F32)],
         [
             VMEM((PLANE, 2 * OWN, MSG), F32),
             VMEM((TOKENS, LAT_LOCAL), F32),
             VMEM((TOKENS, LAT_LOCAL), BF16),
-            VMEM((STEPS + 2, TOKENS, SIDE), F32),
+            VMEM((2 * STEPS + 2, TOKENS, SIDE), F32),
         ],
         flops=4 * 128 * 1024 * D,
     )
@@ -451,13 +460,15 @@
     resid = resid_project(resid_corrupt, resid_clean, w_enc)
     *parts, resid = lax.optimization_barrier((*over_tp(part), resid))
     attn, msg = norm(parts, resid_corrupt, resid_clean, gain)
-    gf = grad_f(cot, w_dec)
+    gf = grad_f(cot, w_dec, active)
     *parts, gf = lax.optimization_barrier((msg, *[send(msg, 0, d) for d in (1, 2, 3)], gf))
     block = line(parts)
+    flipped = flip(w_enc)
     blocks = [block] + [send(block, 1, e) for e in (1, 2, 3)]
+    blocks[2], flipped = lax.optimization_barrier((blocks[2], flipped))
     others = [swap(b) for b in blocks]
     pre_own, side = own_project(blocks, w_enc)
-    raw, keep, give = latents(others, side, pre_own, resid, gf, active, w_enc)
+    raw, keep, give = latents(others, side, pre_own, resid, gf, w_enc, flipped)
     parts = pair_sum(keep, swap(give))
     parts = line_sum([parts[0]] + [send(parts[d], 0, d) for d in (1, 2, 3)])
     total = plane_sum([parts[0]] + [send(parts[e], 1, e) for e in (1, 2, 3)])

time: 82.7 us -> 81.5 us (0.985)
  waiting for transfers between devices: 34.3 us -> 31.7 us
  starting transfers between devices: 26.7 us -> 27.7 us
    ppermute x12, waiting for transfers between devices: 26.3 us -> 22.8 us  [send(): return lax.ppermute(x, 'lat', shift(stage, d))]
    ppermute x12, starting transfers between devices: 16.7 us -> 18.1 us  [send(): return lax.ppermute(x, 'lat', shift(stage, d))]
    ppermute x5, waiting for transfers between devices: 2.94 us -> 3.83 us  [swap(): return lax.ppermute(x, 'lat', CORE_SWAP)]
    pallas_call x11 -> x12, Pallas kernels: 18.3 us -> 18.7 us  [call(): pl.pallas_call(kernel, in_specs=[pl.BlockSpec(memory_space=s) for s in sp...]
  transfers between devices with their start and end apart: 23 -> 23, of which waited for: 14 -> 15; matrix products, arithmetic and copies ran while one was open for 0% -> 0% of each run, Pallas kernels for 9% -> 12%
where the time goes in v3:
time: 81.5 us; the launch traced here: 81.3 us
  waiting for transfers between devices  31.7 us (39%)
  starting transfers between devices  27.7 us (34%)
  Pallas kernels  18.7 us (23%)
  local copies, waits for them, and re-layouts  2.39 us (3%)
  between operations  0.82 us (1%)
    ppermute x12, waiting for transfers between devices, send(): return lax.ppermute(x, 'lat', shift(stage, d))  22.8 us
    pallas_call x12, Pallas kernels, call(): pl.pallas_call(kernel, in_specs=[pl.BlockSpec(memory_space=s) for s in sp...  18.7 us
    ppermute x12, starting transfers between devices, send(): return lax.ppermute(x, 'lat', shift(stage, d))  18.1 us
    ppermute x6, starting transfers between devices, over_tp(): lax.ppermute(x, 'tp', [(i, (i + d) % 4) for i in range(4)])  8.75 us
    ppermute x6, waiting for transfers between devices, over_tp(): lax.ppermute(x, 'tp', [(i, (i + d) % 4) for i in range(4)])  5.12 us
    ppermute x5, waiting for transfers between devices, swap(): return lax.ppermute(x, 'lat', CORE_SWAP)  3.83 us
    unnamed x16, local copies, waits for them, and re-layouts  2.38 us
  transfers between devices with their start and end apart: 23, of which 15 were waited for; matrix products, arithmetic and copies ran while one was open for 0% of the time, Pallas kernels for 12%

profile of v3, /device:TPU:0, one launch (start us, length us, event | category | flops | bytes accessed | tf_op | source)
XLA Modules:
  0.0 81.3 jit_solution(1285201231933514630)
XLA Ops:
  0.7 4.7 %project.1 = (f32[4,8,3584]{2,1,0:T(8,128)S(1)}, f32[8,3584]{1,0:T(8,128)S(1)}) custom-call(bf16[128,1024]{1,0:T(8,128)(2,1)} %zc_ref.1, bf16[128,1024]{1,0:T(8,128)(2,1)} %zn_ref.1, bf16[1024,3584]{1,0:T(8,128)(2,1)} %w_ref.1), custom_call_target="tpu_custom_call" | custom-call | flops 117440512 | bytes 7864320 | tf_op jit(solution)/shard_map/project/pallas_call | solution.py:55
  5.4 3.4 %collective-permute-start.2 = (f32[8,3584]{1,0:T(8,128)S(1)}, f32[8,3584]{1,0:T(8,128)S(1)}, u32[]{:S(2)}, u32[]{:S(2)}) collective-permute-start(f32[8,3584]{1,0:T(8,128)S(1)} %get-tuple-element.44.a_ref), channel_id=1, source_target_pairs={{0,2},{1,3},{2,0},{3,1},{4,6},{5,7},{6,4},{7,5},{8,10},{9,11},{10,... | collective-permute-start | bytes 344072 | tf_op jit(solution)/shard_map/ppermute | solution.py:440
  13.2 2.1 %resid_project.1.resid_ref = f32[2,128,1024]{2,1,0:T(8,128)S(1)} custom-call(bf16[128,3584]{1,0:T(8,128)(2,1)S(1)} %copy-done.1, bf16[128,3584]{1,0:T(8,128)(2,1)S(1)} %copy-done.3, bf16[3584,1024]{1,0:T(8,128)(2,1)S(1)} %copy-done), custom_call_target="tpu_custom_call" | custom-call | flops 1879048192 | bytes 9175040 | tf_op jit(solution)/shard_map/resid_project/pallas_call | solution.py:55
  16.2 2.8 %collective-permute-start.5 = (f32[8,3712]{1,0:T(8,128)S(1)}, f32[8,3712]{1,0:T(8,128)S(1)}, u32[]{:S(2)}, u32[]{:S(2)}) collective-permute-start(f32[8,3712]{1,0:T(8,128)S(1)} %get-tuple-element.53.a_ref), channel_id=1, source_target_pairs={{0,96},{4,28},{8,104},{12,4},{16,112},{20,12},{24,120},{28,20},{32... | collective-permute-start | bytes 356360 | tf_op jit(solution)/shard_map/ppermute | solution.py:445
  20.7 4.1 %grad_f.1.gf_ref = f32[4,128,1024]{2,1,0:T(8,128)S(1)} custom-call(bf16[128,4,3584]{2,1,0:T(4,128)(2,1)S(1)} %copy-done.5, bf16[1024,3584]{1,0:T(8,128)(2,1)S(1)} %copy-done.4, s32[128,1024]{1,0:T(8,128)S(1)} %copy-done.6), custom_call_target="tpu_custom_call" | custom-call | flops 3758096384 | bytes 11534336 | tf_op jit(solution)/shard_map/grad_f/pallas_call | solution.py:55
  25.4 1.2 %collective-permute-done.3.b_ref = f32[8,3712]{1,0:T(8,128)S(1)} collective-permute-done((f32[8,3712]{1,0:T(8,128)S(1)}, f32[8,3712]{1,0:T(8,128)S(1)}, u32[]{:S(2)}, u32[]{:S(2)}) %collective-permute-start.3) | collective-permute-done | bytes 118816 | tf_op jit(solution)/shard_map/ppermute | solution.py:445
  26.6 4.2 %collective-permute-start.9 = (f32[4,8,3712]{2,1,0:T(8,128)S(1)}, f32[4,8,3712]{2,1,0:T(8,128)S(1)}, u32[]{:S(2)}, u32[]{:S(2)}) collective-permute-start(f32[4,8,3712]{2,1,0:T(8,128)S(1)} %line.1.a_ref), channel_id=1, source_target_pairs={{0,16},{4,68},{8,24},{12,76},{16,0},{20,84},{24,8},{28,92},{32,48}... | collective-permute-start | bytes 1425416 | tf_op jit(solution)/shard_map/ppermute | solution.py:445
  31.6 1.3 %collective-permute-start.7 = (f32[4,8,3712]{2,1,0:T(8,128)S(1)}, f32[4,8,3712]{2,1,0:T(8,128)S(1)}, u32[]{:S(2)}, u32[]{:S(2)}) collective-permute-start(f32[4,8,3712]{2,1,0:T(8,128)S(1)} %line.1.a_ref), channel_id=1, source_target_pairs={{0,8},{4,36},{8,16},{12,44},{16,24},{20,52},{24,0},{28,60},{32,40}... | collective-permute-start | bytes 1425416 | tf_op jit(solution)/shard_map/ppermute | solution.py:445
  32.9 1.9 %flip.1.flip_ref = bf16[1024,3584]{1,0:T(8,128)(2,1)S(1)} custom-call(bf16[3584,1024]{1,0:T(8,128)(2,1)S(1)} %copy-done), custom_call_target="tpu_custom_call" | custom-call | flops 1000000 | bytes 7340032 | tf_op jit(solution)/shard_map/flip/pallas_call | solution.py:55
  34.9 2.7 %collective-permute-done.9.c_ref = f32[4,8,3712]{2,1,0:T(8,128)S(1)} collective-permute-done((f32[4,8,3712]{2,1,0:T(8,128)S(1)}, f32[4,8,3712]{2,1,0:T(8,128)S(1)}, u32[]{:S(2)}, u32[]{:S(2)}) %collective-permute-start.9) | collective-permute-done | bytes 475168 | tf_op jit(solution)/shard_map/ppermute | solution.py:445
  37.6 6.5 %collective-permute-done.11.d_ref = f32[4,8,3712]{2,1,0:T(8,128)S(1)} collective-permute-done((f32[4,8,3712]{2,1,0:T(8,128)S(1)}, f32[4,8,3712]{2,1,0:T(8,128)S(1)}, u32[]{:S(2)}, u32[]{:S(2)}) %collective-permute-start.11) | collective-permute-done | bytes 475168 | tf_op jit(solution)/shard_map/ppermute | solution.py:445
  44.6 1.3 %own_project.1 = (f32[128,1024]{1,0:T(8,128)S(1)}, f32[16,8,128]{2,1,0:T(8,128)S(1)}) custom-call(f32[4,8,3712]{2,1,0:T(8,128)S(1)} %line.1.a_ref, f32[4,8,3712]{2,1,0:T(8,128)S(1)} %collective-permute-done.7.b_ref, f32[4,8,3712]{2,1,0:T(8,128)S(1)} %collective-permute-done.9.c_ref, f32[4,8,3712]{2,1,0:T(8,128)S(1)} %collective-permute-done.11.d_ref, ...), custom_call_target="tpu_custom_call" | custom-call | flops 939524096 | bytes 9240576 | tf_op jit(solution)/shard_map/own_project/pallas_call | solution.py:55
  47.3 2.9 %latents.1 = (f32[128,1024]{1,0:T(8,128)S(1)}, f32[64,3840]{1,0:T(8,128)S(1)}, f32[64,3840]{1,0:T(8,128)S(1)}) custom-call(f32[4,8,3712]{2,1,0:T(8,128)S(1)} %collective-permute-done.6.a_ref, f32[4,8,3712]{2,1,0:T(8,128)S(1)} %collective-permute-done.8.b_ref, f32[4,8,3712]{2,1,0:T(8,128)S(1)} %collective-permute-done.10.c_ref, ...), custom_call_target="tpu_custom_call" | custom-call | flops 1879048192 | bytes 20316160 | tf_op jit(solution)/shard_map/latents/pallas_call | solution.py:55
  50.4 2.4 %collective-permute-done.13.b_ref = f32[64,3840]{1,0:T(8,128)S(1)} collective-permute-done((f32[64,3840]{1,0:T(8,128)S(1)}, f32[64,3840]{1,0:T(8,128)S(1)}, u32[]{:S(2)}, u32[]{:S(2)}) %collective-permute-start.13) | collective-permute-done | bytes 983072 | tf_op jit(solution)/shard_map/ppermute | solution.py:449
  53.2 2.0 %collective-permute-start.15 = (f32[4,8,1920]{2,1,0:T(8,128)S(1)}, f32[4,8,1920]{2,1,0:T(8,128)S(1)}, u32[]{:S(2)}, u32[]{:S(2)}) collective-permute-start(f32[4,8,1920]{2,1,0:T(8,128)S(1)} %get-tuple-element.67), channel_id=1, source_target_pairs={{0,64},{4,20},{8,72},{12,28},{16,80},{20,4},{24,88},{28,12},{32,96... | collective-permute-start | bytes 737288 | tf_op jit(solution)/shard_map/ppermute | solution.py:445
  55.2 1.2 %collective-permute-start.16 = (f32[4,8,1920]{2,1,0:T(8,128)S(1)}, f32[4,8,1920]{2,1,0:T(8,128)S(1)}, u32[]{:S(2)}, u32[]{:S(2)}) collective-permute-start(f32[4,8,1920]{2,1,0:T(8,128)S(1)} %get-tuple-element.68), channel_id=1, source_target_pairs={{0,96},{4,28},{8,104},{12,4},{16,112},{20,12},{24,120},{28,20},{32... | collective-permute-start | bytes 737288 | tf_op jit(solution)/shard_map/ppermute | solution.py:445
  56.4 6.8 %collective-permute-done.14.b_ref = f32[4,8,1920]{2,1,0:T(8,128)S(1)} collective-permute-done((f32[4,8,1920]{2,1,0:T(8,128)S(1)}, f32[4,8,1920]{2,1,0:T(8,128)S(1)}, u32[]{:S(2)}, u32[]{:S(2)}) %collective-permute-start.14) | collective-permute-done | bytes 245792 | tf_op jit(solution)/shard_map/ppermute | solution.py:445
  64.3 3.9 %collective-permute-start.18 = (f32[8,1920]{1,0:T(8,128)S(1)}, f32[8,1920]{1,0:T(8,128)S(1)}, u32[]{:S(2)}, u32[]{:S(2)}) collective-permute-start(f32[8,1920]{1,0:T(8,128)S(1)} %get-tuple-element.71), channel_id=1, source_target_pairs={{0,16},{4,68},{8,24},{12,76},{16,0},{20,84},{24,8},{28,92},{32,48}... | collective-permute-start | bytes 184328 | tf_op jit(solution)/shard_map/ppermute | solution.py:445
  68.2 1.5 %collective-permute-done.17.b_ref = f32[8,1920]{1,0:T(8,128)S(1)} collective-permute-done((f32[8,1920]{1,0:T(8,128)S(1)}, f32[8,1920]{1,0:T(8,128)S(1)}, u32[]{:S(2)}, u32[]{:S(2)}) %collective-permute-start.17) | collective-permute-done | bytes 61472 | tf_op jit(solution)/shard_map/ppermute | solution.py:445
  69.7 1.3 %collective-permute-done.18.c_ref = f32[8,1920]{1,0:T(8,128)S(1)} collective-permute-done((f32[8,1920]{1,0:T(8,128)S(1)}, f32[8,1920]{1,0:T(8,128)S(1)}, u32[]{:S(2)}, u32[]{:S(2)}) %collective-permute-start.18) | collective-permute-done | bytes 61472 | tf_op jit(solution)/shard_map/ppermute | solution.py:445
  71.0 1.4 %collective-permute-done.19.d_ref = f32[8,1920]{1,0:T(8,128)S(1)} collective-permute-done((f32[8,1920]{1,0:T(8,128)S(1)}, f32[8,1920]{1,0:T(8,128)S(1)}, u32[]{:S(2)}, u32[]{:S(2)}) %collective-permute-start.19) | collective-permute-done | bytes 61472 | tf_op jit(solution)/shard_map/ppermute | solution.py:445
  72.4 1.3 %collective-permute-start.22 = (f32[8,1920]{1,0:T(8,128)S(1)}, f32[8,1920]{1,0:T(8,128)S(1)}, u32[]{:S(2)}, u32[]{:S(2)}) collective-permute-start(f32[8,1920]{1,0:T(8,128)S(1)} %plane_sum.1.a_ref), channel_id=1, source_target_pairs={{0,2},{1,3},{2,0},{3,1},{4,6},{5,7},{6,4},{7,5},{8,10},{9,11},{10,... | collective-permute-start | bytes 184328 | tf_op jit(solution)/shard_map/ppermute | solution.py:440
  75.7 2.4 %collective-permute-done.22.d_ref = f32[8,1920]{1,0:T(8,128)S(1)} collective-permute-done((f32[8,1920]{1,0:T(8,128)S(1)}, f32[8,1920]{1,0:T(8,128)S(1)}, u32[]{:S(2)}, u32[]{:S(2)}) %collective-permute-start.22) | collective-permute-done | bytes 61472 | tf_op jit(solution)/shard_map/ppermute | solution.py:440
  78.2 2.1 %collective-permute-done.20.b_ref = f32[8,1920]{1,0:T(8,128)S(1)} collective-permute-done((f32[8,1920]{1,0:T(8,128)S(1)}, f32[8,1920]{1,0:T(8,128)S(1)}, u32[]{:S(2)}, u32[]{:S(2)}) %collective-permute-start.20) | collective-permute-done | bytes 61472 | tf_op jit(solution)/shard_map/ppermute | solution.py:440
  (51 shorter events, 15.0 us)
Async XLA Ops:
  0.7 20.0 %copy-start.6 = (s32[128,1024]{1,0:T(8,128)S(1)}, s32[128,1024]{1,0:T(8,128)}, u32[]{:S(2)}) copy-start(s32[128,1024]{1,0:T(8,128)} %active_ref) | copy-start | bytes 1572868
  5.4 9.9 %collective-permute-start.2 = (f32[8,3584]{1,0:T(8,128)S(1)}, f32[8,3584]{1,0:T(8,128)S(1)}, u32[]{:S(2)}, u32[]{:S(2)}) collective-permute-start(f32[8,3584]{1,0:T(8,128)S(1)} %get-tuple-element.44.a_ref), channel_id=1, source_target_pairs={{0,2},{1,3},{2,0},{3,1},{4,6},{5,7},{6,4},{7,5},{8,10},{9,11},{10,... | collective-permute-start | bytes 344072 | tf_op jit(solution)/shard_map/ppermute | solution.py:440
  8.7 6.5 %collective-permute-start.1 = (f32[8,3584]{1,0:T(8,128)S(1)}, f32[8,3584]{1,0:T(8,128)S(1)}, u32[]{:S(2)}, u32[]{:S(2)}) collective-permute-start(f32[8,3584]{1,0:T(8,128)S(1)} %get-tuple-element.44.a_ref), channel_id=1, source_target_pairs={{0,3},{1,0},{2,1},{3,2},{4,7},{5,4},{6,5},{7,6},{8,11},{9,8},{10,9... | collective-permute-start | bytes 344072 | tf_op jit(solution)/shard_map/ppermute | solution.py:440
  9.8 6.0 %collective-permute-start = (f32[8,3584]{1,0:T(8,128)S(1)}, f32[8,3584]{1,0:T(8,128)S(1)}, u32[]{:S(2)}, u32[]{:S(2)}) collective-permute-start(f32[8,3584]{1,0:T(8,128)S(1)} %get-tuple-element.44.a_ref), channel_id=1, source_target_pairs={{0,1},{1,2},{2,3},{3,0},{4,5},{5,6},{6,7},{7,4},{8,9},{9,10},{10,1... | collective-permute-start | bytes 344072 | tf_op jit(solution)/shard_map/ppermute | solution.py:440
  16.2 8.7 %collective-permute-start.5 = (f32[8,3712]{1,0:T(8,128)S(1)}, f32[8,3712]{1,0:T(8,128)S(1)}, u32[]{:S(2)}, u32[]{:S(2)}) collective-permute-start(f32[8,3712]{1,0:T(8,128)S(1)} %get-tuple-element.53.a_ref), channel_id=1, source_target_pairs={{0,96},{4,28},{8,104},{12,4},{16,112},{20,12},{24,120},{28,20},{32... | collective-permute-start | bytes 356360 | tf_op jit(solution)/shard_map/ppermute | solution.py:445
  19.0 6.4 %collective-permute-start.4 = (f32[8,3712]{1,0:T(8,128)S(1)}, f32[8,3712]{1,0:T(8,128)S(1)}, u32[]{:S(2)}, u32[]{:S(2)}) collective-permute-start(f32[8,3712]{1,0:T(8,128)S(1)} %get-tuple-element.53.a_ref), channel_id=1, source_target_pairs={{0,64},{4,20},{8,72},{12,28},{16,80},{20,4},{24,88},{28,12},{32,96... | collective-permute-start | bytes 356360 | tf_op jit(solution)/shard_map/ppermute | solution.py:445
  19.8 6.8 %collective-permute-start.3 = (f32[8,3712]{1,0:T(8,128)S(1)}, f32[8,3712]{1,0:T(8,128)S(1)}, u32[]{:S(2)}, u32[]{:S(2)}) collective-permute-start(f32[8,3712]{1,0:T(8,128)S(1)} %get-tuple-element.53.a_ref), channel_id=1, source_target_pairs={{0,32},{4,12},{8,40},{12,20},{16,48},{20,28},{24,56},{28,4},{32,64... | collective-permute-start | bytes 356360 | tf_op jit(solution)/shard_map/ppermute | solution.py:445
  26.6 11.0 %collective-permute-start.9 = (f32[4,8,3712]{2,1,0:T(8,128)S(1)}, f32[4,8,3712]{2,1,0:T(8,128)S(1)}, u32[]{:S(2)}, u32[]{:S(2)}) collective-permute-start(f32[4,8,3712]{2,1,0:T(8,128)S(1)} %line.1.a_ref), channel_id=1, source_target_pairs={{0,16},{4,68},{8,24},{12,76},{16,0},{20,84},{24,8},{28,92},{32,48}... | collective-permute-start | bytes 1425416 | tf_op jit(solution)/shard_map/ppermute | solution.py:445
  30.9 13.2 %collective-permute-start.11 = (f32[4,8,3712]{2,1,0:T(8,128)S(1)}, f32[4,8,3712]{2,1,0:T(8,128)S(1)}, u32[]{:S(2)}, u32[]{:S(2)}) collective-permute-start(f32[4,8,3712]{2,1,0:T(8,128)S(1)} %line.1.a_ref), channel_id=1, source_target_pairs={{0,24},{4,100},{8,0},{12,108},{16,8},{20,116},{24,16},{28,124},{32... | collective-permute-start | bytes 1425416 | tf_op jit(solution)/shard_map/ppermute | solution.py:445
  31.6 12.5 %collective-permute-start.7 = (f32[4,8,3712]{2,1,0:T(8,128)S(1)}, f32[4,8,3712]{2,1,0:T(8,128)S(1)}, u32[]{:S(2)}, u32[]{:S(2)}) collective-permute-start(f32[4,8,3712]{2,1,0:T(8,128)S(1)} %line.1.a_ref), channel_id=1, source_target_pairs={{0,8},{4,36},{8,16},{12,44},{16,24},{20,52},{24,0},{28,60},{32,40}... | collective-permute-start | bytes 1425416 | tf_op jit(solution)/shard_map/ppermute | solution.py:445
  34.8 11.1 %collective-permute-start.6 = (f32[4,8,3712]{2,1,0:T(8,128)S(1)}, f32[4,8,3712]{2,1,0:T(8,128)S(1)}, u32[]{:S(2)}, u32[]{:S(2)}) collective-permute-start(f32[4,8,3712]{2,1,0:T(8,128)S(1)} %line.1.a_ref), channel_id=1, source_target_pairs={{0,4},{4,0},{8,12},{12,8},{16,20},{20,16},{24,28},{28,24},{32,36},... | collective-permute-start | bytes 1425416 | tf_op jit(solution)/shard_map/ppermute | solution.py:449
  44.1 1.8 %collective-permute-start.12 = (f32[4,8,3712]{2,1,0:T(8,128)S(1)}, f32[4,8,3712]{2,1,0:T(8,128)S(1)}, u32[]{:S(2)}, u32[]{:S(2)}) collective-permute-start(f32[4,8,3712]{2,1,0:T(8,128)S(1)} %collective-permute-done.11.d_ref), channel_id=1, source_target_pairs={{0,4},{4,0},{8,12},{12,8},{16,20},{20,16},{24,28},{28,24},{32,36},... | collective-permute-start | bytes 1425416 | tf_op jit(solution)/shard_map/ppermute | solution.py:449
  44.1 2.5 %collective-permute-start.8 = (f32[4,8,3712]{2,1,0:T(8,128)S(1)}, f32[4,8,3712]{2,1,0:T(8,128)S(1)}, u32[]{:S(2)}, u32[]{:S(2)}) collective-permute-start(f32[4,8,3712]{2,1,0:T(8,128)S(1)} %collective-permute-done.7.b_ref), channel_id=1, source_target_pairs={{0,4},{4,0},{8,12},{12,8},{16,20},{20,16},{24,28},{28,24},{32,36},... | collective-permute-start | bytes 1425416 | tf_op jit(solution)/shard_map/ppermute | solution.py:449
  44.6 2.7 %collective-permute-start.10 = (f32[4,8,3712]{2,1,0:T(8,128)S(1)}, f32[4,8,3712]{2,1,0:T(8,128)S(1)}, u32[]{:S(2)}, u32[]{:S(2)}) collective-permute-start(f32[4,8,3712]{2,1,0:T(8,128)S(1)} %collective-permute-done.9.c_ref), channel_id=1, source_target_pairs={{0,4},{4,0},{8,12},{12,8},{16,20},{20,16},{24,28},{28,24},{32,36},... | collective-permute-start | bytes 1425416 | tf_op jit(solution)/shard_map/ppermute | solution.py:449
  50.2 2.6 %collective-permute-start.13 = (f32[64,3840]{1,0:T(8,128)S(1)}, f32[64,3840]{1,0:T(8,128)S(1)}, u32[]{:S(2)}, u32[]{:S(2)}) collective-permute-start(f32[64,3840]{1,0:T(8,128)S(1)} %get-tuple-element.64), channel_id=1, source_target_pairs={{0,4},{4,0},{8,12},{12,8},{16,20},{20,16},{24,28},{28,24},{32,36},... | collective-permute-start | bytes 2949128 | tf_op jit(solution)/shard_map/ppermute | solution.py:449
  53.1 10.1 %collective-permute-start.14 = (f32[4,8,1920]{2,1,0:T(8,128)S(1)}, f32[4,8,1920]{2,1,0:T(8,128)S(1)}, u32[]{:S(2)}, u32[]{:S(2)}) collective-permute-start(f32[4,8,1920]{2,1,0:T(8,128)S(1)} %get-tuple-element.66), channel_id=1, source_target_pairs={{0,32},{4,12},{8,40},{12,20},{16,48},{20,28},{24,56},{28,4},{32,64... | collective-permute-start | bytes 737288 | tf_op jit(solution)/shard_map/ppermute | solution.py:445
  53.2 10.0 %collective-permute-start.15 = (f32[4,8,1920]{2,1,0:T(8,128)S(1)}, f32[4,8,1920]{2,1,0:T(8,128)S(1)}, u32[]{:S(2)}, u32[]{:S(2)}) collective-permute-start(f32[4,8,1920]{2,1,0:T(8,128)S(1)} %get-tuple-element.67), channel_id=1, source_target_pairs={{0,64},{4,20},{8,72},{12,28},{16,80},{20,4},{24,88},{28,12},{32,96... | collective-permute-start | bytes 737288 | tf_op jit(solution)/shard_map/ppermute | solution.py:445
  55.2 8.9 %collective-permute-start.16 = (f32[4,8,1920]{2,1,0:T(8,128)S(1)}, f32[4,8,1920]{2,1,0:T(8,128)S(1)}, u32[]{:S(2)}, u32[]{:S(2)}) collective-permute-start(f32[4,8,1920]{2,1,0:T(8,128)S(1)} %get-tuple-element.68), channel_id=1, source_target_pairs={{0,96},{4,28},{8,104},{12,4},{16,112},{20,12},{24,120},{28,20},{32... | collective-permute-start | bytes 737288 | tf_op jit(solution)/shard_map/ppermute | solution.py:445
  64.2 5.5 %collective-permute-start.17 = (f32[8,1920]{1,0:T(8,128)S(1)}, f32[8,1920]{1,0:T(8,128)S(1)}, u32[]{:S(2)}, u32[]{:S(2)}) collective-permute-start(f32[8,1920]{1,0:T(8,128)S(1)} %get-tuple-element.70), channel_id=1, source_target_pairs={{0,8},{4,36},{8,16},{12,44},{16,24},{20,52},{24,0},{28,60},{32,40}... | collective-permute-start | bytes 184328 | tf_op jit(solution)/shard_map/ppermute | solution.py:445
  64.3 6.7 %collective-permute-start.18 = (f32[8,1920]{1,0:T(8,128)S(1)}, f32[8,1920]{1,0:T(8,128)S(1)}, u32[]{:S(2)}, u32[]{:S(2)}) collective-permute-start(f32[8,1920]{1,0:T(8,128)S(1)} %get-tuple-element.71), channel_id=1, source_target_pairs={{0,16},{4,68},{8,24},{12,76},{16,0},{20,84},{24,8},{28,92},{32,48}... | collective-permute-start | bytes 184328 | tf_op jit(solution)/shard_map/ppermute | solution.py:445
  68.1 4.2 %collective-permute-start.19 = (f32[8,1920]{1,0:T(8,128)S(1)}, f32[8,1920]{1,0:T(8,128)S(1)}, u32[]{:S(2)}, u32[]{:S(2)}) collective-permute-start(f32[8,1920]{1,0:T(8,128)S(1)} %get-tuple-element.72), channel_id=1, source_target_pairs={{0,24},{4,100},{8,0},{12,108},{16,8},{20,116},{24,16},{28,124},{32... | collective-permute-start | bytes 184328 | tf_op jit(solution)/shard_map/ppermute | solution.py:445
  72.4 5.8 %collective-permute-start.22 = (f32[8,1920]{1,0:T(8,128)S(1)}, f32[8,1920]{1,0:T(8,128)S(1)}, u32[]{:S(2)}, u32[]{:S(2)}) collective-permute-start(f32[8,1920]{1,0:T(8,128)S(1)} %plane_sum.1.a_ref), channel_id=1, source_target_pairs={{0,2},{1,3},{2,0},{3,1},{4,6},{5,7},{6,4},{7,5},{8,10},{9,11},{10,... | collective-permute-start | bytes 184328 | tf_op jit(solution)/shard_map/ppermute | solution.py:440
  73.7 4.5 %collective-permute-start.21 = (f32[8,1920]{1,0:T(8,128)S(1)}, f32[8,1920]{1,0:T(8,128)S(1)}, u32[]{:S(2)}, u32[]{:S(2)}) collective-permute-start(f32[8,1920]{1,0:T(8,128)S(1)} %plane_sum.1.a_ref), channel_id=1, source_target_pairs={{0,3},{1,0},{2,1},{3,2},{4,7},{5,4},{6,5},{7,6},{8,11},{9,8},{10,9... | collective-permute-start | bytes 184328 | tf_op jit(solution)/shard_map/ppermute | solution.py:440
  74.9 5.4 %collective-permute-start.20 = (f32[8,1920]{1,0:T(8,128)S(1)}, f32[8,1920]{1,0:T(8,128)S(1)}, u32[]{:S(2)}, u32[]{:S(2)}) collective-permute-start(f32[8,1920]{1,0:T(8,128)S(1)} %plane_sum.1.a_ref), channel_id=1, source_target_pairs={{0,1},{1,2},{2,3},{3,0},{4,5},{5,6},{6,7},{7,4},{8,9},{9,10},{10,1... | collective-permute-start | bytes 184328 | tf_op jit(solution)/shard_map/ppermute | solution.py:440
  (7 other events, 40.3 us)

commit v4 on v3

--- a/solution.py
+++ b/solution.py
@@ -187,7 +187,7 @@
 
 
 def line_kernel(a_ref, b_ref, c_ref, d_ref, out_ref):
-    for d, ref in enumerate((a_ref, b_ref, c_ref, d_ref)):
+    for d, ref in zip((0, *(1,2,3)), (a_ref, b_ref, c_ref, d_ref)):
         out_ref[d] = ref[...]
 
 
@@ -436,8 +436,8 @@
     )
 
 
-def over_tp(x):
-    others = [lax.ppermute(x, "tp", [(i, (i + d) % 4) for i in range(4)]) for d in (1, 3, 2)]
+def over_tp(x, order):
+    others = [lax.ppermute(x, "tp", [(i, (i + d) % 4) for i in range(4)]) for d in order]
     return [x] + others
 
 
@@ -458,21 +458,23 @@
     )
     gain = post_gain.reshape(1, D)
     resid = resid_project(resid_corrupt, resid_clean, w_enc)
-    *parts, resid = lax.optimization_barrier((*over_tp(part), resid))
+    *parts, resid = lax.optimization_barrier((*over_tp(part, (3,1,2)), resid))
     attn, msg = norm(parts, resid_corrupt, resid_clean, gain)
     gf = grad_f(cot, w_dec, active)
-    *parts, gf = lax.optimization_barrier((msg, *[send(msg, 0, d) for d in (1, 2, 3)], gf))
+    parts = [msg] + [send(msg, 0, d) for d in (1,2,3)]
+    *parts, gf = lax.optimization_barrier((*parts, gf))
     block = line(parts)
     flipped = flip(w_enc)
     blocks = [block] + [send(block, 1, e) for e in (1, 2, 3)]
     blocks[2], flipped = lax.optimization_barrier((blocks[2], flipped))
     others = [swap(b) for b in blocks]
+    *blocks, others[2] = lax.optimization_barrier((*blocks, others[2]))
     pre_own, side = own_project(blocks, w_enc)
     raw, keep, give = latents(others, side, pre_own, resid, gf, w_enc, flipped)
     parts = pair_sum(keep, swap(give))
-    parts = line_sum([parts[0]] + [send(parts[d], 0, d) for d in (1, 2, 3)])
-    total = plane_sum([parts[0]] + [send(parts[e], 1, e) for e in (1, 2, 3)])
-    return tuple(result(over_tp(total), attn, heads, gain, raw))
+    parts = line_sum([parts[0]] + [send(parts[d], 0, d) for d in (2,1,3)])
+    total = plane_sum([parts[0]] + [send(parts[e], 1, e) for e in (2,1,3)])
+    return tuple(result(over_tp(total, (3,1,2)), attn, heads, gain, raw))
 
 
 def solution(mesh):

time: 81.5 us -> 78.9 us (0.968)
  waiting for transfers between devices: 31.7 us -> 26.1 us
  starting transfers between devices: 27.7 us -> 30.8 us
    ppermute x12, waiting for transfers between devices: 22.8 us -> 19.7 us  [send(): return lax.ppermute(x, 'lat', shift(stage, d))]
    ppermute x6, waiting for transfers between devices: 5.12 us -> 3.2 us  [over_tp(): lax.ppermute(x, 'tp', [(i, (i + d) % 4) for i in range(4)])]
    ppermute x6, starting transfers between devices: 8.75 us -> 10.3 us  [over_tp(): lax.ppermute(x, 'tp', [(i, (i + d) % 4) for i in range(4)])]
    ppermute x12, starting transfers between devices: 18.1 us -> 19.3 us  [send(): return lax.ppermute(x, 'lat', shift(stage, d))]
  transfers between devices with their start and end apart: 23 -> 23, of which waited for: 15 -> 14; matrix products, arithmetic and copies ran while one was open for 0% -> 0% of each run, Pallas kernels for 12% -> 12%
where the time goes in v4:
time: 78.9 us; the launch traced here: 78.8 us
  starting transfers between devices  30.8 us (39%)
  waiting for transfers between devices  26.1 us (33%)
  Pallas kernels  18.7 us (24%)
  local copies, waits for them, and re-layouts  2.39 us (3%)
  between operations  0.81 us (1%)
    ppermute x12, waiting for transfers between devices, send(): return lax.ppermute(x, 'lat', shift(stage, d))  19.7 us
    ppermute x12, starting transfers between devices, send(): return lax.ppermute(x, 'lat', shift(stage, d))  19.3 us
    pallas_call x12, Pallas kernels, call(): pl.pallas_call(kernel, in_specs=[pl.BlockSpec(memory_space=s) for s in sp...  18.7 us
    ppermute x6, starting transfers between devices, over_tp(): lax.ppermute(x, 'tp', [(i, (i + d) % 4) for i in range(4)])  10.3 us
    ppermute x6, waiting for transfers between devices, over_tp(): lax.ppermute(x, 'tp', [(i, (i + d) % 4) for i in range(4)])  3.2 us
    ppermute x5, waiting for transfers between devices, swap(): return lax.ppermute(x, 'lat', CORE_SWAP)  3.16 us
    unnamed x16, local copies, waits for them, and re-layouts  2.38 us
  transfers between devices with their start and end apart: 23, of which 14 were waited for; matrix products, arithmetic and copies ran while one was open for 0% of the time, Pallas kernels for 12%

profile of v4, /device:TPU:0, one launch (start us, length us, event | category | flops | bytes accessed | tf_op | source)
XLA Modules:
  0.0 78.8 jit_solution(11107870052146035735)
XLA Ops:
  0.7 4.7 %project.1 = (f32[4,8,3584]{2,1,0:T(8,128)S(1)}, f32[8,3584]{1,0:T(8,128)S(1)}) custom-call(bf16[128,1024]{1,0:T(8,128)(2,1)} %zc_ref.1, bf16[128,1024]{1,0:T(8,128)(2,1)} %zn_ref.1, bf16[1024,3584]{1,0:T(8,128)(2,1)} %w_ref.1), custom_call_target="tpu_custom_call" | custom-call | flops 117440512 | bytes 7864320 | tf_op jit(solution)/shard_map/project/pallas_call | solution.py:55
  5.4 3.4 %collective-permute-start.2 = (f32[8,3584]{1,0:T(8,128)S(1)}, f32[8,3584]{1,0:T(8,128)S(1)}, u32[]{:S(2)}, u32[]{:S(2)}) collective-permute-start(f32[8,3584]{1,0:T(8,128)S(1)} %get-tuple-element.49.a_ref), channel_id=1, source_target_pairs={{0,2},{1,3},{2,0},{3,1},{4,6},{5,7},{6,4},{7,5},{8,10},{9,11},{10,... | collective-permute-start | bytes 344072 | tf_op jit(solution)/shard_map/ppermute | solution.py:440
  9.4 2.6 %collective-permute-start = (f32[8,3584]{1,0:T(8,128)S(1)}, f32[8,3584]{1,0:T(8,128)S(1)}, u32[]{:S(2)}, u32[]{:S(2)}) collective-permute-start(f32[8,3584]{1,0:T(8,128)S(1)} %get-tuple-element.49.a_ref), channel_id=1, source_target_pairs={{0,3},{1,0},{2,1},{3,2},{4,7},{5,4},{6,5},{7,6},{8,11},{9,8},{10,9... | collective-permute-start | bytes 344072 | tf_op jit(solution)/shard_map/ppermute | solution.py:440
  14.4 2.1 %resid_project.1.resid_ref = f32[2,128,1024]{2,1,0:T(8,128)S(1)} custom-call(bf16[128,3584]{1,0:T(8,128)(2,1)S(1)} %copy-done.1, bf16[128,3584]{1,0:T(8,128)(2,1)S(1)} %copy-done.3, bf16[3584,1024]{1,0:T(8,128)(2,1)S(1)} %copy-done), custom_call_target="tpu_custom_call" | custom-call | flops 1879048192 | bytes 9175040 | tf_op jit(solution)/shard_map/resid_project/pallas_call | solution.py:55
  16.8 2.8 %collective-permute-start.5 = (f32[8,3712]{1,0:T(8,128)S(1)}, f32[8,3712]{1,0:T(8,128)S(1)}, u32[]{:S(2)}, u32[]{:S(2)}) collective-permute-start(f32[8,3712]{1,0:T(8,128)S(1)} %get-tuple-element.58.a_ref), channel_id=1, source_target_pairs={{0,96},{4,28},{8,104},{12,4},{16,112},{20,12},{24,120},{28,20},{32... | collective-permute-start | bytes 356360 | tf_op jit(solution)/shard_map/ppermute | solution.py:445
  21.4 4.1 %grad_f.1.gf_ref = f32[4,128,1024]{2,1,0:T(8,128)S(1)} custom-call(bf16[128,4,3584]{2,1,0:T(4,128)(2,1)S(1)} %copy-done.5, bf16[1024,3584]{1,0:T(8,128)(2,1)S(1)} %copy-done.4, s32[128,1024]{1,0:T(8,128)S(1)} %copy-done.6), custom_call_target="tpu_custom_call" | custom-call | flops 3758096384 | bytes 11534336 | tf_op jit(solution)/shard_map/grad_f/pallas_call | solution.py:55
  26.1 1.2 %collective-permute-done.3.b_ref = f32[8,3712]{1,0:T(8,128)S(1)} collective-permute-done((f32[8,3712]{1,0:T(8,128)S(1)}, f32[8,3712]{1,0:T(8,128)S(1)}, u32[]{:S(2)}, u32[]{:S(2)}) %collective-permute-start.3) | collective-permute-done | bytes 118816 | tf_op jit(solution)/shard_map/ppermute | solution.py:445
  27.3 4.0 %collective-permute-start.9 = (f32[4,8,3712]{2,1,0:T(8,128)S(1)}, f32[4,8,3712]{2,1,0:T(8,128)S(1)}, u32[]{:S(2)}, u32[]{:S(2)}) collective-permute-start(f32[4,8,3712]{2,1,0:T(8,128)S(1)} %line.1.a_ref), channel_id=1, source_target_pairs={{0,16},{4,68},{8,24},{12,76},{16,0},{20,84},{24,8},{28,92},{32,48}... | collective-permute-start | bytes 1425416 | tf_op jit(solution)/shard_map/ppermute | solution.py:445
  32.0 1.3 %collective-permute-start.7 = (f32[4,8,3712]{2,1,0:T(8,128)S(1)}, f32[4,8,3712]{2,1,0:T(8,128)S(1)}, u32[]{:S(2)}, u32[]{:S(2)}) collective-permute-start(f32[4,8,3712]{2,1,0:T(8,128)S(1)} %line.1.a_ref), channel_id=1, source_target_pairs={{0,8},{4,36},{8,16},{12,44},{16,24},{20,52},{24,0},{28,60},{32,40}... | collective-permute-start | bytes 1425416 | tf_op jit(solution)/shard_map/ppermute | solution.py:445
  33.3 1.9 %flip.1.flip_ref = bf16[1024,3584]{1,0:T(8,128)(2,1)S(1)} custom-call(bf16[3584,1024]{1,0:T(8,128)(2,1)S(1)} %copy-done), custom_call_target="tpu_custom_call" | custom-call | flops 1000000 | bytes 7340032 | tf_op jit(solution)/shard_map/flip/pallas_call | solution.py:55
  35.2 2.8 %collective-permute-done.9.c_ref = f32[4,8,3712]{2,1,0:T(8,128)S(1)} collective-permute-done((f32[4,8,3712]{2,1,0:T(8,128)S(1)}, f32[4,8,3712]{2,1,0:T(8,128)S(1)}, u32[]{:S(2)}, u32[]{:S(2)}) %collective-permute-start.9) | collective-permute-done | bytes 475168 | tf_op jit(solution)/shard_map/ppermute | solution.py:445
  38.5 5.7 %collective-permute-done.10.d_ref = f32[4,8,3712]{2,1,0:T(8,128)S(1)} collective-permute-done((f32[4,8,3712]{2,1,0:T(8,128)S(1)}, f32[4,8,3712]{2,1,0:T(8,128)S(1)}, u32[]{:S(2)}, u32[]{:S(2)}) %collective-permute-start.10) | collective-permute-done | bytes 475168 | tf_op jit(solution)/shard_map/ppermute | solution.py:445
  44.8 1.3 %own_project.1 = (f32[128,1024]{1,0:T(8,128)S(1)}, f32[16,8,128]{2,1,0:T(8,128)S(1)}) custom-call(f32[4,8,3712]{2,1,0:T(8,128)S(1)} %line.1.a_ref, f32[4,8,3712]{2,1,0:T(8,128)S(1)} %collective-permute-done.7.b_ref, f32[4,8,3712]{2,1,0:T(8,128)S(1)} %collective-permute-done.9.c_ref, f32[4,8,3712]{2,1,0:T(8,128)S(1)} %collective-permute-done.10.d_ref, ...), custom_call_target="tpu_custom_call" | custom-call | flops 939524096 | bytes 9240576 | tf_op jit(solution)/shard_map/own_project/pallas_call | solution.py:55
  46.8 2.9 %latents.1 = (f32[128,1024]{1,0:T(8,128)S(1)}, f32[64,3840]{1,0:T(8,128)S(1)}, f32[64,3840]{1,0:T(8,128)S(1)}) custom-call(f32[4,8,3712]{2,1,0:T(8,128)S(1)} %collective-permute-done.6.a_ref, f32[4,8,3712]{2,1,0:T(8,128)S(1)} %collective-permute-done.8.b_ref, f32[4,8,3712]{2,1,0:T(8,128)S(1)} %collective-permute-done.11.c_ref, ...), custom_call_target="tpu_custom_call" | custom-call | flops 1879048192 | bytes 20316160 | tf_op jit(solution)/shard_map/latents/pallas_call | solution.py:55
  49.9 2.4 %collective-permute-done.13.b_ref = f32[64,3840]{1,0:T(8,128)S(1)} collective-permute-done((f32[64,3840]{1,0:T(8,128)S(1)}, f32[64,3840]{1,0:T(8,128)S(1)}, u32[]{:S(2)}, u32[]{:S(2)}) %collective-permute-start.13) | collective-permute-done | bytes 983072 | tf_op jit(solution)/shard_map/ppermute | solution.py:449
  54.1 2.4 %collective-permute-start.16 = (f32[4,8,1920]{2,1,0:T(8,128)S(1)}, f32[4,8,1920]{2,1,0:T(8,128)S(1)}, u32[]{:S(2)}, u32[]{:S(2)}) collective-permute-start(f32[4,8,1920]{2,1,0:T(8,128)S(1)} %get-tuple-element.78), channel_id=1, source_target_pairs={{0,96},{4,28},{8,104},{12,4},{16,112},{20,12},{24,120},{28,20},{32... | collective-permute-start | bytes 737288 | tf_op jit(solution)/shard_map/ppermute | solution.py:445
  56.5 4.0 %collective-permute-done.14.b_ref = f32[4,8,1920]{2,1,0:T(8,128)S(1)} collective-permute-done((f32[4,8,1920]{2,1,0:T(8,128)S(1)}, f32[4,8,1920]{2,1,0:T(8,128)S(1)}, u32[]{:S(2)}, u32[]{:S(2)}) %collective-permute-start.14) | collective-permute-done | bytes 245792 | tf_op jit(solution)/shard_map/ppermute | solution.py:445
  60.5 2.5 %collective-permute-done.15.c_ref = f32[4,8,1920]{2,1,0:T(8,128)S(1)} collective-permute-done((f32[4,8,1920]{2,1,0:T(8,128)S(1)}, f32[4,8,1920]{2,1,0:T(8,128)S(1)}, u32[]{:S(2)}, u32[]{:S(2)}) %collective-permute-start.15) | collective-permute-done | bytes 245792 | tf_op jit(solution)/shard_map/ppermute | solution.py:445
  63.1 1.7 %collective-permute-start.17 = (f32[8,1920]{1,0:T(8,128)S(1)}, f32[8,1920]{1,0:T(8,128)S(1)}, u32[]{:S(2)}, u32[]{:S(2)}) collective-permute-start(f32[8,1920]{1,0:T(8,128)S(1)} %get-tuple-element.80), channel_id=1, source_target_pairs={{0,16},{4,68},{8,24},{12,76},{16,0},{20,84},{24,8},{28,92},{32,48}... | collective-permute-start | bytes 184328 | tf_op jit(solution)/shard_map/ppermute | solution.py:445
  64.7 1.9 %collective-permute-start.18 = (f32[8,1920]{1,0:T(8,128)S(1)}, f32[8,1920]{1,0:T(8,128)S(1)}, u32[]{:S(2)}, u32[]{:S(2)}) collective-permute-start(f32[8,1920]{1,0:T(8,128)S(1)} %get-tuple-element.81), channel_id=1, source_target_pairs={{0,8},{4,36},{8,16},{12,44},{16,24},{20,52},{24,0},{28,60},{32,40}... | collective-permute-start | bytes 184328 | tf_op jit(solution)/shard_map/ppermute | solution.py:445
  66.6 1.3 %collective-permute-start.19 = (f32[8,1920]{1,0:T(8,128)S(1)}, f32[8,1920]{1,0:T(8,128)S(1)}, u32[]{:S(2)}, u32[]{:S(2)}) collective-permute-start(f32[8,1920]{1,0:T(8,128)S(1)} %get-tuple-element.82), channel_id=1, source_target_pairs={{0,24},{4,100},{8,0},{12,108},{16,8},{20,116},{24,16},{28,124},{32... | collective-permute-start | bytes 184328 | tf_op jit(solution)/shard_map/ppermute | solution.py:445
  68.9 1.3 %collective-permute-done.18.c_ref = f32[8,1920]{1,0:T(8,128)S(1)} collective-permute-done((f32[8,1920]{1,0:T(8,128)S(1)}, f32[8,1920]{1,0:T(8,128)S(1)}, u32[]{:S(2)}, u32[]{:S(2)}) %collective-permute-start.18) | collective-permute-done | bytes 61472 | tf_op jit(solution)/shard_map/ppermute | solution.py:445
  71.3 2.2 %collective-permute-start.21 = (f32[8,1920]{1,0:T(8,128)S(1)}, f32[8,1920]{1,0:T(8,128)S(1)}, u32[]{:S(2)}, u32[]{:S(2)}) collective-permute-start(f32[8,1920]{1,0:T(8,128)S(1)} %plane_sum.1.a_ref), channel_id=1, source_target_pairs={{0,1},{1,2},{2,3},{3,0},{4,5},{5,6},{6,7},{7,4},{8,9},{9,10},{10,1... | collective-permute-start | bytes 184328 | tf_op jit(solution)/shard_map/ppermute | solution.py:440
  74.5 2.2 %collective-permute-done.22.d_ref = f32[8,1920]{1,0:T(8,128)S(1)} collective-permute-done((f32[8,1920]{1,0:T(8,128)S(1)}, f32[8,1920]{1,0:T(8,128)S(1)}, u32[]{:S(2)}, u32[]{:S(2)}) %collective-permute-start.22) | collective-permute-done | bytes 61472 | tf_op jit(solution)/shard_map/ppermute | solution.py:440
  (51 shorter events, 15.3 us)
Async XLA Ops:
  0.7 20.7 %copy-start.6 = (s32[128,1024]{1,0:T(8,128)S(1)}, s32[128,1024]{1,0:T(8,128)}, u32[]{:S(2)}) copy-start(s32[128,1024]{1,0:T(8,128)} %active_ref) | copy-start | bytes 1572868
  5.4 11.1 %collective-permute-start.2 = (f32[8,3584]{1,0:T(8,128)S(1)}, f32[8,3584]{1,0:T(8,128)S(1)}, u32[]{:S(2)}, u32[]{:S(2)}) collective-permute-start(f32[8,3584]{1,0:T(8,128)S(1)} %get-tuple-element.49.a_ref), channel_id=1, source_target_pairs={{0,2},{1,3},{2,0},{3,1},{4,6},{5,7},{6,4},{7,5},{8,10},{9,11},{10,... | collective-permute-start | bytes 344072 | tf_op jit(solution)/shard_map/ppermute | solution.py:440
  8.7 7.7 %collective-permute-start.1 = (f32[8,3584]{1,0:T(8,128)S(1)}, f32[8,3584]{1,0:T(8,128)S(1)}, u32[]{:S(2)}, u32[]{:S(2)}) collective-permute-start(f32[8,3584]{1,0:T(8,128)S(1)} %get-tuple-element.49.a_ref), channel_id=1, source_target_pairs={{0,1},{1,2},{2,3},{3,0},{4,5},{5,6},{6,7},{7,4},{8,9},{9,10},{10,1... | collective-permute-start | bytes 344072 | tf_op jit(solution)/shard_map/ppermute | solution.py:440
  9.4 7.1 %collective-permute-start = (f32[8,3584]{1,0:T(8,128)S(1)}, f32[8,3584]{1,0:T(8,128)S(1)}, u32[]{:S(2)}, u32[]{:S(2)}) collective-permute-start(f32[8,3584]{1,0:T(8,128)S(1)} %get-tuple-element.49.a_ref), channel_id=1, source_target_pairs={{0,3},{1,0},{2,1},{3,2},{4,7},{5,4},{6,5},{7,6},{8,11},{9,8},{10,9... | collective-permute-start | bytes 344072 | tf_op jit(solution)/shard_map/ppermute | solution.py:440
  16.8 8.7 %collective-permute-start.5 = (f32[8,3712]{1,0:T(8,128)S(1)}, f32[8,3712]{1,0:T(8,128)S(1)}, u32[]{:S(2)}, u32[]{:S(2)}) collective-permute-start(f32[8,3712]{1,0:T(8,128)S(1)} %get-tuple-element.58.a_ref), channel_id=1, source_target_pairs={{0,96},{4,28},{8,104},{12,4},{16,112},{20,12},{24,120},{28,20},{32... | collective-permute-start | bytes 356360 | tf_op jit(solution)/shard_map/ppermute | solution.py:445
  19.7 6.4 %collective-permute-start.4 = (f32[8,3712]{1,0:T(8,128)S(1)}, f32[8,3712]{1,0:T(8,128)S(1)}, u32[]{:S(2)}, u32[]{:S(2)}) collective-permute-start(f32[8,3712]{1,0:T(8,128)S(1)} %get-tuple-element.58.a_ref), channel_id=1, source_target_pairs={{0,64},{4,20},{8,72},{12,28},{16,80},{20,4},{24,88},{28,12},{32,96... | collective-permute-start | bytes 356360 | tf_op jit(solution)/shard_map/ppermute | solution.py:445
  20.5 6.8 %collective-permute-start.3 = (f32[8,3712]{1,0:T(8,128)S(1)}, f32[8,3712]{1,0:T(8,128)S(1)}, u32[]{:S(2)}, u32[]{:S(2)}) collective-permute-start(f32[8,3712]{1,0:T(8,128)S(1)} %get-tuple-element.58.a_ref), channel_id=1, source_target_pairs={{0,32},{4,12},{8,40},{12,20},{16,48},{20,28},{24,56},{28,4},{32,64... | collective-permute-start | bytes 356360 | tf_op jit(solution)/shard_map/ppermute | solution.py:445
  27.3 10.7 %collective-permute-start.9 = (f32[4,8,3712]{2,1,0:T(8,128)S(1)}, f32[4,8,3712]{2,1,0:T(8,128)S(1)}, u32[]{:S(2)}, u32[]{:S(2)}) collective-permute-start(f32[4,8,3712]{2,1,0:T(8,128)S(1)} %line.1.a_ref), channel_id=1, source_target_pairs={{0,16},{4,68},{8,24},{12,76},{16,0},{20,84},{24,8},{28,92},{32,48}... | collective-permute-start | bytes 1425416 | tf_op jit(solution)/shard_map/ppermute | solution.py:445
  31.3 13.0 %collective-permute-start.10 = (f32[4,8,3712]{2,1,0:T(8,128)S(1)}, f32[4,8,3712]{2,1,0:T(8,128)S(1)}, u32[]{:S(2)}, u32[]{:S(2)}) collective-permute-start(f32[4,8,3712]{2,1,0:T(8,128)S(1)} %line.1.a_ref), channel_id=1, source_target_pairs={{0,24},{4,100},{8,0},{12,108},{16,8},{20,116},{24,16},{28,124},{32... | collective-permute-start | bytes 1425416 | tf_op jit(solution)/shard_map/ppermute | solution.py:445
  32.0 12.3 %collective-permute-start.7 = (f32[4,8,3712]{2,1,0:T(8,128)S(1)}, f32[4,8,3712]{2,1,0:T(8,128)S(1)}, u32[]{:S(2)}, u32[]{:S(2)}) collective-permute-start(f32[4,8,3712]{2,1,0:T(8,128)S(1)} %line.1.a_ref), channel_id=1, source_target_pairs={{0,8},{4,36},{8,16},{12,44},{16,24},{20,52},{24,0},{28,60},{32,40}... | collective-permute-start | bytes 1425416 | tf_op jit(solution)/shard_map/ppermute | solution.py:445
  38.0 6.8 %collective-permute-start.11 = (f32[4,8,3712]{2,1,0:T(8,128)S(1)}, f32[4,8,3712]{2,1,0:T(8,128)S(1)}, u32[]{:S(2)}, u32[]{:S(2)}) collective-permute-start(f32[4,8,3712]{2,1,0:T(8,128)S(1)} %collective-permute-done.9.c_ref), channel_id=1, source_target_pairs={{0,4},{4,0},{8,12},{12,8},{16,20},{20,16},{24,28},{28,24},{32,36},... | collective-permute-start | bytes 1425416 | tf_op jit(solution)/shard_map/ppermute | solution.py:449
  38.0 8.1 %collective-permute-start.6 = (f32[4,8,3712]{2,1,0:T(8,128)S(1)}, f32[4,8,3712]{2,1,0:T(8,128)S(1)}, u32[]{:S(2)}, u32[]{:S(2)}) collective-permute-start(f32[4,8,3712]{2,1,0:T(8,128)S(1)} %line.1.a_ref), channel_id=1, source_target_pairs={{0,4},{4,0},{8,12},{12,8},{16,20},{20,16},{24,28},{28,24},{32,36},... | collective-permute-start | bytes 1425416 | tf_op jit(solution)/shard_map/ppermute | solution.py:449
  44.3 1.8 %collective-permute-start.12 = (f32[4,8,3712]{2,1,0:T(8,128)S(1)}, f32[4,8,3712]{2,1,0:T(8,128)S(1)}, u32[]{:S(2)}, u32[]{:S(2)}) collective-permute-start(f32[4,8,3712]{2,1,0:T(8,128)S(1)} %collective-permute-done.10.d_ref), channel_id=1, source_target_pairs={{0,4},{4,0},{8,12},{12,8},{16,20},{20,16},{24,28},{28,24},{32,36},... | collective-permute-start | bytes 1425416 | tf_op jit(solution)/shard_map/ppermute | solution.py:449
  44.3 2.5 %collective-permute-start.8 = (f32[4,8,3712]{2,1,0:T(8,128)S(1)}, f32[4,8,3712]{2,1,0:T(8,128)S(1)}, u32[]{:S(2)}, u32[]{:S(2)}) collective-permute-start(f32[4,8,3712]{2,1,0:T(8,128)S(1)} %collective-permute-done.7.b_ref), channel_id=1, source_target_pairs={{0,4},{4,0},{8,12},{12,8},{16,20},{20,16},{24,28},{28,24},{32,36},... | collective-permute-start | bytes 1425416 | tf_op jit(solution)/shard_map/ppermute | solution.py:449
  49.7 2.6 %collective-permute-start.13 = (f32[64,3840]{1,0:T(8,128)S(1)}, f32[64,3840]{1,0:T(8,128)S(1)}, u32[]{:S(2)}, u32[]{:S(2)}) collective-permute-start(f32[64,3840]{1,0:T(8,128)S(1)} %get-tuple-element.74), channel_id=1, source_target_pairs={{0,4},{4,0},{8,12},{12,8},{16,20},{20,16},{24,28},{28,24},{32,36},... | collective-permute-start | bytes 2949128 | tf_op jit(solution)/shard_map/ppermute | solution.py:449
  52.6 7.9 %collective-permute-start.14 = (f32[4,8,1920]{2,1,0:T(8,128)S(1)}, f32[4,8,1920]{2,1,0:T(8,128)S(1)}, u32[]{:S(2)}, u32[]{:S(2)}) collective-permute-start(f32[4,8,1920]{2,1,0:T(8,128)S(1)} %get-tuple-element.76), channel_id=1, source_target_pairs={{0,64},{4,20},{8,72},{12,28},{16,80},{20,4},{24,88},{28,12},{32,96... | collective-permute-start | bytes 737288 | tf_op jit(solution)/shard_map/ppermute | solution.py:445
  53.2 9.7 %collective-permute-start.15 = (f32[4,8,1920]{2,1,0:T(8,128)S(1)}, f32[4,8,1920]{2,1,0:T(8,128)S(1)}, u32[]{:S(2)}, u32[]{:S(2)}) collective-permute-start(f32[4,8,1920]{2,1,0:T(8,128)S(1)} %get-tuple-element.77), channel_id=1, source_target_pairs={{0,32},{4,12},{8,40},{12,20},{16,48},{20,28},{24,56},{28,4},{32,64... | collective-permute-start | bytes 737288 | tf_op jit(solution)/shard_map/ppermute | solution.py:445
  54.1 8.9 %collective-permute-start.16 = (f32[4,8,1920]{2,1,0:T(8,128)S(1)}, f32[4,8,1920]{2,1,0:T(8,128)S(1)}, u32[]{:S(2)}, u32[]{:S(2)}) collective-permute-start(f32[4,8,1920]{2,1,0:T(8,128)S(1)} %get-tuple-element.78), channel_id=1, source_target_pairs={{0,96},{4,28},{8,104},{12,4},{16,112},{20,12},{24,120},{28,20},{32... | collective-permute-start | bytes 737288 | tf_op jit(solution)/shard_map/ppermute | solution.py:445
  63.1 5.8 %collective-permute-start.17 = (f32[8,1920]{1,0:T(8,128)S(1)}, f32[8,1920]{1,0:T(8,128)S(1)}, u32[]{:S(2)}, u32[]{:S(2)}) collective-permute-start(f32[8,1920]{1,0:T(8,128)S(1)} %get-tuple-element.80), channel_id=1, source_target_pairs={{0,16},{4,68},{8,24},{12,76},{16,0},{20,84},{24,8},{28,92},{32,48}... | collective-permute-start | bytes 184328 | tf_op jit(solution)/shard_map/ppermute | solution.py:445
  64.7 5.4 %collective-permute-start.18 = (f32[8,1920]{1,0:T(8,128)S(1)}, f32[8,1920]{1,0:T(8,128)S(1)}, u32[]{:S(2)}, u32[]{:S(2)}) collective-permute-start(f32[8,1920]{1,0:T(8,128)S(1)} %get-tuple-element.81), channel_id=1, source_target_pairs={{0,8},{4,36},{8,16},{12,44},{16,24},{20,52},{24,0},{28,60},{32,40}... | collective-permute-start | bytes 184328 | tf_op jit(solution)/shard_map/ppermute | solution.py:445
  66.6 4.2 %collective-permute-start.19 = (f32[8,1920]{1,0:T(8,128)S(1)}, f32[8,1920]{1,0:T(8,128)S(1)}, u32[]{:S(2)}, u32[]{:S(2)}) collective-permute-start(f32[8,1920]{1,0:T(8,128)S(1)} %get-tuple-element.82), channel_id=1, source_target_pairs={{0,24},{4,100},{8,0},{12,108},{16,8},{20,116},{24,16},{28,124},{32... | collective-permute-start | bytes 184328 | tf_op jit(solution)/shard_map/ppermute | solution.py:445
  70.9 5.9 %collective-permute-start.22 = (f32[8,1920]{1,0:T(8,128)S(1)}, f32[8,1920]{1,0:T(8,128)S(1)}, u32[]{:S(2)}, u32[]{:S(2)}) collective-permute-start(f32[8,1920]{1,0:T(8,128)S(1)} %plane_sum.1.a_ref), channel_id=1, source_target_pairs={{0,2},{1,3},{2,0},{3,1},{4,6},{5,7},{6,4},{7,5},{8,10},{9,11},{10,... | collective-permute-start | bytes 184328 | tf_op jit(solution)/shard_map/ppermute | solution.py:440
  71.3 6.0 %collective-permute-start.21 = (f32[8,1920]{1,0:T(8,128)S(1)}, f32[8,1920]{1,0:T(8,128)S(1)}, u32[]{:S(2)}, u32[]{:S(2)}) collective-permute-start(f32[8,1920]{1,0:T(8,128)S(1)} %plane_sum.1.a_ref), channel_id=1, source_target_pairs={{0,1},{1,2},{2,3},{3,0},{4,5},{5,6},{6,7},{7,4},{8,9},{9,10},{10,1... | collective-permute-start | bytes 184328 | tf_op jit(solution)/shard_map/ppermute | solution.py:440
  73.5 4.2 %collective-permute-start.20 = (f32[8,1920]{1,0:T(8,128)S(1)}, f32[8,1920]{1,0:T(8,128)S(1)}, u32[]{:S(2)}, u32[]{:S(2)}) collective-permute-start(f32[8,1920]{1,0:T(8,128)S(1)} %plane_sum.1.a_ref), channel_id=1, source_target_pairs={{0,3},{1,0},{2,1},{3,2},{4,7},{5,4},{6,5},{7,6},{8,11},{9,8},{10,9... | collective-permute-start | bytes 184328 | tf_op jit(solution)/shard_map/ppermute | solution.py:440
  (7 other events, 41.2 us)

commit v5 on v4

--- a/solution.py
+++ b/solution.py
@@ -82,9 +82,9 @@
     for copy in z_copies:
         copy.start()
     copies = []
-    for h in range(HEADS_LOCAL):
-        rows = pl.ds(h * HEAD_DIM, HEAD_DIM)
-        copies.append(pltpu.make_async_copy(w_ref.at[rows, :], w_s.at[rows, :], sems.at[h]))
+    for i in range(2):
+        rows = pl.ds(i * 2 * HEAD_DIM, 2 * HEAD_DIM)
+        copies.append(pltpu.make_async_copy(w_ref.at[rows, :], w_s.at[rows, :], sems.at[i]))
         copies[-1].start()
     first = (index % 4) * OWN
     row = lax.broadcasted_iota(jnp.int32, (16, 16), 0)
@@ -95,7 +95,8 @@
         copy.wait()
     z = (nn(pick_c, z_s[0]) + nn(pick_n, z_s[1])).astype(BF16)
     for h in range(HEADS_LOCAL):
-        copies[h].wait()
+        if h % 2 == 0:
+            copies[h // 2].wait()
         cols = slice(h * HEAD_DIM, (h + 1) * HEAD_DIM)
         out = nn(z[:, cols], w_s[cols, :])[: 2 * OWN]
         heads_ref[h] = out
@@ -115,7 +116,7 @@
             VMEM((2, 16, 1024), BF16),
             VMEM((1024, D), BF16),
             pltpu.SemaphoreType.DMA((2,)),
-            pltpu.SemaphoreType.DMA((HEADS_LOCAL,)),
+            pltpu.SemaphoreType.DMA((2,)),
         ],
         mib=12,
         flops=2 * 16 * 1024 * D,
@@ -187,7 +188,7 @@
 
 
 def line_kernel(a_ref, b_ref, c_ref, d_ref, out_ref):
-    for d, ref in zip((0, *(1,2,3)), (a_ref, b_ref, c_ref, d_ref)):
+    for d, ref in zip((0, *(3,2,1)), (a_ref, b_ref, c_ref, d_ref)):
         out_ref[d] = ref[...]
 
 
@@ -461,7 +462,7 @@
     *parts, resid = lax.optimization_barrier((*over_tp(part, (3,1,2)), resid))
     attn, msg = norm(parts, resid_corrupt, resid_clean, gain)
     gf = grad_f(cot, w_dec, active)
-    parts = [msg] + [send(msg, 0, d) for d in (1,2,3)]
+    parts = [msg] + [send(msg, 0, d) for d in (3,2,1)]
     *parts, gf = lax.optimization_barrier((*parts, gf))
     block = line(parts)
     flipped = flip(w_enc)

time: 78.9 us -> 77.7 us (0.985)
  waiting for transfers between devices: 26.1 us -> 22.9 us
  starting transfers between devices: 30.8 us -> 33 us
    ppermute x12, waiting for transfers between devices: 19.7 us -> 16.7 us  [send(): return lax.ppermute(x, 'lat', shift(stage, d))]
    ppermute x12, starting transfers between devices: 19.3 us -> 21.5 us  [send(): return lax.ppermute(x, 'lat', shift(stage, d))]
  transfers between devices with their start and end apart: 23 -> 23, of which waited for: 14 -> 12; matrix products, arithmetic and copies ran while one was open for 0% -> 0% of each run, Pallas kernels for 12% -> 12%
where the time goes in v5:
time: 77.7 us; the launch traced here: 77.5 us
  starting transfers between devices  33 us (42%)
  waiting for transfers between devices  22.9 us (29%)
  Pallas kernels  18.5 us (24%)
  local copies, waits for them, and re-layouts  2.39 us (3%)
  between operations  0.83 us (1%)
    ppermute x12, starting transfers between devices, send(): return lax.ppermute(x, 'lat', shift(stage, d))  21.5 us
    pallas_call x12, Pallas kernels, call(): pl.pallas_call(kernel, in_specs=[pl.BlockSpec(memory_space=s) for s in sp...  18.5 us
    ppermute x12, waiting for transfers between devices, send(): return lax.ppermute(x, 'lat', shift(stage, d))  16.7 us
    ppermute x6, starting transfers between devices, over_tp(): lax.ppermute(x, 'tp', [(i, (i + d) % 4) for i in range(4)])  10.2 us
    ppermute x5, waiting for transfers between devices, swap(): return lax.ppermute(x, 'lat', CORE_SWAP)  3.16 us
    ppermute x6, waiting for transfers between devices, over_tp(): lax.ppermute(x, 'tp', [(i, (i + d) % 4) for i in range(4)])  3.02 us
    unnamed x16, local copies, waits for them, and re-layouts  2.38 us
  transfers between devices with their start and end apart: 23, of which 12 were waited for; matrix products, arithmetic and copies ran while one was open for 0% of the time, Pallas kernels for 12%

profile of v5, /device:TPU:0, one launch (start us, length us, event | category | flops | bytes accessed | tf_op | source)
XLA Modules:
  0.0 77.5 jit_solution(12399207711764938832)
XLA Ops:
  0.7 4.4 %project.1 = (f32[4,8,3584]{2,1,0:T(8,128)S(1)}, f32[8,3584]{1,0:T(8,128)S(1)}) custom-call(bf16[128,1024]{1,0:T(8,128)(2,1)} %zc_ref.1, bf16[128,1024]{1,0:T(8,128)(2,1)} %zn_ref.1, bf16[1024,3584]{1,0:T(8,128)(2,1)} %w_ref.1), custom_call_target="tpu_custom_call" | custom-call | flops 117440512 | bytes 7864320 | tf_op jit(solution)/shard_map/project/pallas_call | solution.py:55
  5.1 3.4 %collective-permute-start.2 = (f32[8,3584]{1,0:T(8,128)S(1)}, f32[8,3584]{1,0:T(8,128)S(1)}, u32[]{:S(2)}, u32[]{:S(2)}) collective-permute-start(f32[8,3584]{1,0:T(8,128)S(1)} %get-tuple-element.49.a_ref), channel_id=1, source_target_pairs={{0,2},{1,3},{2,0},{3,1},{4,6},{5,7},{6,4},{7,5},{8,10},{9,11},{10,... | collective-permute-start | bytes 344072 | tf_op jit(solution)/shard_map/ppermute | solution.py:441
  9.1 2.6 %collective-permute-start = (f32[8,3584]{1,0:T(8,128)S(1)}, f32[8,3584]{1,0:T(8,128)S(1)}, u32[]{:S(2)}, u32[]{:S(2)}) collective-permute-start(f32[8,3584]{1,0:T(8,128)S(1)} %get-tuple-element.49.a_ref), channel_id=1, source_target_pairs={{0,3},{1,0},{2,1},{3,2},{4,7},{5,4},{6,5},{7,6},{8,11},{9,8},{10,9... | collective-permute-start | bytes 344072 | tf_op jit(solution)/shard_map/ppermute | solution.py:441
  14.1 2.1 %resid_project.1.resid_ref = f32[2,128,1024]{2,1,0:T(8,128)S(1)} custom-call(bf16[128,3584]{1,0:T(8,128)(2,1)S(1)} %copy-done.1, bf16[128,3584]{1,0:T(8,128)(2,1)S(1)} %copy-done.3, bf16[3584,1024]{1,0:T(8,128)(2,1)S(1)} %copy-done), custom_call_target="tpu_custom_call" | custom-call | flops 1879048192 | bytes 9175040 | tf_op jit(solution)/shard_map/resid_project/pallas_call | solution.py:55
  16.6 1.6 %collective-permute-start.5 = (f32[8,3712]{1,0:T(8,128)S(1)}, f32[8,3712]{1,0:T(8,128)S(1)}, u32[]{:S(2)}, u32[]{:S(2)}) collective-permute-start(f32[8,3712]{1,0:T(8,128)S(1)} %get-tuple-element.58.a_ref), channel_id=1, source_target_pairs={{0,32},{4,12},{8,40},{12,20},{16,48},{20,28},{24,56},{28,4},{32,64... | collective-permute-start | bytes 356360 | tf_op jit(solution)/shard_map/ppermute | solution.py:446
  18.1 2.7 %collective-permute-start.4 = (f32[8,3712]{1,0:T(8,128)S(1)}, f32[8,3712]{1,0:T(8,128)S(1)}, u32[]{:S(2)}, u32[]{:S(2)}) collective-permute-start(f32[8,3712]{1,0:T(8,128)S(1)} %get-tuple-element.58.a_ref), channel_id=1, source_target_pairs={{0,64},{4,20},{8,72},{12,28},{16,80},{20,4},{24,88},{28,12},{32,96... | collective-permute-start | bytes 356360 | tf_op jit(solution)/shard_map/ppermute | solution.py:446
  20.9 1.4 %collective-permute-start.3 = (f32[8,3712]{1,0:T(8,128)S(1)}, f32[8,3712]{1,0:T(8,128)S(1)}, u32[]{:S(2)}, u32[]{:S(2)}) collective-permute-start(f32[8,3712]{1,0:T(8,128)S(1)} %get-tuple-element.58.a_ref), channel_id=1, source_target_pairs={{0,96},{4,28},{8,104},{12,4},{16,112},{20,12},{24,120},{28,20},{32... | collective-permute-start | bytes 356360 | tf_op jit(solution)/shard_map/ppermute | solution.py:446
  22.3 4.1 %grad_f.1.gf_ref = f32[4,128,1024]{2,1,0:T(8,128)S(1)} custom-call(bf16[128,4,3584]{2,1,0:T(4,128)(2,1)S(1)} %copy-done.5, bf16[1024,3584]{1,0:T(8,128)(2,1)S(1)} %copy-done.4, s32[128,1024]{1,0:T(8,128)S(1)} %copy-done.6), custom_call_target="tpu_custom_call" | custom-call | flops 3758096384 | bytes 11534336 | tf_op jit(solution)/shard_map/grad_f/pallas_call | solution.py:55
  26.5 4.0 %collective-permute-start.9 = (f32[4,8,3712]{2,1,0:T(8,128)S(1)}, f32[4,8,3712]{2,1,0:T(8,128)S(1)}, u32[]{:S(2)}, u32[]{:S(2)}) collective-permute-start(f32[4,8,3712]{2,1,0:T(8,128)S(1)} %line.1.a_ref), channel_id=1, source_target_pairs={{0,16},{4,68},{8,24},{12,76},{16,0},{20,84},{24,8},{28,92},{32,48}... | collective-permute-start | bytes 1425416 | tf_op jit(solution)/shard_map/ppermute | solution.py:446
  32.5 1.9 %flip.1.flip_ref = bf16[1024,3584]{1,0:T(8,128)(2,1)S(1)} custom-call(bf16[3584,1024]{1,0:T(8,128)(2,1)S(1)} %copy-done), custom_call_target="tpu_custom_call" | custom-call | flops 1000000 | bytes 7340032 | tf_op jit(solution)/shard_map/flip/pallas_call | solution.py:55
  34.5 2.8 %collective-permute-done.9.c_ref = f32[4,8,3712]{2,1,0:T(8,128)S(1)} collective-permute-done((f32[4,8,3712]{2,1,0:T(8,128)S(1)}, f32[4,8,3712]{2,1,0:T(8,128)S(1)}, u32[]{:S(2)}, u32[]{:S(2)}) %collective-permute-start.9) | collective-permute-done | bytes 475168 | tf_op jit(solution)/shard_map/ppermute | solution.py:446
  37.7 5.5 %collective-permute-done.10.d_ref = f32[4,8,3712]{2,1,0:T(8,128)S(1)} collective-permute-done((f32[4,8,3712]{2,1,0:T(8,128)S(1)}, f32[4,8,3712]{2,1,0:T(8,128)S(1)}, u32[]{:S(2)}, u32[]{:S(2)}) %collective-permute-start.10) | collective-permute-done | bytes 475168 | tf_op jit(solution)/shard_map/ppermute | solution.py:446
  45.8 2.9 %latents.1 = (f32[128,1024]{1,0:T(8,128)S(1)}, f32[64,3840]{1,0:T(8,128)S(1)}, f32[64,3840]{1,0:T(8,128)S(1)}) custom-call(f32[4,8,3712]{2,1,0:T(8,128)S(1)} %collective-permute-done.6.a_ref, f32[4,8,3712]{2,1,0:T(8,128)S(1)} %collective-permute-done.8.b_ref, f32[4,8,3712]{2,1,0:T(8,128)S(1)} %collective-permute-done.11.c_ref, ...), custom_call_target="tpu_custom_call" | custom-call | flops 1879048192 | bytes 20316160 | tf_op jit(solution)/shard_map/latents/pallas_call | solution.py:55
  48.9 2.4 %collective-permute-done.13.b_ref = f32[64,3840]{1,0:T(8,128)S(1)} collective-permute-done((f32[64,3840]{1,0:T(8,128)S(1)}, f32[64,3840]{1,0:T(8,128)S(1)}, u32[]{:S(2)}, u32[]{:S(2)}) %collective-permute-start.13) | collective-permute-done | bytes 983072 | tf_op jit(solution)/shard_map/ppermute | solution.py:450
  51.6 1.5 %collective-permute-start.14 = (f32[4,8,1920]{2,1,0:T(8,128)S(1)}, f32[4,8,1920]{2,1,0:T(8,128)S(1)}, u32[]{:S(2)}, u32[]{:S(2)}) collective-permute-start(f32[4,8,1920]{2,1,0:T(8,128)S(1)} %get-tuple-element.76), channel_id=1, source_target_pairs={{0,64},{4,20},{8,72},{12,28},{16,80},{20,4},{24,88},{28,12},{32,96... | collective-permute-start | bytes 737288 | tf_op jit(solution)/shard_map/ppermute | solution.py:446
  54.3 1.9 %collective-permute-start.16 = (f32[4,8,1920]{2,1,0:T(8,128)S(1)}, f32[4,8,1920]{2,1,0:T(8,128)S(1)}, u32[]{:S(2)}, u32[]{:S(2)}) collective-permute-start(f32[4,8,1920]{2,1,0:T(8,128)S(1)} %get-tuple-element.78), channel_id=1, source_target_pairs={{0,96},{4,28},{8,104},{12,4},{16,112},{20,12},{24,120},{28,20},{32... | collective-permute-start | bytes 737288 | tf_op jit(solution)/shard_map/ppermute | solution.py:446
  56.3 3.2 %collective-permute-done.14.b_ref = f32[4,8,1920]{2,1,0:T(8,128)S(1)} collective-permute-done((f32[4,8,1920]{2,1,0:T(8,128)S(1)}, f32[4,8,1920]{2,1,0:T(8,128)S(1)}, u32[]{:S(2)}, u32[]{:S(2)}) %collective-permute-start.14) | collective-permute-done | bytes 245792 | tf_op jit(solution)/shard_map/ppermute | solution.py:446
  59.4 2.5 %collective-permute-done.15.c_ref = f32[4,8,1920]{2,1,0:T(8,128)S(1)} collective-permute-done((f32[4,8,1920]{2,1,0:T(8,128)S(1)}, f32[4,8,1920]{2,1,0:T(8,128)S(1)}, u32[]{:S(2)}, u32[]{:S(2)}) %collective-permute-start.15) | collective-permute-done | bytes 245792 | tf_op jit(solution)/shard_map/ppermute | solution.py:446
  62.1 1.9 %collective-permute-start.17 = (f32[8,1920]{1,0:T(8,128)S(1)}, f32[8,1920]{1,0:T(8,128)S(1)}, u32[]{:S(2)}, u32[]{:S(2)}) collective-permute-start(f32[8,1920]{1,0:T(8,128)S(1)} %get-tuple-element.80), channel_id=1, source_target_pairs={{0,16},{4,68},{8,24},{12,76},{16,0},{20,84},{24,8},{28,92},{32,48}... | collective-permute-start | bytes 184328 | tf_op jit(solution)/shard_map/ppermute | solution.py:446
  63.9 1.7 %collective-permute-start.18 = (f32[8,1920]{1,0:T(8,128)S(1)}, f32[8,1920]{1,0:T(8,128)S(1)}, u32[]{:S(2)}, u32[]{:S(2)}) collective-permute-start(f32[8,1920]{1,0:T(8,128)S(1)} %get-tuple-element.81), channel_id=1, source_target_pairs={{0,8},{4,36},{8,16},{12,44},{16,24},{20,52},{24,0},{28,60},{32,40}... | collective-permute-start | bytes 184328 | tf_op jit(solution)/shard_map/ppermute | solution.py:446
  65.6 1.5 %collective-permute-start.19 = (f32[8,1920]{1,0:T(8,128)S(1)}, f32[8,1920]{1,0:T(8,128)S(1)}, u32[]{:S(2)}, u32[]{:S(2)}) collective-permute-start(f32[8,1920]{1,0:T(8,128)S(1)} %get-tuple-element.82), channel_id=1, source_target_pairs={{0,24},{4,100},{8,0},{12,108},{16,8},{20,116},{24,16},{28,124},{32... | collective-permute-start | bytes 184328 | tf_op jit(solution)/shard_map/ppermute | solution.py:446
  67.9 1.5 %collective-permute-done.18.c_ref = f32[8,1920]{1,0:T(8,128)S(1)} collective-permute-done((f32[8,1920]{1,0:T(8,128)S(1)}, f32[8,1920]{1,0:T(8,128)S(1)}, u32[]{:S(2)}, u32[]{:S(2)}) %collective-permute-start.18) | collective-permute-done | bytes 61472 | tf_op jit(solution)/shard_map/ppermute | solution.py:446
  70.3 2.0 %collective-permute-start.21 = (f32[8,1920]{1,0:T(8,128)S(1)}, f32[8,1920]{1,0:T(8,128)S(1)}, u32[]{:S(2)}, u32[]{:S(2)}) collective-permute-start(f32[8,1920]{1,0:T(8,128)S(1)} %plane_sum.1.a_ref), channel_id=1, source_target_pairs={{0,1},{1,2},{2,3},{3,0},{4,5},{5,6},{6,7},{7,4},{8,9},{9,10},{10,1... | collective-permute-start | bytes 184328 | tf_op jit(solution)/shard_map/ppermute | solution.py:441
  73.5 2.2 %collective-permute-done.22.d_ref = f32[8,1920]{1,0:T(8,128)S(1)} collective-permute-done((f32[8,1920]{1,0:T(8,128)S(1)}, f32[8,1920]{1,0:T(8,128)S(1)}, u32[]{:S(2)}, u32[]{:S(2)}) %collective-permute-start.22) | collective-permute-done | bytes 61472 | tf_op jit(solution)/shard_map/ppermute | solution.py:441
  (51 shorter events, 14.9 us)
Async XLA Ops:
  0.7 21.6 %copy-start.6 = (s32[128,1024]{1,0:T(8,128)S(1)}, s32[128,1024]{1,0:T(8,128)}, u32[]{:S(2)}) copy-start(s32[128,1024]{1,0:T(8,128)} %active_ref) | copy-start | bytes 1572868
  5.1 11.1 %collective-permute-start.2 = (f32[8,3584]{1,0:T(8,128)S(1)}, f32[8,3584]{1,0:T(8,128)S(1)}, u32[]{:S(2)}, u32[]{:S(2)}) collective-permute-start(f32[8,3584]{1,0:T(8,128)S(1)} %get-tuple-element.49.a_ref), channel_id=1, source_target_pairs={{0,2},{1,3},{2,0},{3,1},{4,6},{5,7},{6,4},{7,5},{8,10},{9,11},{10,... | collective-permute-start | bytes 344072 | tf_op jit(solution)/shard_map/ppermute | solution.py:441
  8.5 7.7 %collective-permute-start.1 = (f32[8,3584]{1,0:T(8,128)S(1)}, f32[8,3584]{1,0:T(8,128)S(1)}, u32[]{:S(2)}, u32[]{:S(2)}) collective-permute-start(f32[8,3584]{1,0:T(8,128)S(1)} %get-tuple-element.49.a_ref), channel_id=1, source_target_pairs={{0,1},{1,2},{2,3},{3,0},{4,5},{5,6},{6,7},{7,4},{8,9},{9,10},{10,1... | collective-permute-start | bytes 344072 | tf_op jit(solution)/shard_map/ppermute | solution.py:441
  9.1 7.0 %collective-permute-start = (f32[8,3584]{1,0:T(8,128)S(1)}, f32[8,3584]{1,0:T(8,128)S(1)}, u32[]{:S(2)}, u32[]{:S(2)}) collective-permute-start(f32[8,3584]{1,0:T(8,128)S(1)} %get-tuple-element.49.a_ref), channel_id=1, source_target_pairs={{0,3},{1,0},{2,1},{3,2},{4,7},{5,4},{6,5},{7,6},{8,11},{9,8},{10,9... | collective-permute-start | bytes 344072 | tf_op jit(solution)/shard_map/ppermute | solution.py:441
  16.6 9.9 %collective-permute-start.5 = (f32[8,3712]{1,0:T(8,128)S(1)}, f32[8,3712]{1,0:T(8,128)S(1)}, u32[]{:S(2)}, u32[]{:S(2)}) collective-permute-start(f32[8,3712]{1,0:T(8,128)S(1)} %get-tuple-element.58.a_ref), channel_id=1, source_target_pairs={{0,32},{4,12},{8,40},{12,20},{16,48},{20,28},{24,56},{28,4},{32,64... | collective-permute-start | bytes 356360 | tf_op jit(solution)/shard_map/ppermute | solution.py:446
  18.1 8.3 %collective-permute-start.4 = (f32[8,3712]{1,0:T(8,128)S(1)}, f32[8,3712]{1,0:T(8,128)S(1)}, u32[]{:S(2)}, u32[]{:S(2)}) collective-permute-start(f32[8,3712]{1,0:T(8,128)S(1)} %get-tuple-element.58.a_ref), channel_id=1, source_target_pairs={{0,64},{4,20},{8,72},{12,28},{16,80},{20,4},{24,88},{28,12},{32,96... | collective-permute-start | bytes 356360 | tf_op jit(solution)/shard_map/ppermute | solution.py:446
  20.9 5.6 %collective-permute-start.3 = (f32[8,3712]{1,0:T(8,128)S(1)}, f32[8,3712]{1,0:T(8,128)S(1)}, u32[]{:S(2)}, u32[]{:S(2)}) collective-permute-start(f32[8,3712]{1,0:T(8,128)S(1)} %get-tuple-element.58.a_ref), channel_id=1, source_target_pairs={{0,96},{4,28},{8,104},{12,4},{16,112},{20,12},{24,120},{28,20},{32... | collective-permute-start | bytes 356360 | tf_op jit(solution)/shard_map/ppermute | solution.py:446
  26.5 10.7 %collective-permute-start.9 = (f32[4,8,3712]{2,1,0:T(8,128)S(1)}, f32[4,8,3712]{2,1,0:T(8,128)S(1)}, u32[]{:S(2)}, u32[]{:S(2)}) collective-permute-start(f32[4,8,3712]{2,1,0:T(8,128)S(1)} %line.1.a_ref), channel_id=1, source_target_pairs={{0,16},{4,68},{8,24},{12,76},{16,0},{20,84},{24,8},{28,92},{32,48}... | collective-permute-start | bytes 1425416 | tf_op jit(solution)/shard_map/ppermute | solution.py:446
  30.5 12.8 %collective-permute-start.10 = (f32[4,8,3712]{2,1,0:T(8,128)S(1)}, f32[4,8,3712]{2,1,0:T(8,128)S(1)}, u32[]{:S(2)}, u32[]{:S(2)}) collective-permute-start(f32[4,8,3712]{2,1,0:T(8,128)S(1)} %line.1.a_ref), channel_id=1, source_target_pairs={{0,24},{4,100},{8,0},{12,108},{16,8},{20,116},{24,16},{28,124},{32... | collective-permute-start | bytes 1425416 | tf_op jit(solution)/shard_map/ppermute | solution.py:446
  31.2 12.1 %collective-permute-start.7 = (f32[4,8,3712]{2,1,0:T(8,128)S(1)}, f32[4,8,3712]{2,1,0:T(8,128)S(1)}, u32[]{:S(2)}, u32[]{:S(2)}) collective-permute-start(f32[4,8,3712]{2,1,0:T(8,128)S(1)} %line.1.a_ref), channel_id=1, source_target_pairs={{0,8},{4,36},{8,16},{12,44},{16,24},{20,52},{24,0},{28,60},{32,40}... | collective-permute-start | bytes 1425416 | tf_op jit(solution)/shard_map/ppermute | solution.py:446
  37.2 6.6 %collective-permute-start.11 = (f32[4,8,3712]{2,1,0:T(8,128)S(1)}, f32[4,8,3712]{2,1,0:T(8,128)S(1)}, u32[]{:S(2)}, u32[]{:S(2)}) collective-permute-start(f32[4,8,3712]{2,1,0:T(8,128)S(1)} %collective-permute-done.9.c_ref), channel_id=1, source_target_pairs={{0,4},{4,0},{8,12},{12,8},{16,20},{20,16},{24,28},{28,24},{32,36},... | collective-permute-start | bytes 1425416 | tf_op jit(solution)/shard_map/ppermute | solution.py:450
  37.2 7.8 %collective-permute-start.6 = (f32[4,8,3712]{2,1,0:T(8,128)S(1)}, f32[4,8,3712]{2,1,0:T(8,128)S(1)}, u32[]{:S(2)}, u32[]{:S(2)}) collective-permute-start(f32[4,8,3712]{2,1,0:T(8,128)S(1)} %line.1.a_ref), channel_id=1, source_target_pairs={{0,4},{4,0},{8,12},{12,8},{16,20},{20,16},{24,28},{28,24},{32,36},... | collective-permute-start | bytes 1425416 | tf_op jit(solution)/shard_map/ppermute | solution.py:450
  43.3 1.8 %collective-permute-start.12 = (f32[4,8,3712]{2,1,0:T(8,128)S(1)}, f32[4,8,3712]{2,1,0:T(8,128)S(1)}, u32[]{:S(2)}, u32[]{:S(2)}) collective-permute-start(f32[4,8,3712]{2,1,0:T(8,128)S(1)} %collective-permute-done.10.d_ref), channel_id=1, source_target_pairs={{0,4},{4,0},{8,12},{12,8},{16,20},{20,16},{24,28},{28,24},{32,36},... | collective-permute-start | bytes 1425416 | tf_op jit(solution)/shard_map/ppermute | solution.py:450
  43.3 2.5 %collective-permute-start.8 = (f32[4,8,3712]{2,1,0:T(8,128)S(1)}, f32[4,8,3712]{2,1,0:T(8,128)S(1)}, u32[]{:S(2)}, u32[]{:S(2)}) collective-permute-start(f32[4,8,3712]{2,1,0:T(8,128)S(1)} %collective-permute-done.7.b_ref), channel_id=1, source_target_pairs={{0,4},{4,0},{8,12},{12,8},{16,20},{20,16},{24,28},{28,24},{32,36},... | collective-permute-start | bytes 1425416 | tf_op jit(solution)/shard_map/ppermute | solution.py:450
  48.7 2.6 %collective-permute-start.13 = (f32[64,3840]{1,0:T(8,128)S(1)}, f32[64,3840]{1,0:T(8,128)S(1)}, u32[]{:S(2)}, u32[]{:S(2)}) collective-permute-start(f32[64,3840]{1,0:T(8,128)S(1)} %get-tuple-element.74), channel_id=1, source_target_pairs={{0,4},{4,0},{8,12},{12,8},{16,20},{20,16},{24,28},{28,24},{32,36},... | collective-permute-start | bytes 2949128 | tf_op jit(solution)/shard_map/ppermute | solution.py:450
  51.6 7.9 %collective-permute-start.14 = (f32[4,8,1920]{2,1,0:T(8,128)S(1)}, f32[4,8,1920]{2,1,0:T(8,128)S(1)}, u32[]{:S(2)}, u32[]{:S(2)}) collective-permute-start(f32[4,8,1920]{2,1,0:T(8,128)S(1)} %get-tuple-element.76), channel_id=1, source_target_pairs={{0,64},{4,20},{8,72},{12,28},{16,80},{20,4},{24,88},{28,12},{32,96... | collective-permute-start | bytes 737288 | tf_op jit(solution)/shard_map/ppermute | solution.py:446
  53.0 8.9 %collective-permute-start.15 = (f32[4,8,1920]{2,1,0:T(8,128)S(1)}, f32[4,8,1920]{2,1,0:T(8,128)S(1)}, u32[]{:S(2)}, u32[]{:S(2)}) collective-permute-start(f32[4,8,1920]{2,1,0:T(8,128)S(1)} %get-tuple-element.77), channel_id=1, source_target_pairs={{0,32},{4,12},{8,40},{12,20},{16,48},{20,28},{24,56},{28,4},{32,64... | collective-permute-start | bytes 737288 | tf_op jit(solution)/shard_map/ppermute | solution.py:446
  54.3 7.6 %collective-permute-start.16 = (f32[4,8,1920]{2,1,0:T(8,128)S(1)}, f32[4,8,1920]{2,1,0:T(8,128)S(1)}, u32[]{:S(2)}, u32[]{:S(2)}) collective-permute-start(f32[4,8,1920]{2,1,0:T(8,128)S(1)} %get-tuple-element.78), channel_id=1, source_target_pairs={{0,96},{4,28},{8,104},{12,4},{16,112},{20,12},{24,120},{28,20},{32... | collective-permute-start | bytes 737288 | tf_op jit(solution)/shard_map/ppermute | solution.py:446
  62.1 5.8 %collective-permute-start.17 = (f32[8,1920]{1,0:T(8,128)S(1)}, f32[8,1920]{1,0:T(8,128)S(1)}, u32[]{:S(2)}, u32[]{:S(2)}) collective-permute-start(f32[8,1920]{1,0:T(8,128)S(1)} %get-tuple-element.80), channel_id=1, source_target_pairs={{0,16},{4,68},{8,24},{12,76},{16,0},{20,84},{24,8},{28,92},{32,48}... | collective-permute-start | bytes 184328 | tf_op jit(solution)/shard_map/ppermute | solution.py:446
  63.9 5.4 %collective-permute-start.18 = (f32[8,1920]{1,0:T(8,128)S(1)}, f32[8,1920]{1,0:T(8,128)S(1)}, u32[]{:S(2)}, u32[]{:S(2)}) collective-permute-start(f32[8,1920]{1,0:T(8,128)S(1)} %get-tuple-element.81), channel_id=1, source_target_pairs={{0,8},{4,36},{8,16},{12,44},{16,24},{20,52},{24,0},{28,60},{32,40}... | collective-permute-start | bytes 184328 | tf_op jit(solution)/shard_map/ppermute | solution.py:446
  65.6 4.2 %collective-permute-start.19 = (f32[8,1920]{1,0:T(8,128)S(1)}, f32[8,1920]{1,0:T(8,128)S(1)}, u32[]{:S(2)}, u32[]{:S(2)}) collective-permute-start(f32[8,1920]{1,0:T(8,128)S(1)} %get-tuple-element.82), channel_id=1, source_target_pairs={{0,24},{4,100},{8,0},{12,108},{16,8},{20,116},{24,16},{28,124},{32... | collective-permute-start | bytes 184328 | tf_op jit(solution)/shard_map/ppermute | solution.py:446
  69.9 5.9 %collective-permute-start.22 = (f32[8,1920]{1,0:T(8,128)S(1)}, f32[8,1920]{1,0:T(8,128)S(1)}, u32[]{:S(2)}, u32[]{:S(2)}) collective-permute-start(f32[8,1920]{1,0:T(8,128)S(1)} %plane_sum.1.a_ref), channel_id=1, source_target_pairs={{0,2},{1,3},{2,0},{3,1},{4,6},{5,7},{6,4},{7,5},{8,10},{9,11},{10,... | collective-permute-start | bytes 184328 | tf_op jit(solution)/shard_map/ppermute | solution.py:441
  70.3 6.1 %collective-permute-start.21 = (f32[8,1920]{1,0:T(8,128)S(1)}, f32[8,1920]{1,0:T(8,128)S(1)}, u32[]{:S(2)}, u32[]{:S(2)}) collective-permute-start(f32[8,1920]{1,0:T(8,128)S(1)} %plane_sum.1.a_ref), channel_id=1, source_target_pairs={{0,1},{1,2},{2,3},{3,0},{4,5},{5,6},{6,7},{7,4},{8,9},{9,10},{10,1... | collective-permute-start | bytes 184328 | tf_op jit(solution)/shard_map/ppermute | solution.py:441
  72.3 4.2 %collective-permute-start.20 = (f32[8,1920]{1,0:T(8,128)S(1)}, f32[8,1920]{1,0:T(8,128)S(1)}, u32[]{:S(2)}, u32[]{:S(2)}) collective-permute-start(f32[8,1920]{1,0:T(8,128)S(1)} %plane_sum.1.a_ref), channel_id=1, source_target_pairs={{0,3},{1,0},{2,1},{3,2},{4,7},{5,4},{6,5},{7,6},{8,11},{9,8},{10,9... | collective-permute-start | bytes 184328 | tf_op jit(solution)/shard_map/ppermute | solution.py:441
  (7 other events, 43.0 us)

commit v6 on v5

--- a/solution.py
+++ b/solution.py
@@ -467,9 +467,10 @@
     block = line(parts)
     flipped = flip(w_enc)
     blocks = [block] + [send(block, 1, e) for e in (1, 2, 3)]
-    blocks[2], flipped = lax.optimization_barrier((blocks[2], flipped))
-    others = [swap(b) for b in blocks]
-    *blocks, others[2] = lax.optimization_barrier((*blocks, others[2]))
+    first = swap(block)
+    blocks[1], flipped, first = lax.optimization_barrier((blocks[1], flipped, first))
+    others = [first] + [swap(b) for b in blocks[1:]]
+    *blocks, others[1] = lax.optimization_barrier((*blocks, others[1]))
     pre_own, side = own_project(blocks, w_enc)
     raw, keep, give = latents(others, side, pre_own, resid, gf, w_enc, flipped)
     parts = pair_sum(keep, swap(give))

time: 77.7 us -> 77.6 us (level)
  starting transfers between devices: 33 us -> 32 us
  waiting for transfers between devices: 22.9 us -> 23.7 us
    ppermute x12, waiting for transfers between devices: 16.7 us -> 17.7 us  [send(): return lax.ppermute(x, 'lat', shift(stage, d))]
    ppermute x5, starting transfers between devices: 1.23 us -> 0.3 us  [swap(): return lax.ppermute(x, 'lat', CORE_SWAP)]
  transfers between devices with their start and end apart: 23 -> 23, of which waited for: 12 -> 13; matrix products, arithmetic and copies ran while one was open for 0% -> 0% of each run, Pallas kernels for 12% -> 12%
where the time goes in v6:
time: 77.6 us; the launch traced here: 77.4 us
  starting transfers between devices  32 us (41%)
  waiting for transfers between devices  23.7 us (31%)
  Pallas kernels  18.4 us (24%)
  local copies, waits for them, and re-layouts  2.39 us (3%)
  between operations  0.84 us (1%)
    ppermute x12, starting transfers between devices, send(): return lax.ppermute(x, 'lat', shift(stage, d))  21.5 us
    pallas_call x12, Pallas kernels, call(): pl.pallas_call(kernel, in_specs=[pl.BlockSpec(memory_space=s) for s in sp...  18.4 us
    ppermute x12, waiting for transfers between devices, send(): return lax.ppermute(x, 'lat', shift(stage, d))  17.7 us
    ppermute x6, starting transfers between devices, over_tp(): lax.ppermute(x, 'tp', [(i, (i + d) % 4) for i in range(4)])  10.2 us
    ppermute x6, waiting for transfers between devices, over_tp(): lax.ppermute(x, 'tp', [(i, (i + d) % 4) for i in range(4)])  3.02 us
    ppermute x5, waiting for transfers between devices, swap(): return lax.ppermute(x, 'lat', CORE_SWAP)  3.01 us
    unnamed x16, local copies, waits for them, and re-layouts  2.38 us
  transfers between devices with their start and end apart: 23, of which 13 were waited for; matrix products, arithmetic and copies ran while one was open for 0% of the time, Pallas kernels for 12%

profile of v6, /device:TPU:0, one launch (start us, length us, event | category | flops | bytes accessed | tf_op | source)
XLA Modules:
  0.0 77.4 jit_solution(6822491854019885129)
XLA Ops:
  0.7 4.4 %project.1 = (f32[4,8,3584]{2,1,0:T(8,128)S(1)}, f32[8,3584]{1,0:T(8,128)S(1)}) custom-call(bf16[128,1024]{1,0:T(8,128)(2,1)} %zc_ref.1, bf16[128,1024]{1,0:T(8,128)(2,1)} %zn_ref.1, bf16[1024,3584]{1,0:T(8,128)(2,1)} %w_ref.1), custom_call_target="tpu_custom_call" | custom-call | flops 117440512 | bytes 7864320 | tf_op jit(solution)/shard_map/project/pallas_call | solution.py:55
  5.1 3.4 %collective-permute-start.2 = (f32[8,3584]{1,0:T(8,128)S(1)}, f32[8,3584]{1,0:T(8,128)S(1)}, u32[]{:S(2)}, u32[]{:S(2)}) collective-permute-start(f32[8,3584]{1,0:T(8,128)S(1)} %get-tuple-element.50.a_ref), channel_id=1, source_target_pairs={{0,2},{1,3},{2,0},{3,1},{4,6},{5,7},{6,4},{7,5},{8,10},{9,11},{10,... | collective-permute-start | bytes 344072 | tf_op jit(solution)/shard_map/ppermute | solution.py:441
  9.1 2.6 %collective-permute-start = (f32[8,3584]{1,0:T(8,128)S(1)}, f32[8,3584]{1,0:T(8,128)S(1)}, u32[]{:S(2)}, u32[]{:S(2)}) collective-permute-start(f32[8,3584]{1,0:T(8,128)S(1)} %get-tuple-element.50.a_ref), channel_id=1, source_target_pairs={{0,3},{1,0},{2,1},{3,2},{4,7},{5,4},{6,5},{7,6},{8,11},{9,8},{10,9... | collective-permute-start | bytes 344072 | tf_op jit(solution)/shard_map/ppermute | solution.py:441
  14.1 2.1 %resid_project.1.resid_ref = f32[2,128,1024]{2,1,0:T(8,128)S(1)} custom-call(bf16[128,3584]{1,0:T(8,128)(2,1)S(1)} %copy-done.1, bf16[128,3584]{1,0:T(8,128)(2,1)S(1)} %copy-done.3, bf16[3584,1024]{1,0:T(8,128)(2,1)S(1)} %copy-done), custom_call_target="tpu_custom_call" | custom-call | flops 1879048192 | bytes 9175040 | tf_op jit(solution)/shard_map/resid_project/pallas_call | solution.py:55
  16.6 1.6 %collective-permute-start.5 = (f32[8,3712]{1,0:T(8,128)S(1)}, f32[8,3712]{1,0:T(8,128)S(1)}, u32[]{:S(2)}, u32[]{:S(2)}) collective-permute-start(f32[8,3712]{1,0:T(8,128)S(1)} %get-tuple-element.59.a_ref), channel_id=1, source_target_pairs={{0,32},{4,12},{8,40},{12,20},{16,48},{20,28},{24,56},{28,4},{32,64... | collective-permute-start | bytes 356360 | tf_op jit(solution)/shard_map/ppermute | solution.py:446
  18.1 2.7 %collective-permute-start.4 = (f32[8,3712]{1,0:T(8,128)S(1)}, f32[8,3712]{1,0:T(8,128)S(1)}, u32[]{:S(2)}, u32[]{:S(2)}) collective-permute-start(f32[8,3712]{1,0:T(8,128)S(1)} %get-tuple-element.59.a_ref), channel_id=1, source_target_pairs={{0,64},{4,20},{8,72},{12,28},{16,80},{20,4},{24,88},{28,12},{32,96... | collective-permute-start | bytes 356360 | tf_op jit(solution)/shard_map/ppermute | solution.py:446
  22.3 4.1 %grad_f.1.gf_ref = f32[4,128,1024]{2,1,0:T(8,128)S(1)} custom-call(bf16[128,4,3584]{2,1,0:T(4,128)(2,1)S(1)} %copy-done.5, bf16[1024,3584]{1,0:T(8,128)(2,1)S(1)} %copy-done.4, s32[128,1024]{1,0:T(8,128)S(1)} %copy-done.6), custom_call_target="tpu_custom_call" | custom-call | flops 3758096384 | bytes 11534336 | tf_op jit(solution)/shard_map/grad_f/pallas_call | solution.py:55
  26.6 2.0 %collective-permute-start.6 = (f32[4,8,3712]{2,1,0:T(8,128)S(1)}, f32[4,8,3712]{2,1,0:T(8,128)S(1)}, u32[]{:S(2)}, u32[]{:S(2)}) collective-permute-start(f32[4,8,3712]{2,1,0:T(8,128)S(1)} %line.1.a_ref), channel_id=1, source_target_pairs={{0,8},{4,36},{8,16},{12,44},{16,24},{20,52},{24,0},{28,60},{32,40}... | collective-permute-start | bytes 1425416 | tf_op jit(solution)/shard_map/ppermute | solution.py:446
  28.6 2.2 %collective-permute-start.9 = (f32[4,8,3712]{2,1,0:T(8,128)S(1)}, f32[4,8,3712]{2,1,0:T(8,128)S(1)}, u32[]{:S(2)}, u32[]{:S(2)}) collective-permute-start(f32[4,8,3712]{2,1,0:T(8,128)S(1)} %line.1.a_ref), channel_id=1, source_target_pairs={{0,24},{4,100},{8,0},{12,108},{16,8},{20,116},{24,16},{28,124},{32... | collective-permute-start | bytes 1425416 | tf_op jit(solution)/shard_map/ppermute | solution.py:446
  30.8 1.8 %collective-permute-start.8 = (f32[4,8,3712]{2,1,0:T(8,128)S(1)}, f32[4,8,3712]{2,1,0:T(8,128)S(1)}, u32[]{:S(2)}, u32[]{:S(2)}) collective-permute-start(f32[4,8,3712]{2,1,0:T(8,128)S(1)} %line.1.a_ref), channel_id=1, source_target_pairs={{0,16},{4,68},{8,24},{12,76},{16,0},{20,84},{24,8},{28,92},{32,48}... | collective-permute-start | bytes 1425416 | tf_op jit(solution)/shard_map/ppermute | solution.py:446
  32.6 1.9 %flip.1.flip_ref = bf16[1024,3584]{1,0:T(8,128)(2,1)S(1)} custom-call(bf16[3584,1024]{1,0:T(8,128)(2,1)S(1)} %copy-done), custom_call_target="tpu_custom_call" | custom-call | flops 1000000 | bytes 7340032 | tf_op jit(solution)/shard_map/flip/pallas_call | solution.py:55
  34.5 2.8 %collective-permute-done.6.b_ref = f32[4,8,3712]{2,1,0:T(8,128)S(1)} collective-permute-done((f32[4,8,3712]{2,1,0:T(8,128)S(1)}, f32[4,8,3712]{2,1,0:T(8,128)S(1)}, u32[]{:S(2)}, u32[]{:S(2)}) %collective-permute-start.6) | collective-permute-done | bytes 475168 | tf_op jit(solution)/shard_map/ppermute | solution.py:446
  37.4 4.7 %collective-permute-done.9.d_ref = f32[4,8,3712]{2,1,0:T(8,128)S(1)} collective-permute-done((f32[4,8,3712]{2,1,0:T(8,128)S(1)}, f32[4,8,3712]{2,1,0:T(8,128)S(1)}, u32[]{:S(2)}, u32[]{:S(2)}) %collective-permute-start.9) | collective-permute-done | bytes 475168 | tf_op jit(solution)/shard_map/ppermute | solution.py:446
  42.1 1.8 %collective-permute-done.8.c_ref = f32[4,8,3712]{2,1,0:T(8,128)S(1)} collective-permute-done((f32[4,8,3712]{2,1,0:T(8,128)S(1)}, f32[4,8,3712]{2,1,0:T(8,128)S(1)}, u32[]{:S(2)}, u32[]{:S(2)}) %collective-permute-start.8) | collective-permute-done | bytes 475168 | tf_op jit(solution)/shard_map/ppermute | solution.py:446
  45.7 2.9 %latents.1 = (f32[128,1024]{1,0:T(8,128)S(1)}, f32[64,3840]{1,0:T(8,128)S(1)}, f32[64,3840]{1,0:T(8,128)S(1)}) custom-call(f32[4,8,3712]{2,1,0:T(8,128)S(1)} %collective-permute-done.7.a_ref, f32[4,8,3712]{2,1,0:T(8,128)S(1)} %collective-permute-done.10.b_ref, f32[4,8,3712]{2,1,0:T(8,128)S(1)} %collective-permute-done.11.c_ref, ...), custom_call_target="tpu_custom_call" | custom-call | flops 1879048192 | bytes 20316160 | tf_op jit(solution)/shard_map/latents/pallas_call | solution.py:55
  48.9 2.4 %collective-permute-done.13.b_ref = f32[64,3840]{1,0:T(8,128)S(1)} collective-permute-done((f32[64,3840]{1,0:T(8,128)S(1)}, f32[64,3840]{1,0:T(8,128)S(1)}, u32[]{:S(2)}, u32[]{:S(2)}) %collective-permute-start.13) | collective-permute-done | bytes 983072 | tf_op jit(solution)/shard_map/ppermute | solution.py:450
  54.3 1.9 %collective-permute-start.16 = (f32[4,8,1920]{2,1,0:T(8,128)S(1)}, f32[4,8,1920]{2,1,0:T(8,128)S(1)}, u32[]{:S(2)}, u32[]{:S(2)}) collective-permute-start(f32[4,8,1920]{2,1,0:T(8,128)S(1)} %get-tuple-element.80), channel_id=1, source_target_pairs={{0,96},{4,28},{8,104},{12,4},{16,112},{20,12},{24,120},{28,20},{32... | collective-permute-start | bytes 737288 | tf_op jit(solution)/shard_map/ppermute | solution.py:446
  56.2 3.2 %collective-permute-done.14.b_ref = f32[4,8,1920]{2,1,0:T(8,128)S(1)} collective-permute-done((f32[4,8,1920]{2,1,0:T(8,128)S(1)}, f32[4,8,1920]{2,1,0:T(8,128)S(1)}, u32[]{:S(2)}, u32[]{:S(2)}) %collective-permute-start.14) | collective-permute-done | bytes 245792 | tf_op jit(solution)/shard_map/ppermute | solution.py:446
  59.4 2.5 %collective-permute-done.15.c_ref = f32[4,8,1920]{2,1,0:T(8,128)S(1)} collective-permute-done((f32[4,8,1920]{2,1,0:T(8,128)S(1)}, f32[4,8,1920]{2,1,0:T(8,128)S(1)}, u32[]{:S(2)}, u32[]{:S(2)}) %collective-permute-start.15) | collective-permute-done | bytes 245792 | tf_op jit(solution)/shard_map/ppermute | solution.py:446
  62.0 1.9 %collective-permute-start.17 = (f32[8,1920]{1,0:T(8,128)S(1)}, f32[8,1920]{1,0:T(8,128)S(1)}, u32[]{:S(2)}, u32[]{:S(2)}) collective-permute-start(f32[8,1920]{1,0:T(8,128)S(1)} %get-tuple-element.82), channel_id=1, source_target_pairs={{0,16},{4,68},{8,24},{12,76},{16,0},{20,84},{24,8},{28,92},{32,48}... | collective-permute-start | bytes 184328 | tf_op jit(solution)/shard_map/ppermute | solution.py:446
  63.9 1.6 %collective-permute-start.18 = (f32[8,1920]{1,0:T(8,128)S(1)}, f32[8,1920]{1,0:T(8,128)S(1)}, u32[]{:S(2)}, u32[]{:S(2)}) collective-permute-start(f32[8,1920]{1,0:T(8,128)S(1)} %get-tuple-element.83), channel_id=1, source_target_pairs={{0,8},{4,36},{8,16},{12,44},{16,24},{20,52},{24,0},{28,60},{32,40}... | collective-permute-start | bytes 184328 | tf_op jit(solution)/shard_map/ppermute | solution.py:446
  65.5 1.6 %collective-permute-start.19 = (f32[8,1920]{1,0:T(8,128)S(1)}, f32[8,1920]{1,0:T(8,128)S(1)}, u32[]{:S(2)}, u32[]{:S(2)}) collective-permute-start(f32[8,1920]{1,0:T(8,128)S(1)} %get-tuple-element.84), channel_id=1, source_target_pairs={{0,24},{4,100},{8,0},{12,108},{16,8},{20,116},{24,16},{28,124},{32... | collective-permute-start | bytes 184328 | tf_op jit(solution)/shard_map/ppermute | solution.py:446
  70.1 2.0 %collective-permute-start.21 = (f32[8,1920]{1,0:T(8,128)S(1)}, f32[8,1920]{1,0:T(8,128)S(1)}, u32[]{:S(2)}, u32[]{:S(2)}) collective-permute-start(f32[8,1920]{1,0:T(8,128)S(1)} %plane_sum.1.a_ref), channel_id=1, source_target_pairs={{0,1},{1,2},{2,3},{3,0},{4,5},{5,6},{6,7},{7,4},{8,9},{9,10},{10,1... | collective-permute-start | bytes 184328 | tf_op jit(solution)/shard_map/ppermute | solution.py:441
  73.4 2.2 %collective-permute-done.22.d_ref = f32[8,1920]{1,0:T(8,128)S(1)} collective-permute-done((f32[8,1920]{1,0:T(8,128)S(1)}, f32[8,1920]{1,0:T(8,128)S(1)}, u32[]{:S(2)}, u32[]{:S(2)}) %collective-permute-start.22) | collective-permute-done | bytes 61472 | tf_op jit(solution)/shard_map/ppermute | solution.py:441
  (51 shorter events, 16.1 us)
Async XLA Ops:
  0.7 21.6 %copy-start.6 = (s32[128,1024]{1,0:T(8,128)S(1)}, s32[128,1024]{1,0:T(8,128)}, u32[]{:S(2)}) copy-start(s32[128,1024]{1,0:T(8,128)} %active_ref) | copy-start | bytes 1572868
  5.1 11.1 %collective-permute-start.2 = (f32[8,3584]{1,0:T(8,128)S(1)}, f32[8,3584]{1,0:T(8,128)S(1)}, u32[]{:S(2)}, u32[]{:S(2)}) collective-permute-start(f32[8,3584]{1,0:T(8,128)S(1)} %get-tuple-element.50.a_ref), channel_id=1, source_target_pairs={{0,2},{1,3},{2,0},{3,1},{4,6},{5,7},{6,4},{7,5},{8,10},{9,11},{10,... | collective-permute-start | bytes 344072 | tf_op jit(solution)/shard_map/ppermute | solution.py:441
  8.5 7.7 %collective-permute-start.1 = (f32[8,3584]{1,0:T(8,128)S(1)}, f32[8,3584]{1,0:T(8,128)S(1)}, u32[]{:S(2)}, u32[]{:S(2)}) collective-permute-start(f32[8,3584]{1,0:T(8,128)S(1)} %get-tuple-element.50.a_ref), channel_id=1, source_target_pairs={{0,1},{1,2},{2,3},{3,0},{4,5},{5,6},{6,7},{7,4},{8,9},{9,10},{10,1... | collective-permute-start | bytes 344072 | tf_op jit(solution)/shard_map/ppermute | solution.py:441
  9.1 7.0 %collective-permute-start = (f32[8,3584]{1,0:T(8,128)S(1)}, f32[8,3584]{1,0:T(8,128)S(1)}, u32[]{:S(2)}, u32[]{:S(2)}) collective-permute-start(f32[8,3584]{1,0:T(8,128)S(1)} %get-tuple-element.50.a_ref), channel_id=1, source_target_pairs={{0,3},{1,0},{2,1},{3,2},{4,7},{5,4},{6,5},{7,6},{8,11},{9,8},{10,9... | collective-permute-start | bytes 344072 | tf_op jit(solution)/shard_map/ppermute | solution.py:441
  16.6 9.9 %collective-permute-start.5 = (f32[8,3712]{1,0:T(8,128)S(1)}, f32[8,3712]{1,0:T(8,128)S(1)}, u32[]{:S(2)}, u32[]{:S(2)}) collective-permute-start(f32[8,3712]{1,0:T(8,128)S(1)} %get-tuple-element.59.a_ref), channel_id=1, source_target_pairs={{0,32},{4,12},{8,40},{12,20},{16,48},{20,28},{24,56},{28,4},{32,64... | collective-permute-start | bytes 356360 | tf_op jit(solution)/shard_map/ppermute | solution.py:446
  18.1 8.3 %collective-permute-start.4 = (f32[8,3712]{1,0:T(8,128)S(1)}, f32[8,3712]{1,0:T(8,128)S(1)}, u32[]{:S(2)}, u32[]{:S(2)}) collective-permute-start(f32[8,3712]{1,0:T(8,128)S(1)} %get-tuple-element.59.a_ref), channel_id=1, source_target_pairs={{0,64},{4,20},{8,72},{12,28},{16,80},{20,4},{24,88},{28,12},{32,96... | collective-permute-start | bytes 356360 | tf_op jit(solution)/shard_map/ppermute | solution.py:446
  20.9 5.6 %collective-permute-start.3 = (f32[8,3712]{1,0:T(8,128)S(1)}, f32[8,3712]{1,0:T(8,128)S(1)}, u32[]{:S(2)}, u32[]{:S(2)}) collective-permute-start(f32[8,3712]{1,0:T(8,128)S(1)} %get-tuple-element.59.a_ref), channel_id=1, source_target_pairs={{0,96},{4,28},{8,104},{12,4},{16,112},{20,12},{24,120},{28,20},{32... | collective-permute-start | bytes 356360 | tf_op jit(solution)/shard_map/ppermute | solution.py:446
  26.5 8.0 %collective-permute-start.7 = (f32[4,8,3712]{2,1,0:T(8,128)S(1)}, f32[4,8,3712]{2,1,0:T(8,128)S(1)}, u32[]{:S(2)}, u32[]{:S(2)}) collective-permute-start(f32[4,8,3712]{2,1,0:T(8,128)S(1)} %line.1.a_ref), channel_id=1, source_target_pairs={{0,4},{4,0},{8,12},{12,8},{16,20},{20,16},{24,28},{28,24},{32,36},... | collective-permute-start | bytes 1425416 | tf_op jit(solution)/shard_map/ppermute | solution.py:450
  26.6 10.7 %collective-permute-start.6 = (f32[4,8,3712]{2,1,0:T(8,128)S(1)}, f32[4,8,3712]{2,1,0:T(8,128)S(1)}, u32[]{:S(2)}, u32[]{:S(2)}) collective-permute-start(f32[4,8,3712]{2,1,0:T(8,128)S(1)} %line.1.a_ref), channel_id=1, source_target_pairs={{0,8},{4,36},{8,16},{12,44},{16,24},{20,52},{24,0},{28,60},{32,40}... | collective-permute-start | bytes 1425416 | tf_op jit(solution)/shard_map/ppermute | solution.py:446
  28.6 13.5 %collective-permute-start.9 = (f32[4,8,3712]{2,1,0:T(8,128)S(1)}, f32[4,8,3712]{2,1,0:T(8,128)S(1)}, u32[]{:S(2)}, u32[]{:S(2)}) collective-permute-start(f32[4,8,3712]{2,1,0:T(8,128)S(1)} %line.1.a_ref), channel_id=1, source_target_pairs={{0,24},{4,100},{8,0},{12,108},{16,8},{20,116},{24,16},{28,124},{32... | collective-permute-start | bytes 1425416 | tf_op jit(solution)/shard_map/ppermute | solution.py:446
  30.8 13.1 %collective-permute-start.8 = (f32[4,8,3712]{2,1,0:T(8,128)S(1)}, f32[4,8,3712]{2,1,0:T(8,128)S(1)}, u32[]{:S(2)}, u32[]{:S(2)}) collective-permute-start(f32[4,8,3712]{2,1,0:T(8,128)S(1)} %line.1.a_ref), channel_id=1, source_target_pairs={{0,16},{4,68},{8,24},{12,76},{16,0},{20,84},{24,8},{28,92},{32,48}... | collective-permute-start | bytes 1425416 | tf_op jit(solution)/shard_map/ppermute | solution.py:446
  37.4 6.6 %collective-permute-start.10 = (f32[4,8,3712]{2,1,0:T(8,128)S(1)}, f32[4,8,3712]{2,1,0:T(8,128)S(1)}, u32[]{:S(2)}, u32[]{:S(2)}) collective-permute-start(f32[4,8,3712]{2,1,0:T(8,128)S(1)} %collective-permute-done.6.b_ref), channel_id=1, source_target_pairs={{0,4},{4,0},{8,12},{12,8},{16,20},{20,16},{24,28},{28,24},{32,36},... | collective-permute-start | bytes 1425416 | tf_op jit(solution)/shard_map/ppermute | solution.py:450
  42.1 3.1 %collective-permute-start.12 = (f32[4,8,3712]{2,1,0:T(8,128)S(1)}, f32[4,8,3712]{2,1,0:T(8,128)S(1)}, u32[]{:S(2)}, u32[]{:S(2)}) collective-permute-start(f32[4,8,3712]{2,1,0:T(8,128)S(1)} %collective-permute-done.9.d_ref), channel_id=1, source_target_pairs={{0,4},{4,0},{8,12},{12,8},{16,20},{20,16},{24,28},{28,24},{32,36},... | collective-permute-start | bytes 1425416 | tf_op jit(solution)/shard_map/ppermute | solution.py:450
  43.9 1.8 %collective-permute-start.11 = (f32[4,8,3712]{2,1,0:T(8,128)S(1)}, f32[4,8,3712]{2,1,0:T(8,128)S(1)}, u32[]{:S(2)}, u32[]{:S(2)}) collective-permute-start(f32[4,8,3712]{2,1,0:T(8,128)S(1)} %collective-permute-done.8.c_ref), channel_id=1, source_target_pairs={{0,4},{4,0},{8,12},{12,8},{16,20},{20,16},{24,28},{28,24},{32,36},... | collective-permute-start | bytes 1425416 | tf_op jit(solution)/shard_map/ppermute | solution.py:450
  48.7 2.6 %collective-permute-start.13 = (f32[64,3840]{1,0:T(8,128)S(1)}, f32[64,3840]{1,0:T(8,128)S(1)}, u32[]{:S(2)}, u32[]{:S(2)}) collective-permute-start(f32[64,3840]{1,0:T(8,128)S(1)} %get-tuple-element.76), channel_id=1, source_target_pairs={{0,4},{4,0},{8,12},{12,8},{16,20},{20,16},{24,28},{28,24},{32,36},... | collective-permute-start | bytes 2949128 | tf_op jit(solution)/shard_map/ppermute | solution.py:450
  51.5 7.9 %collective-permute-start.14 = (f32[4,8,1920]{2,1,0:T(8,128)S(1)}, f32[4,8,1920]{2,1,0:T(8,128)S(1)}, u32[]{:S(2)}, u32[]{:S(2)}) collective-permute-start(f32[4,8,1920]{2,1,0:T(8,128)S(1)} %get-tuple-element.78), channel_id=1, source_target_pairs={{0,64},{4,20},{8,72},{12,28},{16,80},{20,4},{24,88},{28,12},{32,96... | collective-permute-start | bytes 737288 | tf_op jit(solution)/shard_map/ppermute | solution.py:446
  53.0 8.9 %collective-permute-start.15 = (f32[4,8,1920]{2,1,0:T(8,128)S(1)}, f32[4,8,1920]{2,1,0:T(8,128)S(1)}, u32[]{:S(2)}, u32[]{:S(2)}) collective-permute-start(f32[4,8,1920]{2,1,0:T(8,128)S(1)} %get-tuple-element.79), channel_id=1, source_target_pairs={{0,32},{4,12},{8,40},{12,20},{16,48},{20,28},{24,56},{28,4},{32,64... | collective-permute-start | bytes 737288 | tf_op jit(solution)/shard_map/ppermute | solution.py:446
  54.3 7.6 %collective-permute-start.16 = (f32[4,8,1920]{2,1,0:T(8,128)S(1)}, f32[4,8,1920]{2,1,0:T(8,128)S(1)}, u32[]{:S(2)}, u32[]{:S(2)}) collective-permute-start(f32[4,8,1920]{2,1,0:T(8,128)S(1)} %get-tuple-element.80), channel_id=1, source_target_pairs={{0,96},{4,28},{8,104},{12,4},{16,112},{20,12},{24,120},{28,20},{32... | collective-permute-start | bytes 737288 | tf_op jit(solution)/shard_map/ppermute | solution.py:446
  62.0 5.8 %collective-permute-start.17 = (f32[8,1920]{1,0:T(8,128)S(1)}, f32[8,1920]{1,0:T(8,128)S(1)}, u32[]{:S(2)}, u32[]{:S(2)}) collective-permute-start(f32[8,1920]{1,0:T(8,128)S(1)} %get-tuple-element.82), channel_id=1, source_target_pairs={{0,16},{4,68},{8,24},{12,76},{16,0},{20,84},{24,8},{28,92},{32,48}... | collective-permute-start | bytes 184328 | tf_op jit(solution)/shard_map/ppermute | solution.py:446
  63.9 5.4 %collective-permute-start.18 = (f32[8,1920]{1,0:T(8,128)S(1)}, f32[8,1920]{1,0:T(8,128)S(1)}, u32[]{:S(2)}, u32[]{:S(2)}) collective-permute-start(f32[8,1920]{1,0:T(8,128)S(1)} %get-tuple-element.83), channel_id=1, source_target_pairs={{0,8},{4,36},{8,16},{12,44},{16,24},{20,52},{24,0},{28,60},{32,40}... | collective-permute-start | bytes 184328 | tf_op jit(solution)/shard_map/ppermute | solution.py:446
  65.5 4.2 %collective-permute-start.19 = (f32[8,1920]{1,0:T(8,128)S(1)}, f32[8,1920]{1,0:T(8,128)S(1)}, u32[]{:S(2)}, u32[]{:S(2)}) collective-permute-start(f32[8,1920]{1,0:T(8,128)S(1)} %get-tuple-element.84), channel_id=1, source_target_pairs={{0,24},{4,100},{8,0},{12,108},{16,8},{20,116},{24,16},{28,124},{32... | collective-permute-start | bytes 184328 | tf_op jit(solution)/shard_map/ppermute | solution.py:446
  69.7 5.9 %collective-permute-start.22 = (f32[8,1920]{1,0:T(8,128)S(1)}, f32[8,1920]{1,0:T(8,128)S(1)}, u32[]{:S(2)}, u32[]{:S(2)}) collective-permute-start(f32[8,1920]{1,0:T(8,128)S(1)} %plane_sum.1.a_ref), channel_id=1, source_target_pairs={{0,2},{1,3},{2,0},{3,1},{4,6},{5,7},{6,4},{7,5},{8,10},{9,11},{10,... | collective-permute-start | bytes 184328 | tf_op jit(solution)/shard_map/ppermute | solution.py:441
  70.1 6.1 %collective-permute-start.21 = (f32[8,1920]{1,0:T(8,128)S(1)}, f32[8,1920]{1,0:T(8,128)S(1)}, u32[]{:S(2)}, u32[]{:S(2)}) collective-permute-start(f32[8,1920]{1,0:T(8,128)S(1)} %plane_sum.1.a_ref), channel_id=1, source_target_pairs={{0,1},{1,2},{2,3},{3,0},{4,5},{5,6},{6,7},{7,4},{8,9},{9,10},{10,1... | collective-permute-start | bytes 184328 | tf_op jit(solution)/shard_map/ppermute | solution.py:441
  72.2 4.2 %collective-permute-start.20 = (f32[8,1920]{1,0:T(8,128)S(1)}, f32[8,1920]{1,0:T(8,128)S(1)}, u32[]{:S(2)}, u32[]{:S(2)}) collective-permute-start(f32[8,1920]{1,0:T(8,128)S(1)} %plane_sum.1.a_ref), channel_id=1, source_target_pairs={{0,3},{1,0},{2,1},{3,2},{4,7},{5,4},{6,5},{7,6},{8,11},{9,8},{10,9... | collective-permute-start | bytes 184328 | tf_op jit(solution)/shard_map/ppermute | solution.py:441
  (7 other events, 43.0 us)

commit v7 on v6

--- a/solution.py
+++ b/solution.py
@@ -188,7 +188,7 @@
 
 
 def line_kernel(a_ref, b_ref, c_ref, d_ref, out_ref):
-    for d, ref in zip((0, *(3,2,1)), (a_ref, b_ref, c_ref, d_ref)):
+    for d, ref in zip((0, *(2, 3, 1)), (a_ref, b_ref, c_ref, d_ref)):
         out_ref[d] = ref[...]
 
 
@@ -462,7 +462,7 @@
     *parts, resid = lax.optimization_barrier((*over_tp(part, (3,1,2)), resid))
     attn, msg = norm(parts, resid_corrupt, resid_clean, gain)
     gf = grad_f(cot, w_dec, active)
-    parts = [msg] + [send(msg, 0, d) for d in (3,2,1)]
+    parts = [msg] + [send(msg, 0, d) for d in (2, 3, 1)]
     *parts, gf = lax.optimization_barrier((*parts, gf))
     block = line(parts)
     flipped = flip(w_enc)

time: 77.6 us -> 77.3 us (level)
  waiting for transfers between devices: 23.7 us -> 19.6 us
  starting transfers between devices: 32 us -> 35.8 us
    ppermute x12, waiting for transfers between devices: 17.7 us -> 13.6 us  [send(): return lax.ppermute(x, 'lat', shift(stage, d))]
    ppermute x5, starting transfers between devices: 0.3 us -> 4.18 us  [swap(): return lax.ppermute(x, 'lat', CORE_SWAP)]
  transfers between devices with their start and end apart: 23 -> 23, of which waited for: 13 -> 14; matrix products, arithmetic and copies ran while one was open for 0% -> 0% of each run, Pallas kernels for 12% -> 12%
where the time goes in v7:
time: 77.3 us; the launch traced here: 77.1 us
  starting transfers between devices  35.8 us (46%)
  waiting for transfers between devices  19.6 us (25%)
  Pallas kernels  18.4 us (24%)
  local copies, waits for them, and re-layouts  2.39 us (3%)
  between operations  0.83 us (1%)
    ppermute x12, starting transfers between devices, send(): return lax.ppermute(x, 'lat', shift(stage, d))  21.4 us
    pallas_call x12, Pallas kernels, call(): pl.pallas_call(kernel, in_specs=[pl.BlockSpec(memory_space=s) for s in sp...  18.4 us
    ppermute x12, waiting for transfers between devices, send(): return lax.ppermute(x, 'lat', shift(stage, d))  13.6 us
    ppermute x6, starting transfers between devices, over_tp(): lax.ppermute(x, 'tp', [(i, (i + d) % 4) for i in range(4)])  10.2 us
    ppermute x5, starting transfers between devices, swap(): return lax.ppermute(x, 'lat', CORE_SWAP)  4.18 us
    ppermute x6, waiting for transfers between devices, over_tp(): lax.ppermute(x, 'tp', [(i, (i + d) % 4) for i in range(4)])  3.02 us
    ppermute x5, waiting for transfers between devices, swap(): return lax.ppermute(x, 'lat', CORE_SWAP)  2.99 us
    unnamed x16, local copies, waits for them, and re-layouts  2.38 us
  transfers between devices with their start and end apart: 23, of which 14 were waited for; matrix products, arithmetic and copies ran while one was open for 0% of the time, Pallas kernels for 12%

profile of v7, /device:TPU:0, one launch (start us, length us, event | category | flops | bytes accessed | tf_op | source)
XLA Modules:
  0.0 77.1 jit_solution(10877054598238522732)
XLA Ops:
  0.7 4.4 %project.1 = (f32[4,8,3584]{2,1,0:T(8,128)S(1)}, f32[8,3584]{1,0:T(8,128)S(1)}) custom-call(bf16[128,1024]{1,0:T(8,128)(2,1)} %zc_ref.1, bf16[128,1024]{1,0:T(8,128)(2,1)} %zn_ref.1, bf16[1024,3584]{1,0:T(8,128)(2,1)} %w_ref.1), custom_call_target="tpu_custom_call" | custom-call | flops 117440512 | bytes 7864320 | tf_op jit(solution)/shard_map/project/pallas_call | solution.py:55
  5.1 3.4 %collective-permute-start.2 = (f32[8,3584]{1,0:T(8,128)S(1)}, f32[8,3584]{1,0:T(8,128)S(1)}, u32[]{:S(2)}, u32[]{:S(2)}) collective-permute-start(f32[8,3584]{1,0:T(8,128)S(1)} %get-tuple-element.50.a_ref), channel_id=1, source_target_pairs={{0,2},{1,3},{2,0},{3,1},{4,6},{5,7},{6,4},{7,5},{8,10},{9,11},{10,... | collective-permute-start | bytes 344072 | tf_op jit(solution)/shard_map/ppermute | solution.py:441
  9.1 2.6 %collective-permute-start = (f32[8,3584]{1,0:T(8,128)S(1)}, f32[8,3584]{1,0:T(8,128)S(1)}, u32[]{:S(2)}, u32[]{:S(2)}) collective-permute-start(f32[8,3584]{1,0:T(8,128)S(1)} %get-tuple-element.50.a_ref), channel_id=1, source_target_pairs={{0,3},{1,0},{2,1},{3,2},{4,7},{5,4},{6,5},{7,6},{8,11},{9,8},{10,9... | collective-permute-start | bytes 344072 | tf_op jit(solution)/shard_map/ppermute | solution.py:441
  14.1 2.1 %resid_project.1.resid_ref = f32[2,128,1024]{2,1,0:T(8,128)S(1)} custom-call(bf16[128,3584]{1,0:T(8,128)(2,1)S(1)} %copy-done.1, bf16[128,3584]{1,0:T(8,128)(2,1)S(1)} %copy-done.3, bf16[3584,1024]{1,0:T(8,128)(2,1)S(1)} %copy-done), custom_call_target="tpu_custom_call" | custom-call | flops 1879048192 | bytes 9175040 | tf_op jit(solution)/shard_map/resid_project/pallas_call | solution.py:55
  18.1 1.7 %collective-permute-start.4 = (f32[8,3712]{1,0:T(8,128)S(1)}, f32[8,3712]{1,0:T(8,128)S(1)}, u32[]{:S(2)}, u32[]{:S(2)}) collective-permute-start(f32[8,3712]{1,0:T(8,128)S(1)} %get-tuple-element.59.a_ref), channel_id=1, source_target_pairs={{0,96},{4,28},{8,104},{12,4},{16,112},{20,12},{24,120},{28,20},{32... | collective-permute-start | bytes 356360 | tf_op jit(solution)/shard_map/ppermute | solution.py:446
  19.9 1.8 %collective-permute-start.3 = (f32[8,3712]{1,0:T(8,128)S(1)}, f32[8,3712]{1,0:T(8,128)S(1)}, u32[]{:S(2)}, u32[]{:S(2)}) collective-permute-start(f32[8,3712]{1,0:T(8,128)S(1)} %get-tuple-element.59.a_ref), channel_id=1, source_target_pairs={{0,64},{4,20},{8,72},{12,28},{16,80},{20,4},{24,88},{28,12},{32,96... | collective-permute-start | bytes 356360 | tf_op jit(solution)/shard_map/ppermute | solution.py:446
  21.7 4.1 %grad_f.1.gf_ref = f32[4,128,1024]{2,1,0:T(8,128)S(1)} custom-call(bf16[128,4,3584]{2,1,0:T(4,128)(2,1)S(1)} %copy-done.5, bf16[1024,3584]{1,0:T(8,128)(2,1)S(1)} %copy-done.4, s32[128,1024]{1,0:T(8,128)S(1)} %copy-done.6), custom_call_target="tpu_custom_call" | custom-call | flops 3758096384 | bytes 11534336 | tf_op jit(solution)/shard_map/grad_f/pallas_call | solution.py:55
  26.3 2.0 %collective-permute-start.6 = (f32[4,8,3712]{2,1,0:T(8,128)S(1)}, f32[4,8,3712]{2,1,0:T(8,128)S(1)}, u32[]{:S(2)}, u32[]{:S(2)}) collective-permute-start(f32[4,8,3712]{2,1,0:T(8,128)S(1)} %line.1.a_ref), channel_id=1, source_target_pairs={{0,8},{4,36},{8,16},{12,44},{16,24},{20,52},{24,0},{28,60},{32,40}... | collective-permute-start | bytes 1425416 | tf_op jit(solution)/shard_map/ppermute | solution.py:446
  28.3 2.2 %collective-permute-start.9 = (f32[4,8,3712]{2,1,0:T(8,128)S(1)}, f32[4,8,3712]{2,1,0:T(8,128)S(1)}, u32[]{:S(2)}, u32[]{:S(2)}) collective-permute-start(f32[4,8,3712]{2,1,0:T(8,128)S(1)} %line.1.a_ref), channel_id=1, source_target_pairs={{0,24},{4,100},{8,0},{12,108},{16,8},{20,116},{24,16},{28,124},{32... | collective-permute-start | bytes 1425416 | tf_op jit(solution)/shard_map/ppermute | solution.py:446
  30.5 1.8 %collective-permute-start.8 = (f32[4,8,3712]{2,1,0:T(8,128)S(1)}, f32[4,8,3712]{2,1,0:T(8,128)S(1)}, u32[]{:S(2)}, u32[]{:S(2)}) collective-permute-start(f32[4,8,3712]{2,1,0:T(8,128)S(1)} %line.1.a_ref), channel_id=1, source_target_pairs={{0,16},{4,68},{8,24},{12,76},{16,0},{20,84},{24,8},{28,92},{32,48}... | collective-permute-start | bytes 1425416 | tf_op jit(solution)/shard_map/ppermute | solution.py:446
  32.3 1.9 %flip.1.flip_ref = bf16[1024,3584]{1,0:T(8,128)(2,1)S(1)} custom-call(bf16[3584,1024]{1,0:T(8,128)(2,1)S(1)} %copy-done), custom_call_target="tpu_custom_call" | custom-call | flops 1000000 | bytes 7340032 | tf_op jit(solution)/shard_map/flip/pallas_call | solution.py:55
  34.3 2.8 %collective-permute-done.6.b_ref = f32[4,8,3712]{2,1,0:T(8,128)S(1)} collective-permute-done((f32[4,8,3712]{2,1,0:T(8,128)S(1)}, f32[4,8,3712]{2,1,0:T(8,128)S(1)}, u32[]{:S(2)}, u32[]{:S(2)}) %collective-permute-start.6) | collective-permute-done | bytes 475168 | tf_op jit(solution)/shard_map/ppermute | solution.py:446
  37.1 3.9 %collective-permute-start.10 = (f32[4,8,3712]{2,1,0:T(8,128)S(1)}, f32[4,8,3712]{2,1,0:T(8,128)S(1)}, u32[]{:S(2)}, u32[]{:S(2)}) collective-permute-start(f32[4,8,3712]{2,1,0:T(8,128)S(1)} %collective-permute-done.6.b_ref), channel_id=1, source_target_pairs={{0,4},{4,0},{8,12},{12,8},{16,20},{20,16},{24,28},{28,24},{32,36},... | collective-permute-start | bytes 1425416 | tf_op jit(solution)/shard_map/ppermute | solution.py:450
  41.8 1.8 %collective-permute-done.8.c_ref = f32[4,8,3712]{2,1,0:T(8,128)S(1)} collective-permute-done((f32[4,8,3712]{2,1,0:T(8,128)S(1)}, f32[4,8,3712]{2,1,0:T(8,128)S(1)}, u32[]{:S(2)}, u32[]{:S(2)}) %collective-permute-start.8) | collective-permute-done | bytes 475168 | tf_op jit(solution)/shard_map/ppermute | solution.py:446
  45.5 2.9 %latents.1 = (f32[128,1024]{1,0:T(8,128)S(1)}, f32[64,3840]{1,0:T(8,128)S(1)}, f32[64,3840]{1,0:T(8,128)S(1)}) custom-call(f32[4,8,3712]{2,1,0:T(8,128)S(1)} %collective-permute-done.7.a_ref, f32[4,8,3712]{2,1,0:T(8,128)S(1)} %collective-permute-done.10.b_ref, f32[4,8,3712]{2,1,0:T(8,128)S(1)} %collective-permute-done.11.c_ref, ...), custom_call_target="tpu_custom_call" | custom-call | flops 1879048192 | bytes 20316160 | tf_op jit(solution)/shard_map/latents/pallas_call | solution.py:55
  48.6 2.4 %collective-permute-done.13.b_ref = f32[64,3840]{1,0:T(8,128)S(1)} collective-permute-done((f32[64,3840]{1,0:T(8,128)S(1)}, f32[64,3840]{1,0:T(8,128)S(1)}, u32[]{:S(2)}, u32[]{:S(2)}) %collective-permute-start.13) | collective-permute-done | bytes 983072 | tf_op jit(solution)/shard_map/ppermute | solution.py:450
  51.2 1.9 %collective-permute-start.14 = (f32[4,8,1920]{2,1,0:T(8,128)S(1)}, f32[4,8,1920]{2,1,0:T(8,128)S(1)}, u32[]{:S(2)}, u32[]{:S(2)}) collective-permute-start(f32[4,8,1920]{2,1,0:T(8,128)S(1)} %get-tuple-element.78), channel_id=1, source_target_pairs={{0,64},{4,20},{8,72},{12,28},{16,80},{20,4},{24,88},{28,12},{32,96... | collective-permute-start | bytes 737288 | tf_op jit(solution)/shard_map/ppermute | solution.py:446
  53.7 2.6 %collective-permute-start.16 = (f32[4,8,1920]{2,1,0:T(8,128)S(1)}, f32[4,8,1920]{2,1,0:T(8,128)S(1)}, u32[]{:S(2)}, u32[]{:S(2)}) collective-permute-start(f32[4,8,1920]{2,1,0:T(8,128)S(1)} %get-tuple-element.80), channel_id=1, source_target_pairs={{0,96},{4,28},{8,104},{12,4},{16,112},{20,12},{24,120},{28,20},{32... | collective-permute-start | bytes 737288 | tf_op jit(solution)/shard_map/ppermute | solution.py:446
  56.4 2.8 %collective-permute-done.14.b_ref = f32[4,8,1920]{2,1,0:T(8,128)S(1)} collective-permute-done((f32[4,8,1920]{2,1,0:T(8,128)S(1)}, f32[4,8,1920]{2,1,0:T(8,128)S(1)}, u32[]{:S(2)}, u32[]{:S(2)}) %collective-permute-start.14) | collective-permute-done | bytes 245792 | tf_op jit(solution)/shard_map/ppermute | solution.py:446
  59.1 2.5 %collective-permute-done.15.c_ref = f32[4,8,1920]{2,1,0:T(8,128)S(1)} collective-permute-done((f32[4,8,1920]{2,1,0:T(8,128)S(1)}, f32[4,8,1920]{2,1,0:T(8,128)S(1)}, u32[]{:S(2)}, u32[]{:S(2)}) %collective-permute-start.15) | collective-permute-done | bytes 245792 | tf_op jit(solution)/shard_map/ppermute | solution.py:446
  61.7 2.0 %collective-permute-start.17 = (f32[8,1920]{1,0:T(8,128)S(1)}, f32[8,1920]{1,0:T(8,128)S(1)}, u32[]{:S(2)}, u32[]{:S(2)}) collective-permute-start(f32[8,1920]{1,0:T(8,128)S(1)} %get-tuple-element.82), channel_id=1, source_target_pairs={{0,16},{4,68},{8,24},{12,76},{16,0},{20,84},{24,8},{28,92},{32,48}... | collective-permute-start | bytes 184328 | tf_op jit(solution)/shard_map/ppermute | solution.py:446
  65.2 1.7 %collective-permute-start.19 = (f32[8,1920]{1,0:T(8,128)S(1)}, f32[8,1920]{1,0:T(8,128)S(1)}, u32[]{:S(2)}, u32[]{:S(2)}) collective-permute-start(f32[8,1920]{1,0:T(8,128)S(1)} %get-tuple-element.84), channel_id=1, source_target_pairs={{0,24},{4,100},{8,0},{12,108},{16,8},{20,116},{24,16},{28,124},{32... | collective-permute-start | bytes 184328 | tf_op jit(solution)/shard_map/ppermute | solution.py:446
  69.9 2.0 %collective-permute-start.21 = (f32[8,1920]{1,0:T(8,128)S(1)}, f32[8,1920]{1,0:T(8,128)S(1)}, u32[]{:S(2)}, u32[]{:S(2)}) collective-permute-start(f32[8,1920]{1,0:T(8,128)S(1)} %plane_sum.1.a_ref), channel_id=1, source_target_pairs={{0,1},{1,2},{2,3},{3,0},{4,5},{5,6},{6,7},{7,4},{8,9},{9,10},{10,1... | collective-permute-start | bytes 184328 | tf_op jit(solution)/shard_map/ppermute | solution.py:441
  73.1 2.2 %collective-permute-done.22.d_ref = f32[8,1920]{1,0:T(8,128)S(1)} collective-permute-done((f32[8,1920]{1,0:T(8,128)S(1)}, f32[8,1920]{1,0:T(8,128)S(1)}, u32[]{:S(2)}, u32[]{:S(2)}) %collective-permute-start.22) | collective-permute-done | bytes 61472 | tf_op jit(solution)/shard_map/ppermute | solution.py:441
  (51 shorter events, 16.7 us)
Async XLA Ops:
  0.7 21.0 %copy-start.6 = (s32[128,1024]{1,0:T(8,128)S(1)}, s32[128,1024]{1,0:T(8,128)}, u32[]{:S(2)}) copy-start(s32[128,1024]{1,0:T(8,128)} %active_ref) | copy-start | bytes 1572868
  5.1 11.1 %collective-permute-start.2 = (f32[8,3584]{1,0:T(8,128)S(1)}, f32[8,3584]{1,0:T(8,128)S(1)}, u32[]{:S(2)}, u32[]{:S(2)}) collective-permute-start(f32[8,3584]{1,0:T(8,128)S(1)} %get-tuple-element.50.a_ref), channel_id=1, source_target_pairs={{0,2},{1,3},{2,0},{3,1},{4,6},{5,7},{6,4},{7,5},{8,10},{9,11},{10,... | collective-permute-start | bytes 344072 | tf_op jit(solution)/shard_map/ppermute | solution.py:441
  8.5 7.7 %collective-permute-start.1 = (f32[8,3584]{1,0:T(8,128)S(1)}, f32[8,3584]{1,0:T(8,128)S(1)}, u32[]{:S(2)}, u32[]{:S(2)}) collective-permute-start(f32[8,3584]{1,0:T(8,128)S(1)} %get-tuple-element.50.a_ref), channel_id=1, source_target_pairs={{0,1},{1,2},{2,3},{3,0},{4,5},{5,6},{6,7},{7,4},{8,9},{9,10},{10,1... | collective-permute-start | bytes 344072 | tf_op jit(solution)/shard_map/ppermute | solution.py:441
  9.1 7.0 %collective-permute-start = (f32[8,3584]{1,0:T(8,128)S(1)}, f32[8,3584]{1,0:T(8,128)S(1)}, u32[]{:S(2)}, u32[]{:S(2)}) collective-permute-start(f32[8,3584]{1,0:T(8,128)S(1)} %get-tuple-element.50.a_ref), channel_id=1, source_target_pairs={{0,3},{1,0},{2,1},{3,2},{4,7},{5,4},{6,5},{7,6},{8,11},{9,8},{10,9... | collective-permute-start | bytes 344072 | tf_op jit(solution)/shard_map/ppermute | solution.py:441
  16.6 9.3 %collective-permute-start.5 = (f32[8,3712]{1,0:T(8,128)S(1)}, f32[8,3712]{1,0:T(8,128)S(1)}, u32[]{:S(2)}, u32[]{:S(2)}) collective-permute-start(f32[8,3712]{1,0:T(8,128)S(1)} %get-tuple-element.59.a_ref), channel_id=1, source_target_pairs={{0,32},{4,12},{8,40},{12,20},{16,48},{20,28},{24,56},{28,4},{32,64... | collective-permute-start | bytes 356360 | tf_op jit(solution)/shard_map/ppermute | solution.py:446
  18.1 7.7 %collective-permute-start.4 = (f32[8,3712]{1,0:T(8,128)S(1)}, f32[8,3712]{1,0:T(8,128)S(1)}, u32[]{:S(2)}, u32[]{:S(2)}) collective-permute-start(f32[8,3712]{1,0:T(8,128)S(1)} %get-tuple-element.59.a_ref), channel_id=1, source_target_pairs={{0,96},{4,28},{8,104},{12,4},{16,112},{20,12},{24,120},{28,20},{32... | collective-permute-start | bytes 356360 | tf_op jit(solution)/shard_map/ppermute | solution.py:446
  19.9 6.3 %collective-permute-start.3 = (f32[8,3712]{1,0:T(8,128)S(1)}, f32[8,3712]{1,0:T(8,128)S(1)}, u32[]{:S(2)}, u32[]{:S(2)}) collective-permute-start(f32[8,3712]{1,0:T(8,128)S(1)} %get-tuple-element.59.a_ref), channel_id=1, source_target_pairs={{0,64},{4,20},{8,72},{12,28},{16,80},{20,4},{24,88},{28,12},{32,96... | collective-permute-start | bytes 356360 | tf_op jit(solution)/shard_map/ppermute | solution.py:446
  26.3 8.0 %collective-permute-start.7 = (f32[4,8,3712]{2,1,0:T(8,128)S(1)}, f32[4,8,3712]{2,1,0:T(8,128)S(1)}, u32[]{:S(2)}, u32[]{:S(2)}) collective-permute-start(f32[4,8,3712]{2,1,0:T(8,128)S(1)} %line.1.a_ref), channel_id=1, source_target_pairs={{0,4},{4,0},{8,12},{12,8},{16,20},{20,16},{24,28},{28,24},{32,36},... | collective-permute-start | bytes 1425416 | tf_op jit(solution)/shard_map/ppermute | solution.py:450
  26.3 10.7 %collective-permute-start.6 = (f32[4,8,3712]{2,1,0:T(8,128)S(1)}, f32[4,8,3712]{2,1,0:T(8,128)S(1)}, u32[]{:S(2)}, u32[]{:S(2)}) collective-permute-start(f32[4,8,3712]{2,1,0:T(8,128)S(1)} %line.1.a_ref), channel_id=1, source_target_pairs={{0,8},{4,36},{8,16},{12,44},{16,24},{20,52},{24,0},{28,60},{32,40}... | collective-permute-start | bytes 1425416 | tf_op jit(solution)/shard_map/ppermute | solution.py:446
  28.3 13.5 %collective-permute-start.9 = (f32[4,8,3712]{2,1,0:T(8,128)S(1)}, f32[4,8,3712]{2,1,0:T(8,128)S(1)}, u32[]{:S(2)}, u32[]{:S(2)}) collective-permute-start(f32[4,8,3712]{2,1,0:T(8,128)S(1)} %line.1.a_ref), channel_id=1, source_target_pairs={{0,24},{4,100},{8,0},{12,108},{16,8},{20,116},{24,16},{28,124},{32... | collective-permute-start | bytes 1425416 | tf_op jit(solution)/shard_map/ppermute | solution.py:446
  30.5 13.1 %collective-permute-start.8 = (f32[4,8,3712]{2,1,0:T(8,128)S(1)}, f32[4,8,3712]{2,1,0:T(8,128)S(1)}, u32[]{:S(2)}, u32[]{:S(2)}) collective-permute-start(f32[4,8,3712]{2,1,0:T(8,128)S(1)} %line.1.a_ref), channel_id=1, source_target_pairs={{0,16},{4,68},{8,24},{12,76},{16,0},{20,84},{24,8},{28,92},{32,48}... | collective-permute-start | bytes 1425416 | tf_op jit(solution)/shard_map/ppermute | solution.py:446
  37.1 6.6 %collective-permute-start.10 = (f32[4,8,3712]{2,1,0:T(8,128)S(1)}, f32[4,8,3712]{2,1,0:T(8,128)S(1)}, u32[]{:S(2)}, u32[]{:S(2)}) collective-permute-start(f32[4,8,3712]{2,1,0:T(8,128)S(1)} %collective-permute-done.6.b_ref), channel_id=1, source_target_pairs={{0,4},{4,0},{8,12},{12,8},{16,20},{20,16},{24,28},{28,24},{32,36},... | collective-permute-start | bytes 1425416 | tf_op jit(solution)/shard_map/ppermute | solution.py:450
  41.8 3.1 %collective-permute-start.12 = (f32[4,8,3712]{2,1,0:T(8,128)S(1)}, f32[4,8,3712]{2,1,0:T(8,128)S(1)}, u32[]{:S(2)}, u32[]{:S(2)}) collective-permute-start(f32[4,8,3712]{2,1,0:T(8,128)S(1)} %collective-permute-done.9.d_ref), channel_id=1, source_target_pairs={{0,4},{4,0},{8,12},{12,8},{16,20},{20,16},{24,28},{28,24},{32,36},... | collective-permute-start | bytes 1425416 | tf_op jit(solution)/shard_map/ppermute | solution.py:450
  43.6 1.8 %collective-permute-start.11 = (f32[4,8,3712]{2,1,0:T(8,128)S(1)}, f32[4,8,3712]{2,1,0:T(8,128)S(1)}, u32[]{:S(2)}, u32[]{:S(2)}) collective-permute-start(f32[4,8,3712]{2,1,0:T(8,128)S(1)} %collective-permute-done.8.c_ref), channel_id=1, source_target_pairs={{0,4},{4,0},{8,12},{12,8},{16,20},{20,16},{24,28},{28,24},{32,36},... | collective-permute-start | bytes 1425416 | tf_op jit(solution)/shard_map/ppermute | solution.py:450
  48.4 2.6 %collective-permute-start.13 = (f32[64,3840]{1,0:T(8,128)S(1)}, f32[64,3840]{1,0:T(8,128)S(1)}, u32[]{:S(2)}, u32[]{:S(2)}) collective-permute-start(f32[64,3840]{1,0:T(8,128)S(1)} %get-tuple-element.76), channel_id=1, source_target_pairs={{0,4},{4,0},{8,12},{12,8},{16,20},{20,16},{24,28},{28,24},{32,36},... | collective-permute-start | bytes 2949128 | tf_op jit(solution)/shard_map/ppermute | solution.py:450
  51.2 7.9 %collective-permute-start.14 = (f32[4,8,1920]{2,1,0:T(8,128)S(1)}, f32[4,8,1920]{2,1,0:T(8,128)S(1)}, u32[]{:S(2)}, u32[]{:S(2)}) collective-permute-start(f32[4,8,1920]{2,1,0:T(8,128)S(1)} %get-tuple-element.78), channel_id=1, source_target_pairs={{0,64},{4,20},{8,72},{12,28},{16,80},{20,4},{24,88},{28,12},{32,96... | collective-permute-start | bytes 737288 | tf_op jit(solution)/shard_map/ppermute | solution.py:446
  53.1 8.5 %collective-permute-start.15 = (f32[4,8,1920]{2,1,0:T(8,128)S(1)}, f32[4,8,1920]{2,1,0:T(8,128)S(1)}, u32[]{:S(2)}, u32[]{:S(2)}) collective-permute-start(f32[4,8,1920]{2,1,0:T(8,128)S(1)} %get-tuple-element.79), channel_id=1, source_target_pairs={{0,32},{4,12},{8,40},{12,20},{16,48},{20,28},{24,56},{28,4},{32,64... | collective-permute-start | bytes 737288 | tf_op jit(solution)/shard_map/ppermute | solution.py:446
  53.7 7.9 %collective-permute-start.16 = (f32[4,8,1920]{2,1,0:T(8,128)S(1)}, f32[4,8,1920]{2,1,0:T(8,128)S(1)}, u32[]{:S(2)}, u32[]{:S(2)}) collective-permute-start(f32[4,8,1920]{2,1,0:T(8,128)S(1)} %get-tuple-element.80), channel_id=1, source_target_pairs={{0,96},{4,28},{8,104},{12,4},{16,112},{20,12},{24,120},{28,20},{32... | collective-permute-start | bytes 737288 | tf_op jit(solution)/shard_map/ppermute | solution.py:446
  61.7 5.8 %collective-permute-start.17 = (f32[8,1920]{1,0:T(8,128)S(1)}, f32[8,1920]{1,0:T(8,128)S(1)}, u32[]{:S(2)}, u32[]{:S(2)}) collective-permute-start(f32[8,1920]{1,0:T(8,128)S(1)} %get-tuple-element.82), channel_id=1, source_target_pairs={{0,16},{4,68},{8,24},{12,76},{16,0},{20,84},{24,8},{28,92},{32,48}... | collective-permute-start | bytes 184328 | tf_op jit(solution)/shard_map/ppermute | solution.py:446
  63.7 5.4 %collective-permute-start.18 = (f32[8,1920]{1,0:T(8,128)S(1)}, f32[8,1920]{1,0:T(8,128)S(1)}, u32[]{:S(2)}, u32[]{:S(2)}) collective-permute-start(f32[8,1920]{1,0:T(8,128)S(1)} %get-tuple-element.83), channel_id=1, source_target_pairs={{0,8},{4,36},{8,16},{12,44},{16,24},{20,52},{24,0},{28,60},{32,40}... | collective-permute-start | bytes 184328 | tf_op jit(solution)/shard_map/ppermute | solution.py:446
  65.2 4.2 %collective-permute-start.19 = (f32[8,1920]{1,0:T(8,128)S(1)}, f32[8,1920]{1,0:T(8,128)S(1)}, u32[]{:S(2)}, u32[]{:S(2)}) collective-permute-start(f32[8,1920]{1,0:T(8,128)S(1)} %get-tuple-element.84), channel_id=1, source_target_pairs={{0,24},{4,100},{8,0},{12,108},{16,8},{20,116},{24,16},{28,124},{32... | collective-permute-start | bytes 184328 | tf_op jit(solution)/shard_map/ppermute | solution.py:446
  69.5 5.9 %collective-permute-start.22 = (f32[8,1920]{1,0:T(8,128)S(1)}, f32[8,1920]{1,0:T(8,128)S(1)}, u32[]{:S(2)}, u32[]{:S(2)}) collective-permute-start(f32[8,1920]{1,0:T(8,128)S(1)} %plane_sum.1.a_ref), channel_id=1, source_target_pairs={{0,2},{1,3},{2,0},{3,1},{4,6},{5,7},{6,4},{7,5},{8,10},{9,11},{10,... | collective-permute-start | bytes 184328 | tf_op jit(solution)/shard_map/ppermute | solution.py:441
  69.9 6.1 %collective-permute-start.21 = (f32[8,1920]{1,0:T(8,128)S(1)}, f32[8,1920]{1,0:T(8,128)S(1)}, u32[]{:S(2)}, u32[]{:S(2)}) collective-permute-start(f32[8,1920]{1,0:T(8,128)S(1)} %plane_sum.1.a_ref), channel_id=1, source_target_pairs={{0,1},{1,2},{2,3},{3,0},{4,5},{5,6},{6,7},{7,4},{8,9},{9,10},{10,1... | collective-permute-start | bytes 184328 | tf_op jit(solution)/shard_map/ppermute | solution.py:441
  71.9 4.2 %collective-permute-start.20 = (f32[8,1920]{1,0:T(8,128)S(1)}, f32[8,1920]{1,0:T(8,128)S(1)}, u32[]{:S(2)}, u32[]{:S(2)}) collective-permute-start(f32[8,1920]{1,0:T(8,128)S(1)} %plane_sum.1.a_ref), channel_id=1, source_target_pairs={{0,3},{1,0},{2,1},{3,2},{4,7},{5,4},{6,5},{7,6},{8,11},{9,8},{10,9... | collective-permute-start | bytes 184328 | tf_op jit(solution)/shard_map/ppermute | solution.py:441
  (7 other events, 41.8 us)
